TPU v7x, 512 devices: a whole 4x8x8 slice. The times are simulated.
512 devices in a mesh: dp: 4 (over z_lo), blk: 16 (over z_hi, y), uly: 8 (over x, core).
Axes of the slice: x: 4, y: 8, z: 8 (z_hi: 2, z_lo: 4; z = z_hi * 4 + z_lo), core: 2. Of those that a mesh axis runs over, the one named last changes fastest.
Arguments:
- queries: bfloat16 [4, 16384, 1024], P('dp', ('blk', 'uly')), may hold values from -6 to 6
- key_vectors: bfloat16 [4, 16384, 1024], P('dp', ('blk', 'uly')), may hold values from -6 to 6
- value_vectors: bfloat16 [4, 16384, 1024], P('dp', ('blk', 'uly')), may hold values from -6 to 6
- grad_context: bfloat16 [4, 16384, 1024], P('dp', ('blk', 'uly')), may hold values from -6 to 6
- content_bias: float32 [16, 64], P('uly'), may hold values from -3 to 3
- slopes: float32 [16], P('uly'), may hold values from 0.002 to 0.1
- lengths: int32 [4], P('dp'), may hold values from 4096 to 16384, as said below
Outputs:
- context: bfloat16 [4, 16384, 1024], P('dp', ('blk', 'uly'))
- grad_queries: bfloat16 [4, 16384, 1024], P('dp', ('blk', 'uly'))
- grad_keys: bfloat16 [4, 16384, 1024], P('dp', ('blk', 'uly'))
- grad_values: bfloat16 [4, 16384, 1024], P('dp', ('blk', 'uly'))
- grad_bias: float32 [16, 64], P('uly')
- grad_slopes: float32 [16], P('uly')
Inputs may be any that keep to these rules, and one draw needn't show every extreme that they name: `lengths`: frames at or beyond a recording's length are padding; at least one recording of the batch has all 16384 frames valid.
All inputs are finite; a program needn't handle non-finite values.
Results may differ from a plain program's by a relative error of at most 0.012.
The roundings to bfloat16 on the way count: a program that leaves them out, or rounds other values in their place, can miss the bound.
Values may be sent and summed in bfloat16 or wider, within the bound.
No kernel may reach another device: no remote copies, remote signals or barrier semaphores. Data moves between devices by JAX's collectives and lax.ppermute only.
A program may use at most 64 MiB of HBM per device.

v0:
```python
import jax
import jax.numpy as jnp
from jax import lax
from jax.sharding import PartitionSpec as P

masked_score = -1e30


def with_halo(block, sides, width):
    for axis, dim in sides:
        count = lax.axis_size(axis)
        forward = [(i, i + 1) for i in range(count - 1)]
        backward = [(target, source) for source, target in forward]
        low = lax.ppermute(
            lax.slice_in_dim(block, block.shape[dim] - width, None, axis=dim), axis, forward
        )
        high = lax.ppermute(lax.slice_in_dim(block, 0, width, axis=dim), axis, backward)
        block = jnp.concatenate([low, block, high], axis=dim)
    return block


def from_behind(block, axis, distance):
    devices = range(lax.axis_size(axis))
    route = [(i - distance, i) for i in devices if i - distance in devices]
    return lax.ppermute(block, axis, route)


def tile_terms(
    query_tile,
    upstream_tile,
    key_win,
    value_win,
    query_place,
    key_place,
    length,
    slopes,
    context_span,
    factor,
):
    spacing = jnp.abs(query_place[:, None] - key_place[None, :])
    usable = (spacing <= context_span) & (key_place[None, :] >= 0) & (key_place[None, :] < length)
    distance = spacing.astype(jnp.float32)
    scores = (
        jnp.einsum("ihe,jhe->hij", query_tile, key_win, preferred_element_type=jnp.float32) * factor
    )
    scores = jnp.where(usable[None], scores - slopes[:, None, None] * distance[None], masked_score)
    row_max = jnp.max(scores, axis=2, keepdims=True)
    powers = jnp.exp(scores - row_max)
    row_sum = jnp.sum(powers, axis=2, keepdims=True)
    attention = powers / row_sum
    soft_weights = attention.astype(jnp.bfloat16)
    context = jnp.einsum(
        "hij,jhe->ihe", soft_weights, value_win, preferred_element_type=jnp.float32
    )
    context = jnp.where((query_place < length)[:, None, None], context, jnp.zeros_like(context))
    dot_grads = jnp.einsum(
        "ihe,jhe->hij", upstream_tile, value_win, preferred_element_type=jnp.float32
    )
    row_delta = jnp.sum(attention * dot_grads, axis=2, keepdims=True)
    score_grads = attention * (dot_grads - row_delta)
    scaled_grads = (score_grads * factor).astype(jnp.bfloat16)
    query_grad = jnp.einsum(
        "hij,jhe->ihe", scaled_grads, key_win, preferred_element_type=jnp.float32
    )
    slope_grad = -jnp.sum(score_grads * distance[None], axis=(1, 2))
    log_total = (row_max + jnp.log(row_sum))[:, :, 0]
    return (
        context,
        query_grad,
        slope_grad,
        soft_weights,
        scaled_grads,
        log_total,
        row_delta[:, :, 0],
    )


def local(queries, key_vectors, value_vectors, grad_context, content_bias, slopes, lengths):
    query_heads, key_heads, value_heads, upstream_heads = (
        lax.all_to_all(queries, "uly", split_axis=2, concat_axis=1, tiled=True),
        lax.all_to_all(key_vectors, "uly", split_axis=2, concat_axis=1, tiled=True),
        lax.all_to_all(value_vectors, "uly", split_axis=2, concat_axis=1, tiled=True),
        lax.all_to_all(grad_context, "uly", split_axis=2, concat_axis=1, tiled=True),
    )
    heads_here, head_size = content_bias.shape
    block_rows = query_heads.shape[1]
    feature_width = heads_here * head_size
    factor = head_size ** (-0.5)
    tile_rows = min(256, block_rows)
    window = tile_rows + 2 * block_rows
    offsets = jnp.arange(block_rows // tile_rows, dtype=jnp.int32) * tile_rows
    anchor = lax.axis_index("blk") * block_rows
    length = lengths[0]
    row_place = anchor + jnp.arange(block_rows, dtype=jnp.int32)
    query_bias = (
        query_heads[0].reshape(block_rows, heads_here, head_size).astype(jnp.float32)
        + content_bias[None]
    ).astype(jnp.bfloat16)
    upstream_flat = jnp.where(
        (row_place < length)[:, None], upstream_heads[0], jnp.zeros_like(upstream_heads[0])
    )
    upstream_rows = upstream_flat.reshape(block_rows, heads_here, head_size)
    pair_rows = jnp.concatenate([key_heads[0], value_heads[0]], axis=1)
    pair_ext = with_halo(pair_rows, (("blk", 0),), block_rows)
    key_ext = pair_ext[:, :feature_width].reshape(-1, heads_here, head_size)
    value_ext = pair_ext[:, feature_width:].reshape(-1, heads_here, head_size)
    zero_grads = jnp.zeros((block_rows + 2 * block_rows, heads_here, head_size), jnp.float32)

    def query_sweep(running, offset):
        query_tile = lax.dynamic_slice_in_dim(query_bias, offset, tile_rows, 0)
        upstream_tile = lax.dynamic_slice_in_dim(upstream_rows, offset, tile_rows, 0)
        key_win = lax.dynamic_slice_in_dim(key_ext, offset, window, 0)
        value_win = lax.dynamic_slice_in_dim(value_ext, offset, window, 0)
        query_place = anchor + offset + jnp.arange(tile_rows, dtype=jnp.int32)
        key_place = anchor + offset - block_rows + jnp.arange(window, dtype=jnp.int32)
        context, query_grad, slope_grad, soft_weights, scaled_grads, log_total, row_delta = (
            tile_terms(
                query_tile,
                upstream_tile,
                key_win,
                value_win,
                query_place,
                key_place,
                length,
                slopes,
                block_rows,
                factor,
            )
        )
        key_acc, value_acc = running
        key_part = jnp.einsum(
            "hij,ihe->jhe", scaled_grads, query_tile, preferred_element_type=jnp.float32
        )
        value_part = jnp.einsum(
            "hij,ihe->jhe", soft_weights, upstream_tile, preferred_element_type=jnp.float32
        )
        key_acc = lax.dynamic_update_slice_in_dim(
            key_acc, lax.dynamic_slice_in_dim(key_acc, offset, window, 0) + key_part, offset, 0
        )
        value_acc = lax.dynamic_update_slice_in_dim(
            value_acc,
            lax.dynamic_slice_in_dim(value_acc, offset, window, 0) + value_part,
            offset,
            0,
        )
        running = (key_acc, value_acc)
        return (running, (context, query_grad, slope_grad, log_total, row_delta))

    (key_acc, value_acc), (contexts, query_grads, slope_grads, log_totals, row_deltas) = lax.scan(
        query_sweep, (zero_grads, zero_grads), offsets
    )
    grad_ext = jnp.concatenate([key_acc, value_acc], axis=2)
    own_grads = grad_ext[block_rows : block_rows + block_rows]
    for stride, outgoing in ((1, grad_ext[block_rows + block_rows :]), (-1, grad_ext[:block_rows])):
        own_grads = own_grads + from_behind(outgoing, "blk", stride)
    key_grad = own_grads[:, :, :head_size]
    value_grad = own_grads[:, :, head_size:]
    bias_part = jnp.sum(query_grads, axis=(0, 1))
    slope_part = jnp.sum(slope_grads, axis=0)
    bias_sum, slope_sum = lax.psum((bias_part, slope_part), ("dp", "blk"))
    context_out = contexts.reshape(1, block_rows, feature_width).astype(jnp.bfloat16)
    query_out = query_grads.reshape(1, block_rows, feature_width).astype(jnp.bfloat16)
    key_out = key_grad.reshape(1, block_rows, feature_width).astype(jnp.bfloat16)
    value_out = value_grad.reshape(1, block_rows, feature_width).astype(jnp.bfloat16)
    context_tok, query_tok, key_tok, value_tok = (
        lax.all_to_all(context_out, "uly", split_axis=1, concat_axis=2, tiled=True),
        lax.all_to_all(query_out, "uly", split_axis=1, concat_axis=2, tiled=True),
        lax.all_to_all(key_out, "uly", split_axis=1, concat_axis=2, tiled=True),
        lax.all_to_all(value_out, "uly", split_axis=1, concat_axis=2, tiled=True),
    )
    return (context_tok, query_tok, key_tok, value_tok, bias_sum, slope_sum)


def solution(mesh):
    placed = (
        P("dp", ("blk", "uly"), None),
        P("dp", ("blk", "uly"), None),
        P("dp", ("blk", "uly"), None),
        P("dp", ("blk", "uly"), None),
        P("uly", None),
        P("uly"),
        P("dp"),
    )
    return jax.shard_map(
        local,
        mesh=mesh,
        in_specs=placed,
        out_specs=(
            P("dp", ("blk", "uly"), None),
            P("dp", ("blk", "uly"), None),
            P("dp", ("blk", "uly"), None),
            P("dp", ("blk", "uly"), None),
            P("uly", None),
            P("uly"),
        ),
        check_vma=False,
    )
```

profile of v0, /device:TPU:390, one launch (start us, length us, event | category | flops | bytes accessed | tf_op | source)
XLA Modules:
  0.0 605.8 jit_solution(521256281550143878)
XLA Ops:
  2.5 2.2 reduce.2
  5.5 4.8 all-to-all-start.1
  11.5 2.2 reduce.1
  15.7 5.4 all-to-all-start.2
  21.6 2.2 reduce.3
  25.6 2.2 reduce
  28.6 4.8 all-to-all-start
  34.5 3.5 collective-permute-start
  38.0 8.4 %collective-permute-start.1 = (bf16[1024,256]{1,0:T(8,128)(2,1)S(1)}, bf16[1024,256]{1,0:T(8,128)(2,1)}, u32[]{:S(2)}, u32[]{:S(2)}) collective-permute-start(bf16[1024,256]{1,0:T(8,128)(2,1)S(1)} %pad_maximum_fusion.1), channel_id=1, source_target_pairs={{8,0},{16,8},{24,16},{32,24},{40,32},{48,40},{56,48},{64,56},{72,6... | collective-permute-start | bytes 1572872 | tf_op jit(solution)/shard_map/ppermute | solution.py:17
  46.4 4.8 all-to-all-start.3
  52.0 4.7 all-to-all-done.3
  58.6 9.2 %collective-permute-done = bf16[1024,256]{1,0:T(8,128)(2,1)} collective-permute-done((bf16[1024,256]{1,0:T(8,128)(2,1)S(1)}, bf16[1024,256]{1,0:T(8,128)(2,1)}, u32[]{:S(2)}, u32[]{:S(2)}) %collective-permute-start) | collective-permute-done | bytes 524320 | tf_op jit(solution)/shard_map/ppermute | solution.py:14
  73.3 246.8 %while.20 = (s32[]{:T(128)}, f32[3072,2,64]{0,2,1:T(8,128)}, f32[3072,2,64]{0,2,1:T(8,128)}, bf16[4,256,2,64]{1,3,2,0:T(8,128)(2,1)}, f32[4,256,2,64]{1,3,2,0:T(...) while((s32[]{:T(128)}, f32[3072,2,64]{0,2,1:T(8,128)}, ...), condition=%wide.region_5.6_spmd, body=%wide.region_0.5_spmd.sunk | while | flops 1261692672 | bytes 133755464 | solution.py:149
  85.8 1.6 fusion.141
  91.1 5.8 fusion.142
  99.2 2.2 multiply_reduce_fusion.3
  101.4 9.9 %fusion.146 = f32[4,256,2,64]{1,3,2,0:T(8,128)} fusion(f32[4,256,2,64]{1,3,2,0:T(8,128)} %get-tuple-element.384, s32[]{:T(128)} %get-tuple-element.380, f32[2,256,2304]{2,1,0:T(8,128)} %copy-done, bf16[3072,2,64]{0,2,1:T(8,128)(2,1)S(1)} %copy-done.5, s32[]{:T(128)S(6)} %select_n.72, f32[2,256,2304]{2,1,0:T(8,128)} %get-tuple-element.359, ...), kind=kOutput, calls=%fused_computation.27.clone.1 | convolution fusion | flops 159255296 | bytes 19599876 | tf_op jit(solution)/shard_map/while/body/eval_jaxpr/hij,jhe->ihe/dot_general | solution.py:62
  111.3 10.4 %fusion.143 = f32[2304,2,64]{0,2,1:T(8,128)S(1)} fusion(f32[3072,2,64]{0,2,1:T(8,128)} %get-tuple-element.381, s32[]{:T(128)S(6)} %select_n.72, f32[2,256,2304]{2,1,0:T(8,128)} %copy-done, bf16[1024,2,64]{0,2,1:T(8,128)(2,1)} %get-tuple-element.406, s32[]{:T(128)S(6)} %select_n.73, f32[2,256,2304]{2,1,0:T(8,128)} %get-tuple-element.359, ...), kind=kOutput, calls=%fused_computation.16.clone.1 | convolution fusion | flops 159550208 | bytes 21303304 | tf_op jit(solution)/shard_map/while/body/eval_jaxpr/hij,ihe->jhe/dot_general | solution.py:131
  121.7 5.7 dynamic_update_slice.41
  127.4 4.5 fusion.144
  131.9 5.6 dynamic_update_slice.42
  138.2 5.0 fusion.145
  150.6 5.8 fusion.142
  158.7 2.2 multiply_reduce_fusion.3
  160.9 9.9 %fusion.146 = f32[4,256,2,64]{1,3,2,0:T(8,128)} fusion(f32[4,256,2,64]{1,3,2,0:T(8,128)} %get-tuple-element.384, s32[]{:T(128)} %get-tuple-element.380, f32[2,256,2304]{2,1,0:T(8,128)} %copy-done, bf16[3072,2,64]{0,2,1:T(8,128)(2,1)S(1)} %copy-done.5, s32[]{:T(128)S(6)} %select_n.72, f32[2,256,2304]{2,1,0:T(8,128)} %get-tuple-element.359, ...), kind=kOutput, calls=%fused_computation.27.clone.1 | convolution fusion | flops 159255296 | bytes 19599876 | tf_op jit(solution)/shard_map/while/body/eval_jaxpr/hij,jhe->ihe/dot_general | solution.py:62
  170.9 10.4 %fusion.143 = f32[2304,2,64]{0,2,1:T(8,128)S(1)} fusion(f32[3072,2,64]{0,2,1:T(8,128)} %get-tuple-element.381, s32[]{:T(128)S(6)} %select_n.72, f32[2,256,2304]{2,1,0:T(8,128)} %copy-done, bf16[1024,2,64]{0,2,1:T(8,128)(2,1)} %get-tuple-element.406, s32[]{:T(128)S(6)} %select_n.73, f32[2,256,2304]{2,1,0:T(8,128)} %get-tuple-element.359, ...), kind=kOutput, calls=%fused_computation.16.clone.1 | convolution fusion | flops 159550208 | bytes 21303304 | tf_op jit(solution)/shard_map/while/body/eval_jaxpr/hij,ihe->jhe/dot_general | solution.py:131
  181.2 5.6 dynamic_update_slice.41
  186.8 4.5 fusion.144
  191.3 5.6 dynamic_update_slice.42
  197.6 5.0 fusion.145
  210.0 5.8 fusion.142
  218.1 2.2 multiply_reduce_fusion.3
  220.3 9.9 %fusion.146 = f32[4,256,2,64]{1,3,2,0:T(8,128)} fusion(f32[4,256,2,64]{1,3,2,0:T(8,128)} %get-tuple-element.384, s32[]{:T(128)} %get-tuple-element.380, f32[2,256,2304]{2,1,0:T(8,128)} %copy-done, bf16[3072,2,64]{0,2,1:T(8,128)(2,1)S(1)} %copy-done.5, s32[]{:T(128)S(6)} %select_n.72, f32[2,256,2304]{2,1,0:T(8,128)} %get-tuple-element.359, ...), kind=kOutput, calls=%fused_computation.27.clone.1 | convolution fusion | flops 159255296 | bytes 19599876 | tf_op jit(solution)/shard_map/while/body/eval_jaxpr/hij,jhe->ihe/dot_general | solution.py:62
  230.2 10.3 %fusion.143 = f32[2304,2,64]{0,2,1:T(8,128)S(1)} fusion(f32[3072,2,64]{0,2,1:T(8,128)} %get-tuple-element.381, s32[]{:T(128)S(6)} %select_n.72, f32[2,256,2304]{2,1,0:T(8,128)} %copy-done, bf16[1024,2,64]{0,2,1:T(8,128)(2,1)} %get-tuple-element.406, s32[]{:T(128)S(6)} %select_n.73, f32[2,256,2304]{2,1,0:T(8,128)} %get-tuple-element.359, ...), kind=kOutput, calls=%fused_computation.16.clone.1 | convolution fusion | flops 159550208 | bytes 21303304 | tf_op jit(solution)/shard_map/while/body/eval_jaxpr/hij,ihe->jhe/dot_general | solution.py:131
  240.6 5.5 dynamic_update_slice.41
  246.1 4.5 fusion.144
  250.6 5.5 dynamic_update_slice.42
  256.8 5.0 fusion.145
  269.1 5.7 fusion.142
  277.2 2.2 multiply_reduce_fusion.3
  279.4 9.9 %fusion.146 = f32[4,256,2,64]{1,3,2,0:T(8,128)} fusion(f32[4,256,2,64]{1,3,2,0:T(8,128)} %get-tuple-element.384, s32[]{:T(128)} %get-tuple-element.380, f32[2,256,2304]{2,1,0:T(8,128)} %copy-done, bf16[3072,2,64]{0,2,1:T(8,128)(2,1)S(1)} %copy-done.5, s32[]{:T(128)S(6)} %select_n.72, f32[2,256,2304]{2,1,0:T(8,128)} %get-tuple-element.359, ...), kind=kOutput, calls=%fused_computation.27.clone.1 | convolution fusion | flops 159255296 | bytes 19599876 | tf_op jit(solution)/shard_map/while/body/eval_jaxpr/hij,jhe->ihe/dot_general | solution.py:62
  289.3 10.3 %fusion.143 = f32[2304,2,64]{0,2,1:T(8,128)S(1)} fusion(f32[3072,2,64]{0,2,1:T(8,128)} %get-tuple-element.381, s32[]{:T(128)S(6)} %select_n.72, f32[2,256,2304]{2,1,0:T(8,128)} %copy-done, bf16[1024,2,64]{0,2,1:T(8,128)(2,1)} %get-tuple-element.406, s32[]{:T(128)S(6)} %select_n.73, f32[2,256,2304]{2,1,0:T(8,128)} %get-tuple-element.359, ...), kind=kOutput, calls=%fused_computation.16.clone.1 | convolution fusion | flops 159550208 | bytes 21303304 | tf_op jit(solution)/shard_map/while/body/eval_jaxpr/hij,ihe->jhe/dot_general | solution.py:131
  299.7 5.2 dynamic_update_slice.41
  304.8 4.5 fusion.144
  309.3 5.2 dynamic_update_slice.42
  315.1 5.0 fusion.145
  324.7 1.9 collective-permute-start.2
  326.6 11.6 %collective-permute-start.3 = (f32[1024,2,128]{0,2,1:T(8,128)}, f32[1024,2,128]{0,2,1:T(8,128)}, u32[]{:S(2)}, u32[]{:S(2)}) collective-permute-start(f32[1024,2,128]{0,2,1:T(8,128)} %get-tuple-element.261), channel_id=1, source_target_pairs={{8,0},{16,8},{24,16},{32,24},{40,32},{48,40},{56,48},{64,56},{72,6... | collective-permute-start | bytes 3145736 | tf_op jit(solution)/shard_map/ppermute | solution.py:25
  339.4 3.3 reshape.228
  342.7 3.1 reduce.5
  346.6 4.8 all-to-all-start.5
  351.4 2.0 copy.112
  353.3 3.3 reshape.227
  356.6 3.8 reduce.4
  360.4 1.7 reshape.237
  362.1 17.4 %collective-permute-done.2 = f32[1024,2,128]{0,2,1:T(8,128)} collective-permute-done((f32[1024,2,128]{0,2,1:T(8,128)}, f32[1024,2,128]{0,2,1:T(8,128)}, u32[]{:S(2)}, u32[]{:S(2)}) %collective-permute-start.2) | collective-permute-done | bytes 1048608 | tf_op jit(solution)/shard_map/ppermute | solution.py:25
  380.6 2.6 fusion.87
  383.2 4.8 all-to-all-start.4
  389.5 2.2 reduce.7
  393.5 5.4 all-to-all-start.7
  399.3 2.2 reduce.6
  402.3 2.1 all-to-all-done.7
  404.3 5.4 all-to-all-start.6
  409.8 190.2 %all-reduce = (f32[2,64]{1,0:T(2,128)}, f32[2]{0:T(128)}) all-reduce(f32[2,64]{1,0:T(2,128)S(1)} %get-tuple-element.264, f32[2]{0:T(128)S(1)} %reduce_sum.55), channel_id=1, replica_groups=mesh['dp'=4,'blk'=16,'uly'=8] {'dp','blk'}, use_global_device_ids=true, to_apply=%region_7.8 | all-reduce | flops 130 | bytes 1040 | tf_op jit(solution)/shard_map/psum | solution.py:160
  (178 shorter events, 59.1 us)
Async XLA Ops:
  0.6 20.5 %copy-start.7 = (bf16[1,128,1024]{2,1,0:T(8,128)(2,1)S(1)}, bf16[1,128,1024]{2,1,0:T(8,128)(2,1)}, u32[]{:S(2)}) copy-start(bf16[1,128,1024]{2,1,0:T(8,128)(2,1)} %param.12) | copy-start | bytes 786436
  0.6 24.6 %copy-start.8 = (bf16[1,128,1024]{2,1,0:T(8,128)(2,1)S(1)}, bf16[1,128,1024]{2,1,0:T(8,128)(2,1)}, u32[]{:S(2)}) copy-start(bf16[1,128,1024]{2,1,0:T(8,128)(2,1)} %param.9) | copy-start | bytes 786436
  5.5 10.2 %all-to-all-start.1 = ((bf16[8,2,8192]{2,1,0:T(2,128)(2,1)}), bf16[8,2,8192]{2,1,0:T(2,128)(2,1)S(1)}, u32[]{:S(2)}, u32[]{:S(2)}) async-start(bf16[8,2,8192]{2,1,0:T(2,128)(2,1)} %reshape.233), calls=%async_computation.1 | async-start | bytes 524288 | tf_op jit(solution)/shard_map/all_to_all | solution.py:81
  15.7 12.9 %all-to-all-start.2 = ((bf16[8,2,8192]{2,1,0:T(2,128)(2,1)}), bf16[8,2,8192]{2,1,0:T(2,128)(2,1)S(1)}, u32[]{:S(2)}, u32[]{:S(2)}) async-start(bf16[8,2,8192]{2,1,0:T(2,128)(2,1)} %reshape.231), calls=%async_computation.2 | async-start | bytes 524288 | tf_op jit(solution)/shard_map/all_to_all | solution.py:82
  28.6 17.8 %all-to-all-start = ((bf16[8,2,8192]{2,1,0:T(2,128)(2,1)}), bf16[8,2,8192]{2,1,0:T(2,128)(2,1)S(1)}, u32[]{:S(2)}, u32[]{:S(2)}) async-start(bf16[8,2,8192]{2,1,0:T(2,128)(2,1)} %reshape.229), calls=%async_computation | async-start | bytes 524288 | tf_op jit(solution)/shard_map/all_to_all | solution.py:80
  34.2 23.5 %copy-start.9 = (f32[2,64]{1,0:T(2,128)S(1)}, f32[2,64]{1,0:T(2,128)}, u32[]{:S(2)}) copy-start(f32[2,64]{1,0:T(2,128)} %param.13) | copy-start | bytes 1540
  34.5 33.2 %collective-permute-start = (bf16[1024,256]{1,0:T(8,128)(2,1)S(1)}, bf16[1024,256]{1,0:T(8,128)(2,1)}, u32[]{:S(2)}, u32[]{:S(2)}) collective-permute-start(bf16[1024,256]{1,0:T(8,128)(2,1)S(1)} %pad_maximum_fusion.1), channel_id=1, source_target_pairs={{0,8},{8,16},{16,24},{24,32},{32,40},{40,48},{48,56},{56,64},{64,7... | collective-permute-start | bytes 1572872 | tf_op jit(solution)/shard_map/ppermute | solution.py:14
  38.0 29.7 %collective-permute-start.1 = (bf16[1024,256]{1,0:T(8,128)(2,1)S(1)}, bf16[1024,256]{1,0:T(8,128)(2,1)}, u32[]{:S(2)}, u32[]{:S(2)}) collective-permute-start(bf16[1024,256]{1,0:T(8,128)(2,1)S(1)} %pad_maximum_fusion.1), channel_id=1, source_target_pairs={{8,0},{16,8},{24,16},{32,24},{40,32},{48,40},{56,48},{64,56},{72,6... | collective-permute-start | bytes 1572872 | tf_op jit(solution)/shard_map/ppermute | solution.py:17
  46.4 10.3 %all-to-all-start.3 = ((bf16[8,2,8192]{2,1,0:T(2,128)(2,1)}), bf16[8,2,8192]{2,1,0:T(2,128)(2,1)S(1)}, u32[]{:S(2)}, u32[]{:S(2)}) async-start(bf16[8,2,8192]{2,1,0:T(2,128)(2,1)} %reshape.235), calls=%async_computation.3 | async-start | bytes 524288 | tf_op jit(solution)/shard_map/all_to_all | solution.py:83
  69.1 4.3 copy-start.10
  83.7 13.1 %copy-start.1 = (bf16[3072,2,64]{0,2,1:T(8,128)(2,1)}, bf16[3072,2,64]{0,2,1:T(8,128)(2,1)S(1)}, u32[]{:S(2)}) copy-start(bf16[3072,2,64]{0,2,1:T(8,128)(2,1)S(1)} %get-tuple-element.412) | copy-start | bytes 2359300 | tf_op jit(solution)/shard_map/while
  83.7 13.1 %copy-start.3 = (bf16[1024,2,64]{0,2,1:T(8,128)(2,1)}, bf16[1024,2,64]{0,2,1:T(8,128)(2,1)S(1)}, u32[]{:S(2)}) copy-start(bf16[1024,2,64]{0,2,1:T(8,128)(2,1)S(1)} %get-tuple-element.411) | copy-start | bytes 786436 | tf_op jit(solution)/shard_map/while
  96.9 2.3 copy-start.11
  99.2 2.2 copy-start
  99.2 2.2 copy-start.5
  138.2 5.0 copy-start.2
  138.2 5.0 copy-start.4
  143.2 13.1 %copy-start.1 = (bf16[3072,2,64]{0,2,1:T(8,128)(2,1)}, bf16[3072,2,64]{0,2,1:T(8,128)(2,1)S(1)}, u32[]{:S(2)}) copy-start(bf16[3072,2,64]{0,2,1:T(8,128)(2,1)S(1)} %get-tuple-element.412) | copy-start | bytes 2359300 | tf_op jit(solution)/shard_map/while
  143.2 13.1 %copy-start.3 = (bf16[1024,2,64]{0,2,1:T(8,128)(2,1)}, bf16[1024,2,64]{0,2,1:T(8,128)(2,1)S(1)}, u32[]{:S(2)}) copy-start(bf16[1024,2,64]{0,2,1:T(8,128)(2,1)S(1)} %get-tuple-element.411) | copy-start | bytes 786436 | tf_op jit(solution)/shard_map/while
  156.4 2.3 copy-start.11
  158.7 2.2 copy-start
  158.7 2.2 copy-start.5
  197.6 5.0 copy-start.2
  197.6 5.0 copy-start.4
  202.6 13.1 %copy-start.1 = (bf16[3072,2,64]{0,2,1:T(8,128)(2,1)}, bf16[3072,2,64]{0,2,1:T(8,128)(2,1)S(1)}, u32[]{:S(2)}) copy-start(bf16[3072,2,64]{0,2,1:T(8,128)(2,1)S(1)} %get-tuple-element.412) | copy-start | bytes 2359300 | tf_op jit(solution)/shard_map/while
  202.6 13.1 %copy-start.3 = (bf16[1024,2,64]{0,2,1:T(8,128)(2,1)}, bf16[1024,2,64]{0,2,1:T(8,128)(2,1)S(1)}, u32[]{:S(2)}) copy-start(bf16[1024,2,64]{0,2,1:T(8,128)(2,1)S(1)} %get-tuple-element.411) | copy-start | bytes 786436 | tf_op jit(solution)/shard_map/while
  215.8 2.3 copy-start.11
  218.1 2.2 copy-start
  218.1 2.2 copy-start.5
  256.7 5.0 copy-start.2
  256.7 5.0 copy-start.4
  261.8 13.1 %copy-start.1 = (bf16[3072,2,64]{0,2,1:T(8,128)(2,1)}, bf16[3072,2,64]{0,2,1:T(8,128)(2,1)S(1)}, u32[]{:S(2)}) copy-start(bf16[3072,2,64]{0,2,1:T(8,128)(2,1)S(1)} %get-tuple-element.412) | copy-start | bytes 2359300 | tf_op jit(solution)/shard_map/while
  261.8 13.1 %copy-start.3 = (bf16[1024,2,64]{0,2,1:T(8,128)(2,1)}, bf16[1024,2,64]{0,2,1:T(8,128)(2,1)S(1)}, u32[]{:S(2)}) copy-start(bf16[1024,2,64]{0,2,1:T(8,128)(2,1)S(1)} %get-tuple-element.411) | copy-start | bytes 786436 | tf_op jit(solution)/shard_map/while
  274.9 2.3 copy-start.11
  277.2 2.2 copy-start
  277.2 2.2 copy-start.5
  315.1 5.0 copy-start.2
  315.1 5.0 copy-start.4
  320.1 18.1 %copy-start.6 = (f32[4,256,2,64]{1,3,2,0:T(8,128)S(1)}, f32[4,256,2,64]{1,3,2,0:T(8,128)}, u32[]{:S(2)}) copy-start(f32[4,256,2,64]{1,3,2,0:T(8,128)} %get-tuple-element.184) | copy-start | bytes 1572868
  324.7 54.8 %collective-permute-start.2 = (f32[1024,2,128]{0,2,1:T(8,128)}, f32[1024,2,128]{0,2,1:T(8,128)}, u32[]{:S(2)}, u32[]{:S(2)}) collective-permute-start(f32[1024,2,128]{0,2,1:T(8,128)} %get-tuple-element.260), channel_id=1, source_target_pairs={{0,8},{8,16},{16,24},{24,32},{32,40},{40,48},{48,56},{56,64},{64,7... | collective-permute-start | bytes 3145736 | tf_op jit(solution)/shard_map/ppermute | solution.py:25
  326.6 54.0 %collective-permute-start.3 = (f32[1024,2,128]{0,2,1:T(8,128)}, f32[1024,2,128]{0,2,1:T(8,128)}, u32[]{:S(2)}, u32[]{:S(2)}) collective-permute-start(f32[1024,2,128]{0,2,1:T(8,128)} %get-tuple-element.261), channel_id=1, source_target_pairs={{8,0},{16,8},{24,16},{32,24},{40,32},{48,40},{56,48},{64,56},{72,6... | collective-permute-start | bytes 3145736 | tf_op jit(solution)/shard_map/ppermute | solution.py:25
  346.6 36.6 %all-to-all-start.5 = ((bf16[8,2,8192]{2,1,0:T(2,128)(2,1)}), bf16[8,2,8192]{2,1,0:T(2,128)(2,1)S(1)}, u32[]{:S(2)}, u32[]{:S(2)}) async-start(bf16[8,2,8192]{2,1,0:T(2,128)(2,1)} %reshape.239), calls=%async_computation.5 | async-start | bytes 524288 | tf_op jit(solution)/shard_map/all_to_all | solution.py:167
  383.2 10.3 %all-to-all-start.4 = ((bf16[8,2,8192]{2,1,0:T(2,128)(2,1)}), bf16[8,2,8192]{2,1,0:T(2,128)(2,1)S(1)}, u32[]{:S(2)}, u32[]{:S(2)}) async-start(bf16[8,2,8192]{2,1,0:T(2,128)(2,1)} %reshape.237), calls=%async_computation.4 | async-start | bytes 524288 | tf_op jit(solution)/shard_map/all_to_all | solution.py:166
  393.5 10.9 %all-to-all-start.7 = ((bf16[8,2,8192]{2,1,0:T(2,128)(2,1)}), bf16[8,2,8192]{2,1,0:T(2,128)(2,1)S(1)}, u32[]{:S(2)}, u32[]{:S(2)}) async-start(bf16[8,2,8192]{2,1,0:T(2,128)(2,1)} %reshape.243), calls=%async_computation.7 | async-start | bytes 524288 | tf_op jit(solution)/shard_map/all_to_all | solution.py:169
  404.3 199.7 %all-to-all-start.6 = ((bf16[8,2,8192]{2,1,0:T(2,128)(2,1)}), bf16[8,2,8192]{2,1,0:T(2,128)(2,1)S(1)}, u32[]{:S(2)}, u32[]{:S(2)}) async-start(bf16[8,2,8192]{2,1,0:T(2,128)(2,1)} %reshape.241), calls=%async_computation.6 | async-start | bytes 524288 | tf_op jit(solution)/shard_map/all_to_all | solution.py:168
where the time goes:
time: 618 us; the launch traced here: 606 us
  blocking collectives  190 us (31%)
  matrix products  146 us (24%)
  local copies, waits for them, and re-layouts  91 us (15%)
  starting transfers between devices  65.6 us (11%)
  other arithmetic  48 us (8%)
  waiting for transfers between devices  36.6 us (6%)
  loops' own time  26.3 us (4%)
    psum x1, blocking collectives, local(): bias_sum, slope_sum = lax.psum((bias_part, slope_part), ('dp', 'blk'))  190 us
    dot_general x4, matrix products, query_sweep(): jnp.einsum('hij,ihe->jhe', scaled_grads, query_tile, preferred_element_ty...  41.4 us
    dot_general x4, matrix products, tile_terms(): jnp.einsum('hij,jhe->ihe', scaled_grads, key_win, preferred_element_type=...  39.7 us
    another operation x1, loops' own time, local(): lax.scan(query_sweep, (zero_grads, zero_grads), offsets)  26.3 us
    sub x4, matrix products, tile_terms(): powers = jnp.exp(scores - row_max)  23 us
    dynamic_update_slice x4, local copies, waits for them, and re-layouts, query_sweep(): lax.dynamic_update_slice_in_dim(value_acc, lax.dynamic_slice_in_dim(value...  21.9 us
    dynamic_update_slice x4, local copies, waits for them, and re-layouts, query_sweep(): lax.dynamic_update_slice_in_dim(key_acc, lax.dynamic_slice_in_dim(key_acc...  21.9 us
    unnamed x8, other arithmetic  20.2 us
  transfers between devices with their start and end apart: 12, of which 7 were waited for; matrix products, arithmetic and copies ran while one was open for 8% of the time, Pallas kernels for 0%

commit v1 on v0

v1 whole, which is shorter than its diff:
```python
import jax
import jax.numpy as jnp
from jax import lax
from jax.experimental import pallas as pl
from jax.experimental.pallas import tpu as pltpu
from jax.sharding import PartitionSpec as P

BLOCK = 1024
TILE = 256
HALO = BLOCK + TILE
PEERS = 8
CHUNK = BLOCK // PEERS
LANES = 128
HEAD = 64
FACTOR = HEAD**-0.5
LOG2E = 1.4426950408889634
FAR = 1e30
VMEM_LIMIT = 56 * 1024 * 1024
F32 = jnp.float32
BF16 = jnp.bfloat16


def iota(shape, dim):
    return lax.broadcasted_iota(jnp.int32, shape, dim)


def dot_nt(a, b):
    return lax.dot_general(a, b, (((1,), (1,)), ((), ())), preferred_element_type=F32)


def dot_nn(a, b):
    return jnp.dot(a, b, preferred_element_type=F32)


def own_lanes(head, shape):
    lane = iota(shape, 1)
    return lane < HEAD if head == 0 else lane >= HEAD


def spare(head):
    return HEAD if head == 0 else 0


def fill_keys(kv_ref, keys, values, base, start, length):
    shape = (CHUNK, LANES)
    lane = iota(shape, 1)
    for peer in range(PEERS):
        rows = pl.ds(base + peer * CHUNK, CHUNK)
        place = start + peer * CHUNK + iota(shape, 0)
        blocked = jnp.where((place >= 0) & (place < length), 0.0, -FAR)
        key = kv_ref[peer, 0].astype(F32)
        value = kv_ref[peer, 1].astype(F32)
        for head in range(2):
            own, at = own_lanes(head, shape), spare(head)
            keys[head, rows] = jnp.where(own, key, jnp.where(lane == at, blocked, 0.0)).astype(BF16)
            ones = ((lane >= at) & (lane < at + 3)).astype(F32)
            values[head, rows] = jnp.where(own, value, ones).astype(BF16)


def fill_penalty(slopes_ref, penalty):
    for head in range(2):
        slope = slopes_ref[head] * LOG2E
        for piece in range((2 * BLOCK + TILE) // TILE):
            spacing = jnp.abs(iota((TILE, TILE), 0) + BLOCK - piece * TILE - iota((TILE, TILE), 1))
            penalty[head, :, pl.ds(piece * TILE, TILE)] = jnp.where(
                spacing <= BLOCK, spacing.astype(F32) * slope, FAR
            )


def load_queries(qd_ref, bias_ref):
    query = jnp.concatenate([qd_ref[0, 0], qd_ref[1, 0]], axis=0).astype(F32)
    return (query + bias_ref[...]).astype(BF16).astype(F32)


def load_upstream(qd_ref, first, length):
    upstream = jnp.concatenate([qd_ref[0, 1], qd_ref[1, 1]], axis=0).astype(F32)
    place = first + iota((TILE, LANES), 0)
    return jnp.where(place < length, upstream, 0.0)


def with_spare(head, rows, columns):
    lane = iota((TILE, LANES), 1)
    other = jnp.zeros((TILE, LANES), F32)
    for k, column in enumerate(columns):
        other = jnp.where(lane == spare(head) + k, column, other)
    return jnp.where(own_lanes(head, (TILE, LANES)), rows, other)


def thirds(column):
    high = column.astype(BF16).astype(F32)
    middle = (column - high).astype(BF16).astype(F32)
    return high, middle, column - high - middle


def centre_forward(meta, slopes_ref, kv_ref, qd_ref, bias_ref, p_ref, o_ref, keys, values, penalty):
    tile = pl.program_id(0)

    @pl.when(tile == 0)
    def _():
        fill_keys(kv_ref, keys, values, 0, meta[0], meta[1])
        fill_penalty(slopes_ref, penalty)

    query = load_queries(qd_ref, bias_ref)
    for head in range(2):
        at = spare(head)
        rows = with_spare(head, query, (1.0,)).astype(BF16)
        shift = pl.multiple_of(BLOCK - tile * TILE, TILE)
        scores = dot_nt(rows, keys[head]) * (FACTOR * LOG2E) - penalty[head, :, pl.ds(shift, BLOCK)]
        top = jnp.max(scores, axis=1, keepdims=True)
        powers = jnp.exp2(scores - top).astype(BF16)
        p_ref[head] = powers
        out = dot_nn(powers, values[head])
        o_ref[head] = jnp.where(iota((TILE, LANES), 1) == at + 1, top, out)


def halo_both(
    meta,
    slopes_ref,
    low_ref,
    high_ref,
    qd_ref,
    bias_ref,
    o_ref,
    ctx_ref,
    dq_ref,
    stat_ref,
    dlow_ref,
    dhigh_ref,
    slope_ref,
    keys,
    values,
    penalty,
    dkt,
    dvt,
):
    tile = pl.program_id(0)
    first, length = meta[0], meta[1]

    @pl.when(tile == 0)
    def _():
        fill_keys(low_ref, keys, values, 0, first - BLOCK, length)
        fill_keys(high_ref, keys, values, BLOCK, first + BLOCK, length)
        fill_penalty(slopes_ref, penalty)
        dkt[...] = jnp.zeros_like(dkt)
        dvt[...] = jnp.zeros_like(dvt)
        slope_ref[...] = jnp.zeros_like(slope_ref)

    query = load_queries(qd_ref, bias_ref)
    upstream = load_upstream(qd_ref, first + tile * TILE, length)
    begin = pl.multiple_of(tile * TILE, TILE)
    span = pl.ds(begin, HALO)
    shape = (TILE, LANES)
    lane = iota(shape, 1)
    context = jnp.zeros(shape, F32)
    dq = jnp.zeros(shape, F32)
    stats = jnp.zeros(shape, F32)
    inverses, weights, grads = [], [], []
    for head in range(2):
        at, own = spare(head), own_lanes(head, shape)
        rows = with_spare(head, query, (1.0,)).astype(BF16)
        key_win = keys[head, span]
        value_win = values[head, span]
        pieces = []
        for piece in range(HALO // TILE):
            shift = jnp.where(piece < BLOCK // TILE - tile, piece * TILE, piece * TILE + BLOCK)
            pieces.append(penalty[head, :, pl.ds(pl.multiple_of(shift, TILE), TILE)])
        far = jnp.concatenate(pieces, axis=1)
        scores = dot_nt(rows, key_win) * (FACTOR * LOG2E) - far
        held = o_ref[head]
        top_held = held[:, at + 1 : at + 2]
        top = jnp.maximum(top_held, jnp.max(scores, axis=1, keepdims=True))
        powers = jnp.exp2(scores - top).astype(BF16)
        kept = jnp.exp2(top_held - top)
        out = held * kept + dot_nn(powers, value_win)
        inverse = 1.0 / out[:, at : at + 1]
        out = out * inverse
        delta = jnp.sum(jnp.where(own, upstream * out, 0.0), axis=1, keepdims=True)
        context = jnp.where(own, out, context)
        up_rows = with_spare(head, upstream, thirds(-delta)).astype(BF16)
        slope_grads = powers.astype(F32) * dot_nt(up_rows, value_win)
        score_grads = slope_grads.astype(BF16)
        dq = jnp.where(own, dot_nn(score_grads, key_win) * (inverse * FACTOR), dq)
        by_lane = jnp.zeros(shape, F32)
        weighted = slope_grads * far
        for piece in range(HALO // LANES):
            by_lane = by_lane + weighted[:, piece * LANES : (piece + 1) * LANES]
        slope_ref[pl.ds(head * 8, 8)] += jnp.broadcast_to(
            jnp.sum(by_lane * inverse, axis=0, keepdims=True), (8, LANES)
        )
        stats = jnp.where(lane == 2 * head, delta, stats)
        stats = jnp.where(lane == 2 * head + 1, kept * inverse, stats)
        inverses.append(inverse)
        weights.append(powers)
        grads.append(score_grads)
    place = first + tile * TILE + iota(shape, 0)
    ctx_ref[...] = jnp.where(place < length, context, 0.0).astype(BF16)
    dq_ref[...] = dq
    stat_ref[...] = stats
    inverse = jnp.where(lane < HEAD, inverses[0], inverses[1])
    up_cols = (upstream * inverse).T.astype(BF16)
    query_cols = (query * (inverse * FACTOR)).T.astype(BF16)
    for head in range(2):
        part = pl.ds(head * HEAD, HEAD)
        half = slice(head * HEAD, (head + 1) * HEAD)
        dvt[part, span] += dot_nn(up_cols[half], weights[head])
        dkt[part, span] += dot_nn(query_cols[half], grads[head])

    @pl.when(tile == BLOCK // TILE - 1)
    def _():
        for peer in range(PEERS):
            for side, out_ref in ((0, dlow_ref), (BLOCK, dhigh_ref)):
                cols = pl.ds(side + peer * CHUNK, CHUNK)
                out_ref[peer, 0] = dkt[:, cols].T.astype(BF16)
                out_ref[peer, 1] = dvt[:, cols].T.astype(BF16)


def centre_backward(
    meta,
    slopes_ref,
    kv_ref,
    qd_ref,
    bias_ref,
    p_ref,
    stat_ref,
    ctx_ref,
    dq_ref,
    halo_slope_ref,
    cq_ref,
    dkv_ref,
    sums_ref,
    keys,
    values,
    penalty,
    dkt,
    dvt,
    slope_acc,
):
    tile = pl.program_id(0)
    first, length = meta[0], meta[1]

    @pl.when(tile == 0)
    def _():
        fill_keys(kv_ref, keys, values, 0, first, length)
        fill_penalty(slopes_ref, penalty)
        dkt[...] = jnp.zeros_like(dkt)
        dvt[...] = jnp.zeros_like(dvt)
        slope_acc[...] = halo_slope_ref[...]
        sums_ref[...] = jnp.zeros_like(sums_ref)

    query = load_queries(qd_ref, bias_ref)
    upstream = load_upstream(qd_ref, first + tile * TILE, length)
    shift = pl.multiple_of(BLOCK - tile * TILE, TILE)
    shape = (TILE, LANES)
    lane = iota(shape, 1)
    dq = dq_ref[...]
    stats = stat_ref[...]
    scales = [stats[:, 2 * head + 1 : 2 * head + 2] for head in range(2)]
    scale = jnp.where(lane < HEAD, scales[0], scales[1])
    up_cols = (upstream * scale).T.astype(BF16)
    query_cols = (query * (scale * FACTOR)).T.astype(BF16)
    for head in range(2):
        own = own_lanes(head, shape)
        delta = stats[:, 2 * head : 2 * head + 1]
        up_rows = with_spare(head, upstream, thirds(-delta)).astype(BF16)
        powers = p_ref[head]
        slope_grads = powers.astype(F32) * dot_nt(up_rows, values[head])
        score_grads = slope_grads.astype(BF16)
        dq = dq + jnp.where(own, dot_nn(score_grads, keys[head]) * (scales[head] * FACTOR), 0.0)
        weighted = slope_grads * penalty[head, :, pl.ds(shift, BLOCK)]
        by_lane = jnp.zeros(shape, F32)
        for piece in range(BLOCK // LANES):
            by_lane = by_lane + weighted[:, piece * LANES : (piece + 1) * LANES]
        slope_acc[pl.ds(head * 8, 8)] += jnp.broadcast_to(
            jnp.sum(by_lane * scales[head], axis=0, keepdims=True), (8, LANES)
        )
        part = pl.ds(head * HEAD, HEAD)
        half = slice(head * HEAD, (head + 1) * HEAD)
        dvt[part] += dot_nn(up_cols[half], powers)
        dkt[part] += dot_nn(query_cols[half], score_grads)
    for half in range(2):
        rows = slice(half * CHUNK, (half + 1) * CHUNK)
        cq_ref[half, 0] = ctx_ref[rows]
        cq_ref[half, 1] = dq[rows].astype(BF16)
    sums_ref[0:1] += jnp.sum(dq, axis=0, keepdims=True)

    @pl.when(tile == BLOCK // TILE - 1)
    def _():
        row = iota((1, LANES), 1)
        totals = []
        for head in range(2):
            total = jnp.sum(slope_acc[pl.ds(head * 8, 1)], axis=1, keepdims=True)
            totals.append(-total / (slopes_ref[head] * LOG2E))
        sums_ref[1:2] = jnp.where(row == 0, totals[0], jnp.where(row == 1, totals[1], 0.0))
        for peer in range(PEERS):
            cols = pl.ds(peer * CHUNK, CHUNK)
            dkv_ref[peer, 0] = dkt[:, cols].T
            dkv_ref[peer, 1] = dvt[:, cols].T


SMEM = pl.BlockSpec(memory_space=pltpu.SMEM)
TILES = BLOCK // TILE


def whole(*shape):
    return pl.BlockSpec(shape, lambda tile: (0,) * len(shape))


def spec_rows(*shape):
    return pl.BlockSpec(shape, lambda tile: (tile,) + (0,) * (len(shape) - 1))


def spec_heads(width):
    return pl.BlockSpec((2, TILE, width), lambda tile: (0, tile, 0))


PAIR = (PEERS, 2, CHUNK, LANES)
PAIR_TILE = (2, 2, CHUNK, LANES)


def params():
    return pltpu.CompilerParams(
        dimension_semantics=("arbitrary",), vmem_limit_bytes=VMEM_LIMIT
    )


def cost(keys, products):
    pairs = 2 * BLOCK * keys
    return pl.CostEstimate(
        flops=2 * pairs * LANES * products, bytes_accessed=8 * 1024 * 1024, transcendentals=pairs
    )


def shaped(shape, kind):
    return jax.ShapeDtypeStruct(shape, kind)


def run_centre_forward(meta, slopes, kv, qd, bias):
    return pl.pallas_call(
        centre_forward,
        grid=(TILES,),
        in_specs=[SMEM, SMEM, whole(*PAIR), spec_rows(*PAIR_TILE), whole(1, LANES)],
        out_specs=[spec_heads(BLOCK), spec_heads(LANES)],
        out_shape=[shaped((2, BLOCK, BLOCK), BF16), shaped((2, BLOCK, LANES), F32)],
        scratch_shapes=[
            pltpu.VMEM((2, BLOCK, LANES), BF16),
            pltpu.VMEM((2, BLOCK, LANES), BF16),
            pltpu.VMEM((2, TILE, 2 * BLOCK + TILE), F32),
        ],
        compiler_params=params(),
        cost_estimate=cost(BLOCK, 2),
        name="centre_forward",
    )(meta, slopes, kv, qd, bias)


def run_halo(meta, slopes, low, high, qd, bias, held):
    return pl.pallas_call(
        halo_both,
        grid=(TILES,),
        in_specs=[
            SMEM,
            SMEM,
            whole(*PAIR),
            whole(*PAIR),
            spec_rows(*PAIR_TILE),
            whole(1, LANES),
            spec_heads(LANES),
        ],
        out_specs=[
            spec_rows(TILE, LANES),
            spec_rows(TILE, LANES),
            spec_rows(TILE, LANES),
            whole(*PAIR),
            whole(*PAIR),
            whole(16, LANES),
        ],
        out_shape=[
            shaped((BLOCK, LANES), BF16),
            shaped((BLOCK, LANES), F32),
            shaped((BLOCK, LANES), F32),
            shaped(PAIR, BF16),
            shaped(PAIR, BF16),
            shaped((16, LANES), F32),
        ],
        scratch_shapes=[
            pltpu.VMEM((2, 2 * BLOCK, LANES), BF16),
            pltpu.VMEM((2, 2 * BLOCK, LANES), BF16),
            pltpu.VMEM((2, TILE, 2 * BLOCK + TILE), F32),
            pltpu.VMEM((LANES, 2 * BLOCK), F32),
            pltpu.VMEM((LANES, 2 * BLOCK), F32),
        ],
        compiler_params=params(),
        cost_estimate=cost(HALO, 6),
        name="halo_both",
    )(meta, slopes, low, high, qd, bias, held)


def run_centre_backward(meta, slopes, kv, qd, bias, powers, stats, context, dq, halo_slope):
    return pl.pallas_call(
        centre_backward,
        grid=(TILES,),
        in_specs=[
            SMEM,
            SMEM,
            whole(*PAIR),
            spec_rows(*PAIR_TILE),
            whole(1, LANES),
            spec_heads(BLOCK),
            spec_rows(TILE, LANES),
            spec_rows(TILE, LANES),
            spec_rows(TILE, LANES),
            whole(16, LANES),
        ],
        out_specs=[spec_rows(*PAIR_TILE), whole(*PAIR), whole(2, LANES)],
        out_shape=[shaped(PAIR, BF16), shaped(PAIR, F32), shaped((2, LANES), F32)],
        scratch_shapes=[
            pltpu.VMEM((2, BLOCK, LANES), BF16),
            pltpu.VMEM((2, BLOCK, LANES), BF16),
            pltpu.VMEM((2, TILE, 2 * BLOCK + TILE), F32),
            pltpu.VMEM((LANES, BLOCK), F32),
            pltpu.VMEM((LANES, BLOCK), F32),
            pltpu.VMEM((16, LANES), F32),
        ],
        compiler_params=params(),
        cost_estimate=cost(BLOCK, 4),
        name="centre_backward",
    )(meta, slopes, kv, qd, bias, powers, stats, context, dq, halo_slope)


def split_pair(first_ref, second_ref, out_ref):
    for peer in range(PEERS):
        cols = pl.ds(peer * LANES, LANES)
        out_ref[peer, 0] = first_ref[0, :, cols]
        out_ref[peer, 1] = second_ref[0, :, cols]


def run_split(first, second):
    return pl.pallas_call(split_pair, out_shape=shaped(PAIR, BF16), name="split_pair")(first, second)


def join_pair(pair_ref, first_ref, second_ref):
    for peer in range(PEERS):
        cols = pl.ds(peer * LANES, LANES)
        first_ref[0, :, cols] = pair_ref[peer, 0]
        second_ref[0, :, cols] = pair_ref[peer, 1]


def run_join(pair):
    whole_rows = shaped((1, CHUNK, PEERS * LANES), BF16)
    return pl.pallas_call(join_pair, out_shape=[whole_rows, whole_rows], name="join_pair")(pair)


def across(pair):
    return lax.all_to_all(pair, "uly", split_axis=0, concat_axis=0, tiled=True)


def from_behind(block, distance):
    count = lax.axis_size("blk")
    route = [(i - distance, i) for i in range(count) if 0 <= i - distance < count]
    return lax.ppermute(block, "blk", route)


def local(queries, key_vectors, value_vectors, grad_context, content_bias, slopes, lengths):
    kv = across(run_split(key_vectors, value_vectors))
    low = from_behind(kv, 1)
    high = from_behind(kv, -1)
    qd = across(run_split(queries, grad_context))
    start = (lax.axis_index("blk") * BLOCK).astype(jnp.int32)
    meta = jnp.stack([start, lengths[0]])
    bias = content_bias.reshape(1, LANES)
    powers, held = run_centre_forward(meta, slopes, kv, qd, bias)
    context, dq, stats, dlow, dhigh, halo_slope = run_halo(
        meta, slopes, low, high, qd, bias, held
    )
    from_low = from_behind(dhigh, 1)
    from_high = from_behind(dlow, -1)
    cq, dkv, sums = run_centre_backward(
        meta, slopes, kv, qd, bias, powers, stats, context, dq, halo_slope
    )
    group = lax.axis_size("dp") * lax.axis_size("blk")
    spread = lax.all_to_all(
        jnp.broadcast_to(sums[None], (group, 2, LANES)), ("dp", "blk"), 0, 0, tiled=True
    )
    context_out, query_out = run_join(across(cq))
    dkv = (dkv + from_low.astype(F32) + from_high.astype(F32)).astype(BF16)
    key_out, value_out = run_join(across(dkv))
    total = jnp.sum(spread, axis=0)
    return (
        context_out,
        query_out,
        key_out,
        value_out,
        total[0].reshape(2, HEAD),
        total[1, :2],
    )


def solution(mesh):
    rows = P("dp", ("blk", "uly"), None)
    return jax.shard_map(
        local,
        mesh=mesh,
        in_specs=(rows, rows, rows, rows, P("uly", None), P("uly"), P("dp")),
        out_specs=(rows, rows, rows, rows, P("uly", None), P("uly")),
        check_vma=False,
    )
```

time: 618 us -> 154 us (0.25)
  the two profiles are of different devices: /device:TPU:390 before, /device:TPU:1 now
where the time goes in v1:
time: 154 us; the launch traced here: 153 us
  Pallas kernels  44.7 us (29%)
  blocking collectives  40.8 us (26%)
  starting transfers between devices  35.2 us (23%)
  waiting for transfers between devices  23.4 us (15%)
  local copies, waits for them, and re-layouts  5.11 us (3%)
  other arithmetic  2.91 us (2%)
    all_to_all x1, blocking collectives, local(): lax.all_to_all(jnp.broadcast_to(sums[None], (group, 2, LANES)), ('dp', 'b...  40.8 us
    all_to_all x4, starting transfers between devices, across(): return lax.all_to_all(pair, 'uly', split_axis=0, concat_axis=0, tiled=True)  26.8 us
    all_to_all x4, waiting for transfers between devices, across(): return lax.all_to_all(pair, 'uly', split_axis=0, concat_axis=0, tiled=True)  23.4 us
    pallas_call x1, Pallas kernels, run_halo(): pl.pallas_call(halo_both, grid=(TILES,), in_specs=[SMEM, SMEM, whole(*PAI...  19.3 us
    pallas_call x1, Pallas kernels, run_centre_backward(): pl.pallas_call(centre_backward, grid=(TILES,), in_specs=[SMEM, SMEM, whol...  9.58 us
    ppermute x4, starting transfers between devices, from_behind(): return lax.ppermute(block, 'blk', route)  8.34 us
    pallas_call x1, Pallas kernels, run_centre_forward(): pl.pallas_call(centre_forward, grid=(TILES,), in_specs=[SMEM, SMEM, whole...  8.01 us
    pallas_call x2, Pallas kernels, run_join(): pl.pallas_call(join_pair, out_shape=[whole_rows, whole_rows], name='join_...  3.95 us
  transfers between devices with their start and end apart: 8, of which 4 were waited for; matrix products, arithmetic and copies ran while one was open for 4% of the time, Pallas kernels for 14%

profile of v1, /device:TPU:1, one launch (start us, length us, event | category | flops | bytes accessed | tf_op | source)
XLA Modules:
  0.0 153.4 jit_solution(2959816945238249847)
XLA Ops:
  0.6 0.0 copy-start.6
  0.6 1.9 %split_pair.2 = bf16[8,2,128,128]{3,2,1,0:T(8,128)(2,1)} custom-call(bf16[1,128,1024]{2,1,0:T(8,128)(2,1)} %first_ref.2, bf16[1,128,1024]{2,1,0:T(8,128)(2,1)} %second_ref.2), custom_call_target="tpu_custom_call" | custom-call | tf_op jit(solution)/shard_map/split_pair/pallas_call | solution.py:437
  2.6 10.3 %all-to-all-start = ((bf16[8,2,128,128]{3,2,1,0:T(8,128)(2,1)}), bf16[8,2,128,128]{3,2,1,0:T(8,128)(2,1)S(1)}, u32[]{:S(2)}, u32[]{:S(2)}) async-start(bf16[8,2,128,128]{3,2,1,0:T(8,128)(2,1)} %split_pair.2), calls=%async_computation | async-start | bytes 1048576 | tf_op jit(solution)/shard_map/all_to_all | solution.py:453
  12.8 1.9 %split_pair.3 = bf16[8,2,128,128]{3,2,1,0:T(8,128)(2,1)} custom-call(bf16[1,128,1024]{2,1,0:T(8,128)(2,1)} %first_ref.3, bf16[1,128,1024]{2,1,0:T(8,128)(2,1)} %second_ref.3), custom_call_target="tpu_custom_call" | custom-call | tf_op jit(solution)/shard_map/split_pair/pallas_call | solution.py:437
  14.8 7.6 %all-to-all-done.kv_ref = bf16[8,2,128,128]{3,2,1,0:T(8,128)(2,1)S(1)} async-done(((bf16[8,2,128,128]{3,2,1,0:T(8,128)(2,1)}), bf16[8,2,128,128]{3,2,1,0:T(8,128)(2,1)S(1)}, u32[]{:S(2)}, u32[]{:S(2)}) %all-to-all-start) | async-done | bytes 524320 | tf_op jit(solution)/shard_map/all_to_all | solution.py:453
  22.3 0.0 copy-start.2
  22.3 4.3 %all-to-all-start.1 = ((bf16[8,2,128,128]{3,2,1,0:T(8,128)(2,1)}), bf16[8,2,128,128]{3,2,1,0:T(8,128)(2,1)S(1)}, u32[]{:S(2)}, u32[]{:S(2)}) async-start(bf16[8,2,128,128]{3,2,1,0:T(8,128)(2,1)} %split_pair.3), calls=%async_computation.1 | async-start | bytes 1048576 | tf_op jit(solution)/shard_map/all_to_all | solution.py:453
  26.6 1.3 collective-permute-start.1
  27.9 4.0 %collective-permute-start = (bf16[8,2,128,128]{3,2,1,0:T(8,128)(2,1)S(1)}, bf16[8,2,128,128]{3,2,1,0:T(8,128)(2,1)S(1)}, u32[]{:S(2)}, u32[]{:S(2)}) collective-permute-start(bf16[8,2,128,128]{3,2,1,0:T(8,128)(2,1)S(1)} %all-to-all-done.kv_ref), channel_id=1, source_target_pairs={{0,8},{8,16},{16,24},{24,32},{32,40},{40,48},{48,56},{56,64},{64,7... | collective-permute-start | bytes 1572872 | tf_op jit(solution)/shard_map/ppermute | solution.py:459
  32.6 0.0 copy-done.6
  32.6 0.6 reshape.16.bias_ref
  33.2 0.6 pad_add_fusion.meta
  33.8 2.3 %all-to-all-done.1.qd_ref = bf16[8,2,128,128]{3,2,1,0:T(8,128)(2,1)S(1)} async-done(((bf16[8,2,128,128]{3,2,1,0:T(8,128)(2,1)}), bf16[8,2,128,128]{3,2,1,0:T(8,128)(2,1)S(1)}, u32[]{:S(2)}, u32[]{:S(2)}) %all-to-all-start.1) | async-done | bytes 524320 | tf_op jit(solution)/shard_map/all_to_all | solution.py:453
  36.1 0.0 copy-done.2
  36.1 0.0 copy-start.3
  36.1 0.8 copy-done.3
  36.9 8.0 %centre_forward.1 = (bf16[2,1024,1024]{2,1,0:T(8,128)(2,1)}, f32[2,1024,128]{2,1,0:T(8,128)}) custom-call(s32[2]{0:T(128)} %pad_add_fusion.meta, f32[2]{0:T(128)} %slopes_ref.5, bf16[8,2,128,128]{3,2,1,0:T(8,128)(2,1)} %copy-done.2, bf16[8,2,128,128]{3,2,1,0:T(8,128)(2,1)} %copy-done.3, f32[1,128]{1,0:T(1,128)} %reshape.16.bias_ref), custom_call_target="tpu_custom_call" | custom-call | flops 1073741824 | bytes 8388608 | tf_op jit(solution)/shard_map/centre_forward/pallas_call | solution.py:338
  44.9 0.0 collective-permute-done.1.high_ref
  44.9 0.0 copy-start.4
  44.9 0.0 collective-permute-done.low_ref
  45.0 0.0 copy-start.5
  45.0 0.8 copy-done.4
  45.7 0.2 copy-done.5
  46.0 19.3 %halo_both.1 = (bf16[1024,128]{1,0:T(8,128)(2,1)}, f32[1024,128]{1,0:T(8,128)}, f32[1024,128]{1,0:T(8,128)}, bf16[8,2,128,128]{3,2,1,0:T(8,128)(2,1)}, bf16[8,2,...) custom-call(s32[2]{0:T(128)} %pad_add_fusion.meta, f32[2]{0:T(128)} %slopes_ref.5, bf16[8,2,128,128]{3,2,1,0:T(8,128)(2,1)} %copy-done.5, ...), custom_call_target="tpu_custom_call" | custom-call | flops 4026531840 | bytes 8388608 | tf_op jit(solution)/shard_map/halo_both/pallas_call | solution.py:356
  65.2 1.8 %collective-permute-start.2 = (bf16[8,2,128,128]{3,2,1,0:T(8,128)(2,1)}, bf16[8,2,128,128]{3,2,1,0:T(8,128)(2,1)S(1)}, u32[]{:S(2)}, u32[]{:S(2)}) collective-permute-start(bf16[8,2,128,128]{3,2,1,0:T(8,128)(2,1)} %get-tuple-element.31), channel_id=1, source_target_pairs={{0,8},{8,16},{16,24},{24,32},{32,40},{40,48},{48,56},{56,64},{64,7... | collective-permute-start | bytes 1572872 | tf_op jit(solution)/shard_map/ppermute | solution.py:459
  67.0 1.3 collective-permute-start.3
  68.3 9.6 %centre_backward.1 = (bf16[8,2,128,128]{3,2,1,0:T(8,128)(2,1)}, f32[8,2,128,128]{3,2,1,0:T(8,128)}, f32[2,128]{1,0:T(2,128)}) custom-call(s32[2]{0:T(128)} %pad_add_fusion.meta, f32[2]{0:T(128)} %slopes_ref.5, bf16[8,2,128,128]{3,2,1,0:T(8,128)(2,1)} %copy-done.2, bf16[8,2,128,128]{3,2,1,0:T(8,128)(2,1)} %copy-done.3, f32[1,128]{1,0:T(1,128)} %reshape.16.bias_ref, ...), custom_call_target="tpu_custom_call" | custom-call | flops 2147483648 | bytes 8388608 | tf_op jit(solution)/shard_map/centre_backward/pallas_call | solution.py:398
  77.9 0.7 broadcast_in_dim.2
  78.6 40.8 %all_to_all.25 = f32[64,2,128]{2,1,0:T(2,128)S(1)} all-to-all(f32[64,2,128]{2,1,0:T(2,128)S(1)} %broadcast_in_dim.2), channel_id=1, replica_groups=mesh['dp'=4,'blk'=16,'uly'=8] {'dp','blk'}, dimensions={0} | all-to-all | bytes 131072 | tf_op jit(solution)/shard_map/all_to_all | solution.py:480
  119.4 8.0 %all-to-all-start.2 = ((bf16[8,2,128,128]{3,2,1,0:T(8,128)(2,1)}), bf16[8,2,128,128]{3,2,1,0:T(8,128)(2,1)S(1)}, u32[]{:S(2)}, u32[]{:S(2)}) async-start(bf16[8,2,128,128]{3,2,1,0:T(8,128)(2,1)} %get-tuple-element.27), calls=%async_computation.2 | async-start | bytes 1048576 | tf_op jit(solution)/shard_map/all_to_all | solution.py:453
  127.4 0.0 collective-permute-done.2
  127.4 0.0 collective-permute-done.3
  127.4 2.2 %add_convert_fusion = bf16[8,2,128,128]{3,2,1,0:T(8,128)(2,1)} fusion(bf16[8,2,128,128]{3,2,1,0:T(8,128)(2,1)S(1)} %collective-permute-done.3, f32[8,2,128,128]{3,2,1,0:T(8,128)} %get-tuple-element.30, bf16[8,2,128,128]{3,2,1,0:T(8,128)(2,1)S(1)} %collective-permute-done.2), kind=kLoop, calls=%fused_computation | loop fusion | flops 1310720 | bytes 2621440 | tf_op jit(solution)/shard_map/convert_element_type | solution.py:484
  129.6 7.2 %all-to-all-done.2.pair_ref = bf16[8,2,128,128]{3,2,1,0:T(8,128)(2,1)S(1)} async-done(((bf16[8,2,128,128]{3,2,1,0:T(8,128)(2,1)}), bf16[8,2,128,128]{3,2,1,0:T(8,128)(2,1)S(1)}, u32[]{:S(2)}, u32[]{:S(2)}) %all-to-all-start.2) | async-done | bytes 524320 | tf_op jit(solution)/shard_map/all_to_all | solution.py:453
  136.9 0.0 copy-start
  136.9 4.3 %all-to-all-start.3 = ((bf16[8,2,128,128]{3,2,1,0:T(8,128)(2,1)}), bf16[8,2,128,128]{3,2,1,0:T(8,128)(2,1)S(1)}, u32[]{:S(2)}, u32[]{:S(2)}) async-start(bf16[8,2,128,128]{3,2,1,0:T(8,128)(2,1)} %add_convert_fusion), calls=%async_computation.3 | async-start | bytes 1048576 | tf_op jit(solution)/shard_map/all_to_all | solution.py:453
  141.1 0.1 reduce_sum.9
  141.2 0.6 reshape_squeeze.3
  141.9 0.5 slice_bitcast_fusion
  142.4 0.0 copy-done
  142.4 2.0 %join_pair.2 = (bf16[1,128,1024]{2,1,0:T(8,128)(2,1)}, bf16[1,128,1024]{2,1,0:T(8,128)(2,1)}) custom-call(bf16[8,2,128,128]{3,2,1,0:T(8,128)(2,1)} %copy-done), custom_call_target="tpu_custom_call" | custom-call | tf_op jit(solution)/shard_map/join_pair/pallas_call | solution.py:449
  144.4 6.3 %all-to-all-done.3.pair_ref = bf16[8,2,128,128]{3,2,1,0:T(8,128)(2,1)S(1)} async-done(((bf16[8,2,128,128]{3,2,1,0:T(8,128)(2,1)}), bf16[8,2,128,128]{3,2,1,0:T(8,128)(2,1)S(1)}, u32[]{:S(2)}, u32[]{:S(2)}) %all-to-all-start.3) | async-done | bytes 524320 | tf_op jit(solution)/shard_map/all_to_all | solution.py:453
  150.6 0.0 copy-start.1
  150.6 0.8 copy-done.1
  151.4 2.0 %join_pair.3 = (bf16[1,128,1024]{2,1,0:T(8,128)(2,1)}, bf16[1,128,1024]{2,1,0:T(8,128)(2,1)}) custom-call(bf16[8,2,128,128]{3,2,1,0:T(8,128)(2,1)} %copy-done.1), custom_call_target="tpu_custom_call" | custom-call | tf_op jit(solution)/shard_map/join_pair/pallas_call | solution.py:449
  (1 shorter events, 0.0 us)
Async XLA Ops:
  0.6 31.9 %copy-start.6 = (f32[2,64]{1,0:T(2,128)S(1)}, f32[2,64]{1,0:T(2,128)}, u32[]{:S(2)}) copy-start(f32[2,64]{1,0:T(2,128)} %param.11) | copy-start | bytes 1540
  2.6 19.8 %all-to-all-start = ((bf16[8,2,128,128]{3,2,1,0:T(8,128)(2,1)}), bf16[8,2,128,128]{3,2,1,0:T(8,128)(2,1)S(1)}, u32[]{:S(2)}, u32[]{:S(2)}) async-start(bf16[8,2,128,128]{3,2,1,0:T(8,128)(2,1)} %split_pair.2), calls=%async_computation | async-start | bytes 1048576 | tf_op jit(solution)/shard_map/all_to_all | solution.py:453
  22.3 13.8 %copy-start.2 = (bf16[8,2,128,128]{3,2,1,0:T(8,128)(2,1)}, bf16[8,2,128,128]{3,2,1,0:T(8,128)(2,1)S(1)}, u32[]{:S(2)}) copy-start(bf16[8,2,128,128]{3,2,1,0:T(8,128)(2,1)S(1)} %all-to-all-done.kv_ref) | copy-start | bytes 1572868
  22.3 13.8 %all-to-all-start.1 = ((bf16[8,2,128,128]{3,2,1,0:T(8,128)(2,1)}), bf16[8,2,128,128]{3,2,1,0:T(8,128)(2,1)S(1)}, u32[]{:S(2)}, u32[]{:S(2)}) async-start(bf16[8,2,128,128]{3,2,1,0:T(8,128)(2,1)} %split_pair.3), calls=%async_computation.1 | async-start | bytes 1048576 | tf_op jit(solution)/shard_map/all_to_all | solution.py:453
  26.6 18.3 %collective-permute-start.1 = (bf16[8,2,128,128]{3,2,1,0:T(8,128)(2,1)S(1)}, bf16[8,2,128,128]{3,2,1,0:T(8,128)(2,1)S(1)}, u32[]{:S(2)}, u32[]{:S(2)}) collective-permute-start(bf16[8,2,128,128]{3,2,1,0:T(8,128)(2,1)S(1)} %all-to-all-done.kv_ref), channel_id=1, source_target_pairs={{8,0},{16,8},{24,16},{32,24},{40,32},{48,40},{56,48},{64,56},{72,6... | collective-permute-start | bytes 1572872 | tf_op jit(solution)/shard_map/ppermute | solution.py:459
  27.9 17.0 %collective-permute-start = (bf16[8,2,128,128]{3,2,1,0:T(8,128)(2,1)S(1)}, bf16[8,2,128,128]{3,2,1,0:T(8,128)(2,1)S(1)}, u32[]{:S(2)}, u32[]{:S(2)}) collective-permute-start(bf16[8,2,128,128]{3,2,1,0:T(8,128)(2,1)S(1)} %all-to-all-done.kv_ref), channel_id=1, source_target_pairs={{0,8},{8,16},{16,24},{24,32},{32,40},{40,48},{48,56},{56,64},{64,7... | collective-permute-start | bytes 1572872 | tf_op jit(solution)/shard_map/ppermute | solution.py:459
  36.1 0.8 copy-start.3
  44.9 0.8 copy-start.4
  45.0 1.0 copy-start.5
  65.2 62.2 %collective-permute-start.2 = (bf16[8,2,128,128]{3,2,1,0:T(8,128)(2,1)}, bf16[8,2,128,128]{3,2,1,0:T(8,128)(2,1)S(1)}, u32[]{:S(2)}, u32[]{:S(2)}) collective-permute-start(bf16[8,2,128,128]{3,2,1,0:T(8,128)(2,1)} %get-tuple-element.31), channel_id=1, source_target_pairs={{0,8},{8,16},{16,24},{24,32},{32,40},{40,48},{48,56},{56,64},{64,7... | collective-permute-start | bytes 1572872 | tf_op jit(solution)/shard_map/ppermute | solution.py:459
  67.0 60.4 %collective-permute-start.3 = (bf16[8,2,128,128]{3,2,1,0:T(8,128)(2,1)}, bf16[8,2,128,128]{3,2,1,0:T(8,128)(2,1)S(1)}, u32[]{:S(2)}, u32[]{:S(2)}) collective-permute-start(bf16[8,2,128,128]{3,2,1,0:T(8,128)(2,1)} %get-tuple-element.32), channel_id=1, source_target_pairs={{8,0},{16,8},{24,16},{32,24},{40,32},{48,40},{56,48},{64,56},{72,6... | collective-permute-start | bytes 1572872 | tf_op jit(solution)/shard_map/ppermute | solution.py:459
  119.4 17.5 %all-to-all-start.2 = ((bf16[8,2,128,128]{3,2,1,0:T(8,128)(2,1)}), bf16[8,2,128,128]{3,2,1,0:T(8,128)(2,1)S(1)}, u32[]{:S(2)}, u32[]{:S(2)}) async-start(bf16[8,2,128,128]{3,2,1,0:T(8,128)(2,1)} %get-tuple-element.27), calls=%async_computation.2 | async-start | bytes 1048576 | tf_op jit(solution)/shard_map/all_to_all | solution.py:453
  136.9 5.5 %copy-start = (bf16[8,2,128,128]{3,2,1,0:T(8,128)(2,1)}, bf16[8,2,128,128]{3,2,1,0:T(8,128)(2,1)S(1)}, u32[]{:S(2)}) copy-start(bf16[8,2,128,128]{3,2,1,0:T(8,128)(2,1)S(1)} %all-to-all-done.2.pair_ref) | copy-start | bytes 1572868
  136.9 13.8 %all-to-all-start.3 = ((bf16[8,2,128,128]{3,2,1,0:T(8,128)(2,1)}), bf16[8,2,128,128]{3,2,1,0:T(8,128)(2,1)S(1)}, u32[]{:S(2)}, u32[]{:S(2)}) async-start(bf16[8,2,128,128]{3,2,1,0:T(8,128)(2,1)} %add_convert_fusion), calls=%async_computation.3 | async-start | bytes 1048576 | tf_op jit(solution)/shard_map/all_to_all | solution.py:453
  150.6 0.8 copy-start.1

commit v2 on v1

v2 whole, which is shorter than its diff:
```python
import jax
import jax.numpy as jnp
from jax import lax
from jax.experimental import pallas as pl
from jax.experimental.pallas import tpu as pltpu
from jax.sharding import PartitionSpec as P

BLOCK = 1024
TILE = 256
TILES = BLOCK // TILE
HALO = BLOCK + TILE
PEERS = 8
CHUNK = BLOCK // PEERS
LANES = 128
HEAD = 64
FACTOR = HEAD**-0.5
LOG2E = 1.4426950408889634
FAR = 1e30
VMEM_LIMIT = 40 * 1024 * 1024
F32 = jnp.float32
BF16 = jnp.bfloat16


def iota(shape, dim):
    return lax.broadcasted_iota(jnp.int32, shape, dim)


def dot_nt(a, b):
    return lax.dot_general(a, b, (((1,), (1,)), ((), ())), preferred_element_type=F32)


def dot_nn(a, b):
    return jnp.dot(a, b, preferred_element_type=F32)


def own_lanes(head, shape):
    lane = iota(shape, 1)
    return lane < HEAD if head == 0 else lane >= HEAD


def spare(head):
    return HEAD if head == 0 else 0


def fill_keys(kv_ref, keys, values, base, start, length):
    shape = (CHUNK, LANES)
    lane = iota(shape, 1)
    for peer in range(PEERS):
        rows = pl.ds(base + peer * CHUNK, CHUNK)
        place = start + peer * CHUNK + iota(shape, 0)
        blocked = jnp.where((place >= 0) & (place < length), 0.0, -FAR)
        key = kv_ref[peer, 0].astype(F32)
        value = kv_ref[peer, 1].astype(F32)
        for head in range(2):
            own, at = own_lanes(head, shape), spare(head)
            keys[head, rows] = jnp.where(own, key, jnp.where(lane == at, blocked, 0.0)).astype(BF16)
            ones = ((lane >= at) & (lane < at + 3)).astype(F32)
            values[head, rows] = jnp.where(own, value, ones).astype(BF16)


def fill_penalty(slopes_ref, penalty, pieces):
    for piece in pieces:
        spacing = jnp.abs(iota((TILE, TILE), 0) + BLOCK - piece * TILE - iota((TILE, TILE), 1))
        for head in range(2):
            cost_here = spacing.astype(F32) * (slopes_ref[head] * LOG2E)
            if piece in (0, 2 * BLOCK // TILE):
                cost_here = jnp.where(spacing <= BLOCK, cost_here, FAR)
            penalty[head, :, pl.ds(piece * TILE, TILE)] = cost_here


def load_queries(qd_ref, bias_ref, tile):
    query = jnp.concatenate([qd_ref[2 * tile, 0], qd_ref[2 * tile + 1, 0]], axis=0).astype(F32)
    return (query + bias_ref[...]).astype(BF16).astype(F32)


def load_upstream(qd_ref, tile, first, length):
    upstream = jnp.concatenate([qd_ref[2 * tile, 1], qd_ref[2 * tile + 1, 1]], axis=0).astype(F32)
    place = first + tile * TILE + iota((TILE, LANES), 0)
    return jnp.where(place < length, upstream, 0.0)


def with_spare(head, rows, columns):
    lane = iota((TILE, LANES), 1)
    other = jnp.zeros((TILE, LANES), F32)
    for k, column in enumerate(columns):
        other = jnp.where(lane == spare(head) + k, column, other)
    return jnp.where(own_lanes(head, (TILE, LANES)), rows, other)


def thirds(column):
    high = column.astype(BF16).astype(F32)
    middle = (column - high).astype(BF16).astype(F32)
    return high, middle, column - high - middle


def staggered(stages):
    chains = [{"tile": tile, "head": head} for tile in range(TILES) for head in range(2)]
    for step in range(len(chains) + len(stages) - 1):
        for depth, stage in enumerate(stages):
            if 0 <= step - depth < len(chains):
                stage(chains[step - depth], **{k: chains[step - depth][k] for k in ("tile", "head")})
    return chains


def head_half(head):
    return slice(head * HEAD, (head + 1) * HEAD)


def lane_sums(weighted):
    total = weighted[:, :LANES]
    for piece in range(1, weighted.shape[1] // LANES):
        total = total + weighted[:, piece * LANES : (piece + 1) * LANES]
    return total


def centre_forward(meta, slopes_ref, kv_ref, qd_ref, bias_ref, p_ref, o_ref, keys, values, penalty):
    fill_keys(kv_ref, keys, values, 0, meta[0], meta[1])
    fill_penalty(slopes_ref, penalty, range(1, 2 * BLOCK // TILE))

    def score(c, tile, head):
        rows = with_spare(head, load_queries(qd_ref, bias_ref, tile), (1.0,)).astype(BF16)
        far = penalty[head, :, pl.ds(BLOCK - tile * TILE, BLOCK)]
        c["scores"] = dot_nt(rows, keys[head]) * (FACTOR * LOG2E) - far

    def soften(c, tile, head):
        scores = c.pop("scores")
        c["top"] = jnp.max(scores, axis=1, keepdims=True)
        c["powers"] = jnp.exp2(scores - c["top"]).astype(BF16)

    def weigh(c, tile, head):
        rows = pl.ds(tile * TILE, TILE)
        powers = c.pop("powers")
        p_ref[head, rows] = powers
        out = dot_nn(powers, values[head])
        o_ref[head, rows] = jnp.where(iota((TILE, LANES), 1) == spare(head) + 1, c["top"], out)

    staggered([score, soften, weigh])


def halo_both(
    meta,
    slopes_ref,
    low_ref,
    high_ref,
    qd_ref,
    bias_ref,
    o_ref,
    ctx_ref,
    dq_ref,
    stat_ref,
    dlow_ref,
    dhigh_ref,
    slope_ref,
    keys,
    values,
    penalty,
    dkt,
    dvt,
):
    first, length = meta[0], meta[1]
    fill_keys(low_ref, keys, values, 0, first - BLOCK, length)
    fill_keys(high_ref, keys, values, BLOCK, first + BLOCK, length)
    fill_penalty(slopes_ref, penalty, [p for p in range(9) if p != BLOCK // TILE])
    dkt[...] = jnp.zeros_like(dkt)
    dvt[...] = jnp.zeros_like(dvt)
    shape = (TILE, LANES)
    lane = iota(shape, 1)

    def penalty_of(tile, head):
        low = penalty[head, :, pl.ds(0, BLOCK - tile * TILE)]
        high = penalty[head, :, pl.ds(2 * BLOCK - tile * TILE, (tile + 1) * TILE)]
        return jnp.concatenate([low, high], axis=1)

    def score(c, tile, head):
        c["span"] = pl.ds(tile * TILE, HALO)
        c["query"] = load_queries(qd_ref, bias_ref, tile)
        rows = with_spare(head, c["query"], (1.0,)).astype(BF16)
        scores = dot_nt(rows, keys[head, c["span"]]) * (FACTOR * LOG2E)
        c["scores"] = scores - penalty_of(tile, head)

    def soften(c, tile, head):
        scores = c.pop("scores")
        held = o_ref[head, pl.ds(tile * TILE, TILE)]
        top_held = held[:, spare(head) + 1 : spare(head) + 2]
        top = jnp.maximum(top_held, jnp.max(scores, axis=1, keepdims=True))
        c["powers"] = jnp.exp2(scores - top).astype(BF16)
        c["kept"] = jnp.exp2(top_held - top)

    def weigh(c, tile, head):
        held = o_ref[head, pl.ds(tile * TILE, TILE)]
        out = held * c["kept"] + dot_nn(c["powers"], values[head, c["span"]])
        c["inverse"] = 1.0 / out[:, spare(head) : spare(head) + 1]
        c["out"] = out * c["inverse"]

    def grade(c, tile, head):
        upstream = load_upstream(qd_ref, tile, first, length)
        c["upstream"] = upstream
        own = own_lanes(head, shape)
        c["delta"] = jnp.sum(jnp.where(own, upstream * c["out"], 0.0), axis=1, keepdims=True)
        up_rows = with_spare(head, upstream, thirds(-c["delta"])).astype(BF16)
        c["slope_grads"] = dot_nt(up_rows, values[head, c["span"]])

    def scale(c, tile, head):
        slope_grads = c["powers"].astype(F32) * c.pop("slope_grads")
        c["grads"] = slope_grads.astype(BF16)
        by_lane = lane_sums(slope_grads * penalty_of(tile, head)) * c["inverse"]
        c["slope"] = jnp.sum(by_lane, axis=0, keepdims=True)

    def spread(c, tile, head):
        inverse = c["inverse"]
        c["dq"] = dot_nn(c["grads"], keys[head, c["span"]]) * (inverse * FACTOR)
        part = pl.ds(head * HEAD, HEAD)
        up_cols = (c["upstream"] * inverse).T[head_half(head)].astype(BF16)
        query_cols = (c["query"] * (inverse * FACTOR)).T[head_half(head)].astype(BF16)
        dvt[part, c["span"]] += dot_nn(up_cols, c.pop("powers"))
        dkt[part, c["span"]] += dot_nn(query_cols, c.pop("grads"))

    def finish(c, tile, head):
        if head == 0:
            c_first[tile] = c
            return
        pair = (c_first[tile], c)
        rows = pl.ds(tile * TILE, TILE)
        place = first + tile * TILE + iota(shape, 0)
        context = jnp.where(lane < HEAD, pair[0]["out"], pair[1]["out"])
        ctx_ref[rows] = jnp.where(place < length, context, 0.0).astype(BF16)
        dq_ref[rows] = jnp.where(lane < HEAD, pair[0]["dq"], pair[1]["dq"])
        stats = jnp.zeros(shape, F32)
        for k in range(2):
            stats = jnp.where(lane == 2 * k, pair[k]["delta"], stats)
            stats = jnp.where(lane == 2 * k + 1, pair[k]["kept"] * pair[k]["inverse"], stats)
        stat_ref[rows] = stats

    c_first = {}
    chains = staggered([score, soften, weigh, grade, scale, spread, finish])
    for head in range(2):
        total = sum(c["slope"] for c in chains if c["head"] == head)
        slope_ref[pl.ds(head * 8, 8)] = jnp.broadcast_to(total, (8, LANES))
    for peer in range(PEERS):
        for side, out_ref in ((0, dlow_ref), (BLOCK, dhigh_ref)):
            cols = pl.ds(side + peer * CHUNK, CHUNK)
            out_ref[peer, 0] = dkt[:, cols].T.astype(BF16)
            out_ref[peer, 1] = dvt[:, cols].T.astype(BF16)


def centre_backward(
    meta,
    slopes_ref,
    kv_ref,
    qd_ref,
    bias_ref,
    p_ref,
    stat_ref,
    ctx_ref,
    dq_ref,
    halo_slope_ref,
    cq_ref,
    dkv_ref,
    sums_ref,
    keys,
    values,
    penalty,
    dkt,
    dvt,
):
    first, length = meta[0], meta[1]
    fill_keys(kv_ref, keys, values, 0, first, length)
    fill_penalty(slopes_ref, penalty, range(1, 2 * BLOCK // TILE))
    dkt[...] = jnp.zeros_like(dkt)
    dvt[...] = jnp.zeros_like(dvt)
    shape = (TILE, LANES)
    lane = iota(shape, 1)

    def grade(c, tile, head):
        stats = stat_ref[pl.ds(tile * TILE, TILE)]
        delta = stats[:, 2 * head : 2 * head + 1]
        c["scale"] = stats[:, 2 * head + 1 : 2 * head + 2]
        c["upstream"] = load_upstream(qd_ref, tile, first, length)
        up_rows = with_spare(head, c["upstream"], thirds(-delta)).astype(BF16)
        c["slope_grads"] = dot_nt(up_rows, values[head])

    def scale(c, tile, head):
        c["powers"] = p_ref[head, pl.ds(tile * TILE, TILE)]
        slope_grads = c["powers"].astype(F32) * c.pop("slope_grads")
        c["grads"] = slope_grads.astype(BF16)
        far = penalty[head, :, pl.ds(BLOCK - tile * TILE, BLOCK)]
        c["slope"] = jnp.sum(lane_sums(slope_grads * far) * c["scale"], axis=0, keepdims=True)

    def spread(c, tile, head):
        ratio = c["scale"]
        c["dq"] = dot_nn(c["grads"], keys[head]) * (ratio * FACTOR)
        part = pl.ds(head * HEAD, HEAD)
        query = load_queries(qd_ref, bias_ref, tile)
        up_cols = (c["upstream"] * ratio).T[head_half(head)].astype(BF16)
        query_cols = (query * (ratio * FACTOR)).T[head_half(head)].astype(BF16)
        dvt[part] += dot_nn(up_cols, c.pop("powers"))
        dkt[part] += dot_nn(query_cols, c.pop("grads"))

    def finish(c, tile, head):
        if head == 0:
            c_first[tile] = c
            return
        dq = jnp.where(lane < HEAD, c_first[tile]["dq"], c["dq"])
        dq = dq + dq_ref[pl.ds(tile * TILE, TILE)]
        c["bias"] = jnp.sum(dq, axis=0, keepdims=True)
        for half in range(2):
            rows = slice(half * CHUNK, (half + 1) * CHUNK)
            cq_ref[2 * tile + half, 0] = ctx_ref[pl.ds(tile * TILE + half * CHUNK, CHUNK)]
            cq_ref[2 * tile + half, 1] = dq[rows].astype(BF16)

    c_first = {}
    chains = staggered([grade, scale, spread, finish])
    sums_ref[0:1] = sum(c["bias"] for c in chains if c["head"] == 1)
    row = iota((1, LANES), 1)
    totals = []
    for head in range(2):
        total = sum(c["slope"] for c in chains if c["head"] == head)
        total = jnp.sum(total + halo_slope_ref[pl.ds(head * 8, 1)], axis=1, keepdims=True)
        totals.append(-total / (slopes_ref[head] * LOG2E))
    sums_ref[1:2] = jnp.where(row == 0, totals[0], jnp.where(row == 1, totals[1], 0.0))
    for peer in range(PEERS):
        cols = pl.ds(peer * CHUNK, CHUNK)
        dkv_ref[peer, 0] = dkt[:, cols].T
        dkv_ref[peer, 1] = dvt[:, cols].T


SMEM = pl.BlockSpec(memory_space=pltpu.SMEM)
VMEM = pl.BlockSpec(memory_space=pltpu.VMEM)
PAIR = (PEERS, 2, CHUNK, LANES)


def params():
    return pltpu.CompilerParams(vmem_limit_bytes=VMEM_LIMIT)


def cost(keys, products):
    pairs = 2 * BLOCK * keys
    return pl.CostEstimate(
        flops=2 * pairs * LANES * products, bytes_accessed=8 * 1024 * 1024, transcendentals=pairs
    )


def shaped(shape, kind):
    return jax.ShapeDtypeStruct(shape, kind)


def run_centre_forward(meta, slopes, kv, qd, bias):
    return pl.pallas_call(
        centre_forward,
        in_specs=[SMEM, SMEM] + [VMEM] * 3,
        out_specs=[VMEM] * 2,
        out_shape=[shaped((2, BLOCK, BLOCK), BF16), shaped((2, BLOCK, LANES), F32)],
        scratch_shapes=[
            pltpu.VMEM((2, BLOCK, LANES), BF16),
            pltpu.VMEM((2, BLOCK, LANES), BF16),
            pltpu.VMEM((2, TILE, 2 * BLOCK + TILE), F32),
        ],
        compiler_params=params(),
        cost_estimate=cost(BLOCK, 2),
        name="centre_forward",
    )(meta, slopes, kv, qd, bias)


def run_halo(meta, slopes, low, high, qd, bias, held):
    return pl.pallas_call(
        halo_both,
        in_specs=[SMEM, SMEM] + [VMEM] * 5,
        out_specs=[VMEM] * 6,
        out_shape=[
            shaped((BLOCK, LANES), BF16),
            shaped((BLOCK, LANES), F32),
            shaped((BLOCK, LANES), F32),
            shaped(PAIR, BF16),
            shaped(PAIR, BF16),
            shaped((16, LANES), F32),
        ],
        scratch_shapes=[
            pltpu.VMEM((2, 2 * BLOCK, LANES), BF16),
            pltpu.VMEM((2, 2 * BLOCK, LANES), BF16),
            pltpu.VMEM((2, TILE, 2 * BLOCK + TILE), F32),
            pltpu.VMEM((LANES, 2 * BLOCK), F32),
            pltpu.VMEM((LANES, 2 * BLOCK), F32),
        ],
        compiler_params=params(),
        cost_estimate=cost(HALO, 6),
        name="halo_both",
    )(meta, slopes, low, high, qd, bias, held)


def run_centre_backward(meta, slopes, kv, qd, bias, powers, stats, context, dq, halo_slope):
    return pl.pallas_call(
        centre_backward,
        in_specs=[SMEM, SMEM] + [VMEM] * 8,
        out_specs=[VMEM] * 3,
        out_shape=[shaped(PAIR, BF16), shaped(PAIR, F32), shaped((2, LANES), F32)],
        scratch_shapes=[
            pltpu.VMEM((2, BLOCK, LANES), BF16),
            pltpu.VMEM((2, BLOCK, LANES), BF16),
            pltpu.VMEM((2, TILE, 2 * BLOCK + TILE), F32),
            pltpu.VMEM((LANES, BLOCK), F32),
            pltpu.VMEM((LANES, BLOCK), F32),
        ],
        compiler_params=params(),
        cost_estimate=cost(BLOCK, 4),
        name="centre_backward",
    )(meta, slopes, kv, qd, bias, powers, stats, context, dq, halo_slope)


def split_pair(first_ref, second_ref, out_ref):
    for peer in range(PEERS):
        cols = pl.ds(peer * LANES, LANES)
        out_ref[peer, 0] = first_ref[0, :, cols]
        out_ref[peer, 1] = second_ref[0, :, cols]


def run_split(first, second):
    return pl.pallas_call(split_pair, out_shape=shaped(PAIR, BF16), name="split_pair")(first, second)


def gather_grads(cq_ref, dkv_ref, low_ref, high_ref, out_ref):
    for peer in range(PEERS):
        for part in range(2):
            out_ref[peer, part] = cq_ref[peer, part]
            passed = low_ref[peer, part].astype(F32) + high_ref[peer, part].astype(F32)
            out_ref[peer, 2 + part] = (dkv_ref[peer, part] + passed).astype(BF16)


def run_gather(cq, dkv, from_low, from_high):
    return pl.pallas_call(
        gather_grads, out_shape=shaped((PEERS, 4, CHUNK, LANES), BF16), name="gather_grads"
    )(cq, dkv, from_low, from_high)


def join_four(parts_ref, *out_refs):
    for peer in range(PEERS):
        cols = pl.ds(peer * LANES, LANES)
        for part in range(4):
            out_refs[part][0, :, cols] = parts_ref[peer, part]


def run_join(parts):
    whole_rows = shaped((1, CHUNK, PEERS * LANES), BF16)
    return pl.pallas_call(join_four, out_shape=[whole_rows] * 4, name="join_four")(parts)


def across(pair):
    return lax.all_to_all(pair, "uly", split_axis=0, concat_axis=0, tiled=True)


def from_behind(block, distance):
    count = lax.axis_size("blk")
    route = [(i - distance, i) for i in range(count) if 0 <= i - distance < count]
    return lax.ppermute(block, "blk", route)


def local(queries, key_vectors, value_vectors, grad_context, content_bias, slopes, lengths):
    kv = across(run_split(key_vectors, value_vectors))
    low = from_behind(kv, 1)
    high = from_behind(kv, -1)
    qd = across(run_split(queries, grad_context))
    start = (lax.axis_index("blk") * BLOCK).astype(jnp.int32)
    meta = jnp.stack([start, lengths[0]])
    bias = content_bias.reshape(1, LANES)
    powers, held = run_centre_forward(meta, slopes, kv, qd, bias)
    context, dq, stats, dlow, dhigh, halo_slope = run_halo(
        meta, slopes, low, high, qd, bias, held
    )
    from_low = from_behind(dhigh, 1)
    from_high = from_behind(dlow, -1)
    cq, dkv, sums = run_centre_backward(
        meta, slopes, kv, qd, bias, powers, stats, context, dq, halo_slope
    )
    group = lax.axis_size("dp") * lax.axis_size("blk")
    spread = lax.all_to_all(
        jnp.broadcast_to(sums[None], (group, 2, LANES)), ("dp", "blk"), 0, 0, tiled=True
    )
    grads = run_gather(cq, dkv, from_low, from_high)
    context_out, query_out, key_out, value_out = run_join(across(grads))
    total = jnp.sum(spread, axis=0)
    return (
        context_out,
        query_out,
        key_out,
        value_out,
        total[0].reshape(2, HEAD),
        total[1, :2],
    )


def solution(mesh):
    rows = P("dp", ("blk", "uly"), None)
    return jax.shard_map(
        local,
        mesh=mesh,
        in_specs=(rows, rows, rows, rows, P("uly", None), P("uly"), P("dp")),
        out_specs=(rows, rows, rows, rows, P("uly", None), P("uly")),
        check_vma=False,
    )
```

time: 154 us -> 137 us (0.89)
  blocking collectives: 40.8 us -> 0 us
  starting transfers between devices: 35.2 us -> 63.4 us
  Pallas kernels: 44.7 us -> 31.4 us
  waiting for transfers between devices: 23.4 us -> 34.6 us
  other arithmetic: 2.91 us -> 0.15 us
    all_to_all x1 -> x0, blocking collectives: 40.8 us -> none  [local(): lax.all_to_all(jnp.broadcast_to(sums[None], (group, 2, LANES)), ('dp', 'b...]
    all_to_all x0 -> x1, starting transfers between devices: none -> 30.1 us  [local(): lax.all_to_all(jnp.broadcast_to(sums[None], (group, 2, LANES)), ('dp', 'b...]
    pallas_call x5, Pallas kernels: 40.8 us -> 27.5 us  [the longest x1 11.6 us: run_halo(): pl.pallas_call(halo_both, in_specs=[SMEM, SMEM] + [VMEM] * 5, out_specs=[...]
    all_to_all x0 -> x1, waiting for transfers between devices: none -> 7.26 us  [local(): lax.all_to_all(jnp.broadcast_to(sums[None], (group, 2, LANES)), ('dp', 'b...]
    all_to_all x4 -> x3, starting transfers between devices: 26.8 us -> 22.6 us  [across(): return lax.all_to_all(pair, 'uly', split_axis=0, concat_axis=0, tiled=True)]
    ppermute x4, waiting for transfers between devices: 0.01 us -> 2.51 us  [from_behind(): return lax.ppermute(block, 'blk', route)]
    ppermute x4, starting transfers between devices: 8.34 us -> 10.7 us  [from_behind(): return lax.ppermute(block, 'blk', route)]
    convert_element_type x1 -> x0, other arithmetic: 2.24 us -> none  [local(): dkv = (dkv + from_low.astype(F32) + from_high.astype(F32)).astype(BF16)]
  transfers between devices with their start and end apart: 8 -> 8, of which waited for: 4 -> 6; matrix products, arithmetic and copies ran while one was open for 4% -> 2% of each run, Pallas kernels for 14% -> 11%
where the time goes in v2:
time: 137 us; the launch traced here: 136 us
  starting transfers between devices  63.4 us (46%)
  waiting for transfers between devices  34.6 us (25%)
  Pallas kernels  31.4 us (23%)
  local copies, waits for them, and re-layouts  5.47 us (4%)
  between operations  1.41 us (1%)
    all_to_all x1, starting transfers between devices, local(): lax.all_to_all(jnp.broadcast_to(sums[None], (group, 2, LANES)), ('dp', 'b...  30.1 us
    all_to_all x3, waiting for transfers between devices, across(): return lax.all_to_all(pair, 'uly', split_axis=0, concat_axis=0, tiled=True)  24.8 us
    all_to_all x3, starting transfers between devices, across(): return lax.all_to_all(pair, 'uly', split_axis=0, concat_axis=0, tiled=True)  22.6 us
    pallas_call x1, Pallas kernels, run_halo(): pl.pallas_call(halo_both, in_specs=[SMEM, SMEM] + [VMEM] * 5, out_specs=[...  11.6 us
    ppermute x4, starting transfers between devices, from_behind(): return lax.ppermute(block, 'blk', route)  10.7 us
    all_to_all x1, waiting for transfers between devices, local(): lax.all_to_all(jnp.broadcast_to(sums[None], (group, 2, LANES)), ('dp', 'b...  7.26 us
    pallas_call x1, Pallas kernels, run_centre_backward(): pl.pallas_call(centre_backward, in_specs=[SMEM, SMEM] + [VMEM] * 8, out_s...  6.46 us
    pallas_call x1, Pallas kernels, run_centre_forward(): pl.pallas_call(centre_forward, in_specs=[SMEM, SMEM] + [VMEM] * 3, out_sp...  4.12 us
  transfers between devices with their start and end apart: 8, of which 6 were waited for; matrix products, arithmetic and copies ran while one was open for 2% of the time, Pallas kernels for 11%

profile of v2, /device:TPU:1, one launch (start us, length us, event | category | flops | bytes accessed | tf_op | source)
XLA Modules:
  0.0 136.3 jit_solution(7067221854668119126)
XLA Ops:
  0.6 0.0 copy-start.5
  0.6 0.0 copy-start.2
  0.7 1.9 %split_pair.2 = bf16[8,2,128,128]{3,2,1,0:T(8,128)(2,1)} custom-call(bf16[1,128,1024]{2,1,0:T(8,128)(2,1)} %first_ref.2, bf16[1,128,1024]{2,1,0:T(8,128)(2,1)} %second_ref.2), custom_call_target="tpu_custom_call" | custom-call | tf_op jit(solution)/shard_map/split_pair/pallas_call | solution.py:417
  2.6 10.3 %all-to-all-start = ((bf16[8,2,128,128]{3,2,1,0:T(8,128)(2,1)}), bf16[8,2,128,128]{3,2,1,0:T(8,128)(2,1)S(1)}, u32[]{:S(2)}, u32[]{:S(2)}) async-start(bf16[8,2,128,128]{3,2,1,0:T(8,128)(2,1)} %split_pair.2), calls=%async_computation | async-start | bytes 1048576 | tf_op jit(solution)/shard_map/all_to_all | solution.py:447
  12.9 1.9 %split_pair.3 = bf16[8,2,128,128]{3,2,1,0:T(8,128)(2,1)} custom-call(bf16[1,128,1024]{2,1,0:T(8,128)(2,1)} %first_ref.3, bf16[1,128,1024]{2,1,0:T(8,128)(2,1)} %second_ref.3), custom_call_target="tpu_custom_call" | custom-call | tf_op jit(solution)/shard_map/split_pair/pallas_call | solution.py:417
  14.8 7.6 %all-to-all-done.kv_ref = bf16[8,2,128,128]{3,2,1,0:T(8,128)(2,1)S(1)} async-done(((bf16[8,2,128,128]{3,2,1,0:T(8,128)(2,1)}), bf16[8,2,128,128]{3,2,1,0:T(8,128)(2,1)S(1)}, u32[]{:S(2)}, u32[]{:S(2)}) %all-to-all-start) | async-done | bytes 524320 | tf_op jit(solution)/shard_map/all_to_all | solution.py:447
  22.4 4.3 %all-to-all-start.1 = ((bf16[8,2,128,128]{3,2,1,0:T(8,128)(2,1)}), bf16[8,2,128,128]{3,2,1,0:T(8,128)(2,1)S(1)}, u32[]{:S(2)}, u32[]{:S(2)}) async-start(bf16[8,2,128,128]{3,2,1,0:T(8,128)(2,1)} %split_pair.3), calls=%async_computation.1 | async-start | bytes 1048576 | tf_op jit(solution)/shard_map/all_to_all | solution.py:447
  26.6 1.3 collective-permute-start.1
  27.9 4.0 %collective-permute-start = (bf16[8,2,128,128]{3,2,1,0:T(8,128)(2,1)S(1)}, bf16[8,2,128,128]{3,2,1,0:T(8,128)(2,1)S(1)}, u32[]{:S(2)}, u32[]{:S(2)}) collective-permute-start(bf16[8,2,128,128]{3,2,1,0:T(8,128)(2,1)S(1)} %all-to-all-done.kv_ref), channel_id=1, source_target_pairs={{0,8},{8,16},{16,24},{24,32},{32,40},{40,48},{48,56},{56,64},{64,7... | collective-permute-start | bytes 1572872 | tf_op jit(solution)/shard_map/ppermute | solution.py:453
  32.6 0.0 copy-done.5
  32.6 0.1 reshape.16.bias_ref
  32.7 0.1 pad_add_fusion.meta
  32.8 3.4 %all-to-all-done.1.qd_ref = bf16[8,2,128,128]{3,2,1,0:T(8,128)(2,1)S(1)} async-done(((bf16[8,2,128,128]{3,2,1,0:T(8,128)(2,1)}), bf16[8,2,128,128]{3,2,1,0:T(8,128)(2,1)S(1)}, u32[]{:S(2)}, u32[]{:S(2)}) %all-to-all-start.1) | async-done | bytes 524320 | tf_op jit(solution)/shard_map/all_to_all | solution.py:447
  36.1 0.0 copy-done.2
  36.1 4.1 %centre_forward.1 = (bf16[2,1024,1024]{2,1,0:T(8,128)(2,1)S(1)}, f32[2,1024,128]{2,1,0:T(8,128)S(1)}) custom-call(s32[2]{0:T(128)S(1)} %pad_add_fusion.meta, f32[2]{0:T(128)S(1)} %copy-done.2, bf16[8,2,128,128]{3,2,1,0:T(8,128)(2,1)S(1)} %all-to-all-done.kv_ref, bf16[8,2,128,128]{3,2,1,0:T(8,128)(2,1)S(1)} %all-to-all-done.1.qd_ref, ...), custom_call_target="tpu_custom_call" | custom-call | flops 1073741824 | bytes 8388608 | tf_op jit(solution)/shard_map/centre_forward/pallas_call | solution.py:348
  40.2 1.6 %collective-permute-done.1.high_ref = bf16[8,2,128,128]{3,2,1,0:T(8,128)(2,1)S(1)} collective-permute-done((bf16[8,2,128,128]{3,2,1,0:T(8,128)(2,1)S(1)}, bf16[8,2,128,128]{3,2,1,0:T(8,128)(2,1)S(1)}, u32[]{:S(2)}, u32[]{:S(2)}) %collective-permute-start.1) | collective-permute-done | bytes 524320 | tf_op jit(solution)/shard_map/ppermute | solution.py:453
  41.9 0.9 collective-permute-done.low_ref
  42.8 11.6 %halo_both.1 = (bf16[1024,128]{1,0:T(8,128)(2,1)S(1)}, f32[1024,128]{1,0:T(8,128)S(1)}, f32[1024,128]{1,0:T(8,128)S(1)}, bf16[8,2,128,128]{3,2,1,0:T(8,128)(2,1)...) custom-call(s32[2]{0:T(128)S(1)} %pad_add_fusion.meta, f32[2]{0:T(128)S(1)} %copy-done.2, ...), custom_call_target="tpu_custom_call" | custom-call | flops 4026531840 | bytes 8388608 | tf_op jit(solution)/shard_map/halo_both/pallas_call | solution.py:365
  54.4 4.1 %collective-permute-start.2 = (bf16[8,2,128,128]{3,2,1,0:T(8,128)(2,1)S(1)}, bf16[8,2,128,128]{3,2,1,0:T(8,128)(2,1)S(1)}, u32[]{:S(2)}, u32[]{:S(2)}) collective-permute-start(bf16[8,2,128,128]{3,2,1,0:T(8,128)(2,1)S(1)} %get-tuple-element.29), channel_id=1, source_target_pairs={{0,8},{8,16},{16,24},{24,32},{32,40},{40,48},{48,56},{56,64},{64,7... | collective-permute-start | bytes 1572872 | tf_op jit(solution)/shard_map/ppermute | solution.py:453
  58.5 1.3 collective-permute-start.3
  59.8 6.5 %centre_backward.1 = (bf16[8,2,128,128]{3,2,1,0:T(8,128)(2,1)S(1)}, f32[8,2,128,128]{3,2,1,0:T(8,128)S(1)}, f32[2,128]{1,0:T(2,128)S(1)}) custom-call(s32[2]{0:T(128)S(1)} %pad_add_fusion.meta, f32[2]{0:T(128)S(1)} %copy-done.2, bf16[8,2,128,128]{3,2,1,0:T(8,128)(2,1)S(1)} %all-to-all-done.kv_ref, bf16[8,2,128,128]{3,2,1,0:T(8,128)(2,1)S(1)} %all-to-all-done.1.qd_ref, ...), custom_call_target="tpu_custom_call" | custom-call | flops 2147483648 | bytes 8388608 | tf_op jit(solution)/shard_map/centre_backward/pallas_call | solution.py:391
  66.3 0.0 copy-start
  66.3 1.0 copy-done
  67.3 0.0 copy-start.1
  67.3 0.8 copy-done.1
  68.1 0.6 broadcast_in_dim.2
  68.8 30.1 %all-to-all-start.3 = ((f32[64,2,128]{2,1,0:T(2,128)}), f32[64,2,128]{2,1,0:T(2,128)S(1)}, u32[]{:S(2)}, u32[]{:S(2)}) async-start(f32[64,2,128]{2,1,0:T(2,128)} %broadcast_in_dim.2), calls=%async_computation.3 | async-start | bytes 131072 | tf_op jit(solution)/shard_map/all_to_all | solution.py:474
  98.9 0.0 collective-permute-done.2.low_ref
  98.9 0.0 copy-start.4
  98.9 0.0 collective-permute-done.3.high_ref
  98.9 0.8 copy-done.4
  99.7 2.8 %gather_grads.1 = bf16[8,4,128,128]{3,2,1,0:T(8,128)(2,1)} custom-call(bf16[8,2,128,128]{3,2,1,0:T(8,128)(2,1)} %copy-done.1, f32[8,2,128,128]{3,2,1,0:T(8,128)} %copy-done, bf16[8,2,128,128]{3,2,1,0:T(8,128)(2,1)} %copy-done.4, bf16[8,2,128,128]{3,2,1,0:T(8,128)(2,1)} %collective-permute-done.3.high_ref), custom_call_target="tpu_custom_call" | custom-call | tf_op jit(solution)/shard_map/gather_grads/pallas_call | solution.py:429
  102.5 7.3 %all-to-all-done.3 = f32[64,2,128]{2,1,0:T(2,128)S(1)} async-done(((f32[64,2,128]{2,1,0:T(2,128)}), f32[64,2,128]{2,1,0:T(2,128)S(1)}, u32[]{:S(2)}, u32[]{:S(2)}) %all-to-all-start.3) | async-done | bytes 65568 | tf_op jit(solution)/shard_map/all_to_all | solution.py:474
  109.8 8.0 %all-to-all-start.2 = ((bf16[8,4,128,128]{3,2,1,0:T(8,128)(2,1)}), bf16[8,4,128,128]{3,2,1,0:T(8,128)(2,1)S(1)}, u32[]{:S(2)}, u32[]{:S(2)}) async-start(bf16[8,4,128,128]{3,2,1,0:T(8,128)(2,1)} %gather_grads.1), calls=%async_computation.2 | async-start | bytes 2097152 | tf_op jit(solution)/shard_map/all_to_all | solution.py:447
  117.8 0.1 reduce_sum.9
  117.9 0.6 reshape_squeeze.3
  118.5 0.5 slice_bitcast_fusion
  119.0 13.8 %all-to-all-done.2.parts_ref = bf16[8,4,128,128]{3,2,1,0:T(8,128)(2,1)S(1)} async-done(((bf16[8,4,128,128]{3,2,1,0:T(8,128)(2,1)}), bf16[8,4,128,128]{3,2,1,0:T(8,128)(2,1)S(1)}, u32[]{:S(2)}, u32[]{:S(2)}) %all-to-all-start.2) | async-done | bytes 1048608 | tf_op jit(solution)/shard_map/all_to_all | solution.py:447
  132.9 0.0 copy-start.3
  132.9 1.0 copy-done.3
  133.9 2.5 %join_four.1 = (bf16[1,128,1024]{2,1,0:T(8,128)(2,1)}, bf16[1,128,1024]{2,1,0:T(8,128)(2,1)}, bf16[1,128,1024]{2,1,0:T(8,128)(2,1)}, bf16[1,128,1024]{2,1,0:T(8,128)(2,1)}) custom-call(bf16[8,4,128,128]{3,2,1,0:T(8,128)(2,1)} %copy-done.3), custom_call_target="tpu_custom_call" | custom-call | tf_op jit(solution)/shard_map/join_four/pallas_call | solution.py:443
  (1 shorter events, 0.0 us)
Async XLA Ops:
  0.6 32.0 %copy-start.5 = (f32[2,64]{1,0:T(2,128)S(1)}, f32[2,64]{1,0:T(2,128)}, u32[]{:S(2)}) copy-start(f32[2,64]{1,0:T(2,128)} %param.11) | copy-start | bytes 1540
  0.6 35.5 %copy-start.2 = (f32[2]{0:T(128)S(1)}, f32[2]{0:T(128)}, u32[]{:S(2)}) copy-start(f32[2]{0:T(128)} %slopes_ref.5) | copy-start | bytes 28
  2.6 19.8 %all-to-all-start = ((bf16[8,2,128,128]{3,2,1,0:T(8,128)(2,1)}), bf16[8,2,128,128]{3,2,1,0:T(8,128)(2,1)S(1)}, u32[]{:S(2)}, u32[]{:S(2)}) async-start(bf16[8,2,128,128]{3,2,1,0:T(8,128)(2,1)} %split_pair.2), calls=%async_computation | async-start | bytes 1048576 | tf_op jit(solution)/shard_map/all_to_all | solution.py:447
  22.4 13.8 %all-to-all-start.1 = ((bf16[8,2,128,128]{3,2,1,0:T(8,128)(2,1)}), bf16[8,2,128,128]{3,2,1,0:T(8,128)(2,1)S(1)}, u32[]{:S(2)}, u32[]{:S(2)}) async-start(bf16[8,2,128,128]{3,2,1,0:T(8,128)(2,1)} %split_pair.3), calls=%async_computation.1 | async-start | bytes 1048576 | tf_op jit(solution)/shard_map/all_to_all | solution.py:447
  26.6 15.3 %collective-permute-start.1 = (bf16[8,2,128,128]{3,2,1,0:T(8,128)(2,1)S(1)}, bf16[8,2,128,128]{3,2,1,0:T(8,128)(2,1)S(1)}, u32[]{:S(2)}, u32[]{:S(2)}) collective-permute-start(bf16[8,2,128,128]{3,2,1,0:T(8,128)(2,1)S(1)} %all-to-all-done.kv_ref), channel_id=1, source_target_pairs={{8,0},{16,8},{24,16},{32,24},{40,32},{48,40},{56,48},{64,56},{72,6... | collective-permute-start | bytes 1572872 | tf_op jit(solution)/shard_map/ppermute | solution.py:453
  27.9 14.8 %collective-permute-start = (bf16[8,2,128,128]{3,2,1,0:T(8,128)(2,1)S(1)}, bf16[8,2,128,128]{3,2,1,0:T(8,128)(2,1)S(1)}, u32[]{:S(2)}, u32[]{:S(2)}) collective-permute-start(bf16[8,2,128,128]{3,2,1,0:T(8,128)(2,1)S(1)} %all-to-all-done.kv_ref), channel_id=1, source_target_pairs={{0,8},{8,16},{16,24},{24,32},{32,40},{40,48},{48,56},{56,64},{64,7... | collective-permute-start | bytes 1572872 | tf_op jit(solution)/shard_map/ppermute | solution.py:453
  54.4 44.5 %collective-permute-start.2 = (bf16[8,2,128,128]{3,2,1,0:T(8,128)(2,1)S(1)}, bf16[8,2,128,128]{3,2,1,0:T(8,128)(2,1)S(1)}, u32[]{:S(2)}, u32[]{:S(2)}) collective-permute-start(bf16[8,2,128,128]{3,2,1,0:T(8,128)(2,1)S(1)} %get-tuple-element.29), channel_id=1, source_target_pairs={{0,8},{8,16},{16,24},{24,32},{32,40},{40,48},{48,56},{56,64},{64,7... | collective-permute-start | bytes 1572872 | tf_op jit(solution)/shard_map/ppermute | solution.py:453
  58.5 40.3 %collective-permute-start.3 = (bf16[8,2,128,128]{3,2,1,0:T(8,128)(2,1)S(1)}, bf16[8,2,128,128]{3,2,1,0:T(8,128)(2,1)}, u32[]{:S(2)}, u32[]{:S(2)}) collective-permute-start(bf16[8,2,128,128]{3,2,1,0:T(8,128)(2,1)S(1)} %get-tuple-element.30), channel_id=1, source_target_pairs={{8,0},{16,8},{24,16},{32,24},{40,32},{48,40},{56,48},{64,56},{72,6... | collective-permute-start | bytes 1572872 | tf_op jit(solution)/shard_map/ppermute | solution.py:453
  66.3 1.0 copy-start
  67.3 0.8 copy-start.1
  68.8 41.0 %all-to-all-start.3 = ((f32[64,2,128]{2,1,0:T(2,128)}), f32[64,2,128]{2,1,0:T(2,128)S(1)}, u32[]{:S(2)}, u32[]{:S(2)}) async-start(f32[64,2,128]{2,1,0:T(2,128)} %broadcast_in_dim.2), calls=%async_computation.3 | async-start | bytes 131072 | tf_op jit(solution)/shard_map/all_to_all | solution.py:474
  98.9 0.8 copy-start.4
  109.8 23.1 %all-to-all-start.2 = ((bf16[8,4,128,128]{3,2,1,0:T(8,128)(2,1)}), bf16[8,4,128,128]{3,2,1,0:T(8,128)(2,1)S(1)}, u32[]{:S(2)}, u32[]{:S(2)}) async-start(bf16[8,4,128,128]{3,2,1,0:T(8,128)(2,1)} %gather_grads.1), calls=%async_computation.2 | async-start | bytes 2097152 | tf_op jit(solution)/shard_map/all_to_all | solution.py:447
  132.9 1.0 copy-start.3

commit v3 on v2

--- a/solution.py
+++ b/solution.py
@@ -46,7 +46,7 @@
     shape = (CHUNK, LANES)
     lane = iota(shape, 1)
     for peer in range(PEERS):
-        rows = pl.ds(base + peer * CHUNK, CHUNK)
+        rows = pl.ds(pl.multiple_of(base + peer * CHUNK, CHUNK), CHUNK)
         place = start + peer * CHUNK + iota(shape, 0)
         blocked = jnp.where((place >= 0) & (place < length), 0.0, -FAR)
         key = kv_ref[peer, 0].astype(F32)
@@ -140,16 +140,16 @@
 def halo_both(
     meta,
     slopes_ref,
-    low_ref,
-    high_ref,
+    second_ref,
+    first_ref,
     qd_ref,
     bias_ref,
     o_ref,
     ctx_ref,
     dq_ref,
     stat_ref,
-    dlow_ref,
-    dhigh_ref,
+    dfirst_ref,
+    dsecond_ref,
     slope_ref,
     keys,
     values,
@@ -158,8 +158,9 @@
     dvt,
 ):
     first, length = meta[0], meta[1]
-    fill_keys(low_ref, keys, values, 0, first - BLOCK, length)
-    fill_keys(high_ref, keys, values, BLOCK, first + BLOCK, length)
+    odd = lax.rem(first // BLOCK, 2)
+    fill_keys(first_ref, keys, values, odd * BLOCK, first + (2 * odd - 1) * BLOCK, length)
+    fill_keys(second_ref, keys, values, (1 - odd) * BLOCK, first - (2 * odd - 1) * BLOCK, length)
     fill_penalty(slopes_ref, penalty, [p for p in range(9) if p != BLOCK // TILE])
     dkt[...] = jnp.zeros_like(dkt)
     dvt[...] = jnp.zeros_like(dvt)
@@ -237,8 +238,8 @@
         total = sum(c["slope"] for c in chains if c["head"] == head)
         slope_ref[pl.ds(head * 8, 8)] = jnp.broadcast_to(total, (8, LANES))
     for peer in range(PEERS):
-        for side, out_ref in ((0, dlow_ref), (BLOCK, dhigh_ref)):
-            cols = pl.ds(side + peer * CHUNK, CHUNK)
+        for side, out_ref in ((odd, dfirst_ref), (1 - odd, dsecond_ref)):
+            cols = pl.ds(pl.multiple_of(side * BLOCK + peer * CHUNK, CHUNK), CHUNK)
             out_ref[peer, 0] = dkt[:, cols].T.astype(BF16)
             out_ref[peer, 1] = dvt[:, cols].T.astype(BF16)
 
@@ -356,12 +357,12 @@
             pltpu.VMEM((2, TILE, 2 * BLOCK + TILE), F32),
         ],
         compiler_params=params(),
-        cost_estimate=cost(BLOCK, 2),
+        cost_estimate=pl.CostEstimate(flops=1000, bytes_accessed=1000, transcendentals=0),
         name="centre_forward",
     )(meta, slopes, kv, qd, bias)
 
 
-def run_halo(meta, slopes, low, high, qd, bias, held):
+def run_halo(meta, slopes, kv_first, kv_second, qd, bias, held):
     return pl.pallas_call(
         halo_both,
         in_specs=[SMEM, SMEM] + [VMEM] * 5,
@@ -384,7 +385,7 @@
         compiler_params=params(),
         cost_estimate=cost(HALO, 6),
         name="halo_both",
-    )(meta, slopes, low, high, qd, bias, held)
+    )(meta, slopes, kv_second, kv_first, qd, bias, held)
 
 
 def run_centre_backward(meta, slopes, kv, qd, bias, powers, stats, context, dq, halo_slope):
@@ -401,7 +402,7 @@
             pltpu.VMEM((LANES, BLOCK), F32),
         ],
         compiler_params=params(),
-        cost_estimate=cost(BLOCK, 4),
+        cost_estimate=pl.CostEstimate(flops=1000, bytes_accessed=1000, transcendentals=0),
         name="centre_backward",
     )(meta, slopes, kv, qd, bias, powers, stats, context, dq, halo_slope)
 
@@ -417,18 +418,18 @@
     return pl.pallas_call(split_pair, out_shape=shaped(PAIR, BF16), name="split_pair")(first, second)
 
 
-def gather_grads(cq_ref, dkv_ref, low_ref, high_ref, out_ref):
+def gather_grads(cq_ref, dkv_ref, first_ref, second_ref, out_ref):
     for peer in range(PEERS):
         for part in range(2):
             out_ref[peer, part] = cq_ref[peer, part]
-            passed = low_ref[peer, part].astype(F32) + high_ref[peer, part].astype(F32)
+            passed = first_ref[peer, part].astype(F32) + second_ref[peer, part].astype(F32)
             out_ref[peer, 2 + part] = (dkv_ref[peer, part] + passed).astype(BF16)
 
 
-def run_gather(cq, dkv, from_low, from_high):
+def run_gather(cq, dkv, from_first, from_second):
     return pl.pallas_call(
         gather_grads, out_shape=shaped((PEERS, 4, CHUNK, LANES), BF16), name="gather_grads"
-    )(cq, dkv, from_low, from_high)
+    )(cq, dkv, from_first, from_second)
 
 
 def join_four(parts_ref, *out_refs):
@@ -447,26 +448,25 @@
     return lax.all_to_all(pair, "uly", split_axis=0, concat_axis=0, tiled=True)
 
 
-def from_behind(block, distance):
-    count = lax.axis_size("blk")
-    route = [(i - distance, i) for i in range(count) if 0 <= i - distance < count]
-    return lax.ppermute(block, "blk", route)
+def swapped(block, lowest):
+    pairs = [(i, i + 1) for i in range(lowest, lax.axis_size("blk") - 1, 2)]
+    return lax.ppermute(block, "blk", pairs + [(high, low) for low, high in pairs])
 
 
 def local(queries, key_vectors, value_vectors, grad_context, content_bias, slopes, lengths):
     kv = across(run_split(key_vectors, value_vectors))
-    low = from_behind(kv, 1)
-    high = from_behind(kv, -1)
+    kv_first = swapped(kv, 1)
+    kv_second = swapped(kv, 0)
     qd = across(run_split(queries, grad_context))
     start = (lax.axis_index("blk") * BLOCK).astype(jnp.int32)
     meta = jnp.stack([start, lengths[0]])
     bias = content_bias.reshape(1, LANES)
     powers, held = run_centre_forward(meta, slopes, kv, qd, bias)
-    context, dq, stats, dlow, dhigh, halo_slope = run_halo(
-        meta, slopes, low, high, qd, bias, held
-    )
-    from_low = from_behind(dhigh, 1)
-    from_high = from_behind(dlow, -1)
+    context, dq, stats, dfirst, dsecond, halo_slope = run_halo(
+        meta, slopes, kv_first, kv_second, qd, bias, held
+    )
+    from_first = swapped(dfirst, 1)
+    from_second = swapped(dsecond, 0)
     cq, dkv, sums = run_centre_backward(
         meta, slopes, kv, qd, bias, powers, stats, context, dq, halo_slope
     )
@@ -474,7 +474,7 @@
     spread = lax.all_to_all(
         jnp.broadcast_to(sums[None], (group, 2, LANES)), ("dp", "blk"), 0, 0, tiled=True
     )
-    grads = run_gather(cq, dkv, from_low, from_high)
+    grads = run_gather(cq, dkv, from_first, from_second)
     context_out, query_out, key_out, value_out = run_join(across(grads))
     total = jnp.sum(spread, axis=0)
     return (

time: 137 us -> 127 us (0.927)
  starting transfers between devices: 63.4 us -> 39 us
  blocking collectives: 0 us -> 19.6 us
  waiting for transfers between devices: 34.6 us -> 30.7 us
    all_to_all x0 -> x1, blocking collectives: none -> 19.6 us  [across(): return lax.all_to_all(pair, 'uly', split_axis=0, concat_axis=0, tiled=True)]
    all_to_all x1, starting transfers between devices: 30.1 us -> 15.8 us  [local(): lax.all_to_all(jnp.broadcast_to(sums[None], (group, 2, LANES)), ('dp', 'b...]
    all_to_all x3 -> x2, starting transfers between devices: 22.6 us -> 13.1 us  [across(): return lax.all_to_all(pair, 'uly', split_axis=0, concat_axis=0, tiled=True)]
    ppermute x4, waiting for transfers between devices: 2.51 us -> 0.01 us  [swapped(): lax.ppermute(block, 'blk', pairs + [(high, low) for low, high in pairs])]
    all_to_all x3 -> x2, waiting for transfers between devices: 24.8 us -> 22.5 us  [across(): return lax.all_to_all(pair, 'uly', split_axis=0, concat_axis=0, tiled=True)]
    unnamed x12 -> x10, local copies, waits for them, and re-layouts: 3.56 us -> 2.75 us
  transfers between devices with their start and end apart: 8 -> 7, of which waited for: 6 -> 3; matrix products, arithmetic and copies ran while one was open for 2% -> 2% of each run, Pallas kernels for 11% -> 12%
where the time goes in v3:
time: 127 us; the launch traced here: 126 us
  starting transfers between devices  39 us (31%)
  Pallas kernels  31 us (24%)
  waiting for transfers between devices  30.7 us (24%)
  blocking collectives  19.6 us (15%)
  local copies, waits for them, and re-layouts  4.65 us (4%)
  between operations  1.41 us (1%)
    all_to_all x2, waiting for transfers between devices, across(): return lax.all_to_all(pair, 'uly', split_axis=0, concat_axis=0, tiled=True)  22.5 us
    all_to_all x1, blocking collectives, across(): return lax.all_to_all(pair, 'uly', split_axis=0, concat_axis=0, tiled=True)  19.6 us
    all_to_all x1, starting transfers between devices, local(): lax.all_to_all(jnp.broadcast_to(sums[None], (group, 2, LANES)), ('dp', 'b...  15.8 us
    all_to_all x2, starting transfers between devices, across(): return lax.all_to_all(pair, 'uly', split_axis=0, concat_axis=0, tiled=True)  13.1 us
    pallas_call x1, Pallas kernels, run_halo(): pl.pallas_call(halo_both, in_specs=[SMEM, SMEM] + [VMEM] * 5, out_specs=[...  11.5 us
    ppermute x4, starting transfers between devices, swapped(): lax.ppermute(block, 'blk', pairs + [(high, low) for low, high in pairs])  10.1 us
    all_to_all x1, waiting for transfers between devices, local(): lax.all_to_all(jnp.broadcast_to(sums[None], (group, 2, LANES)), ('dp', 'b...  8.1 us
    pallas_call x1, Pallas kernels, run_centre_backward(): pl.pallas_call(centre_backward, in_specs=[SMEM, SMEM] + [VMEM] * 8, out_s...  6.13 us
  transfers between devices with their start and end apart: 7, of which 3 were waited for; matrix products, arithmetic and copies ran while one was open for 2% of the time, Pallas kernels for 12%

profile of v3, /device:TPU:1, one launch (start us, length us, event | category | flops | bytes accessed | tf_op | source)
XLA Modules:
  0.0 126.4 jit_solution(633740114239007880)
XLA Ops:
  0.6 0.0 copy-start.4
  0.6 0.0 copy-start.2
  0.7 1.9 %split_pair.2 = bf16[8,2,128,128]{3,2,1,0:T(8,128)(2,1)} custom-call(bf16[1,128,1024]{2,1,0:T(8,128)(2,1)} %first_ref.2, bf16[1,128,1024]{2,1,0:T(8,128)(2,1)} %second_ref.2), custom_call_target="tpu_custom_call" | custom-call | tf_op jit(solution)/shard_map/split_pair/pallas_call | solution.py:418
  2.6 19.6 %all_to_all.20.kv_ref = bf16[8,2,128,128]{3,2,1,0:T(8,128)(2,1)S(1)} all-to-all(bf16[8,2,128,128]{3,2,1,0:T(8,128)(2,1)} %split_pair.2), channel_id=1, replica_groups=mesh['dp'=4,'blk'=16,'uly'=8] {'uly'}, dimensions={0} | all-to-all | bytes 1048576 | tf_op jit(solution)/shard_map/all_to_all | solution.py:448
  22.2 0.7 collective-permute-start.1
  22.9 1.9 %collective-permute-start = (bf16[8,2,128,128]{3,2,1,0:T(8,128)(2,1)S(1)}, bf16[8,2,128,128]{3,2,1,0:T(8,128)(2,1)S(1)}, u32[]{:S(2)}, u32[]{:S(2)}) collective-permute-start(bf16[8,2,128,128]{3,2,1,0:T(8,128)(2,1)S(1)} %all_to_all.20.kv_ref), channel_id=1, source_target_pairs={{0,8},{16,24},{32,40},{48,56},{64,72},{80,88},{96,104},{112,120},{... | collective-permute-start | bytes 1572872 | tf_op jit(solution)/shard_map/ppermute | solution.py:453
  24.8 1.9 %split_pair.3 = bf16[8,2,128,128]{3,2,1,0:T(8,128)(2,1)} custom-call(bf16[1,128,1024]{2,1,0:T(8,128)(2,1)} %first_ref.3, bf16[1,128,1024]{2,1,0:T(8,128)(2,1)} %second_ref.3), custom_call_target="tpu_custom_call" | custom-call | tf_op jit(solution)/shard_map/split_pair/pallas_call | solution.py:418
  26.7 4.4 %all-to-all-start.1 = ((bf16[8,2,128,128]{3,2,1,0:T(8,128)(2,1)}), bf16[8,2,128,128]{3,2,1,0:T(8,128)(2,1)S(1)}, u32[]{:S(2)}, u32[]{:S(2)}) async-start(bf16[8,2,128,128]{3,2,1,0:T(8,128)(2,1)} %split_pair.3), calls=%async_computation.1 | async-start | bytes 1048576 | tf_op jit(solution)/shard_map/all_to_all | solution.py:448
  31.8 0.0 copy-done.4
  31.8 0.1 reshape.16.bias_ref
  31.9 0.1 pad_add_fusion.meta
  32.0 8.7 %all-to-all-done.1.qd_ref = bf16[8,2,128,128]{3,2,1,0:T(8,128)(2,1)S(1)} async-done(((bf16[8,2,128,128]{3,2,1,0:T(8,128)(2,1)}), bf16[8,2,128,128]{3,2,1,0:T(8,128)(2,1)S(1)}, u32[]{:S(2)}, u32[]{:S(2)}) %all-to-all-start.1) | async-done | bytes 524320 | tf_op jit(solution)/shard_map/all_to_all | solution.py:448
  40.7 0.0 copy-done.2
  40.7 4.1 %centre_forward.1 = (bf16[2,1024,1024]{2,1,0:T(8,128)(2,1)S(1)}, f32[2,1024,128]{2,1,0:T(8,128)S(1)}) custom-call(s32[2]{0:T(128)S(1)} %pad_add_fusion.meta, f32[2]{0:T(128)S(1)} %copy-done.2, bf16[8,2,128,128]{3,2,1,0:T(8,128)(2,1)S(1)} %all_to_all.20.kv_ref, bf16[8,2,128,128]{3,2,1,0:T(8,128)(2,1)S(1)} %all-to-all-done.1.qd_ref, f32[1,128]{1,0:T(1,128)S(1)} %reshape.16.bias_ref), custom_call_target="tpu_custom_call" | custom-call | flops 1000 | bytes 1000 | tf_op jit(solution)/shard_map/centre_forward/pallas_call | solution.py:349
  44.8 0.0 collective-permute-done.1.first_ref
  44.8 0.0 collective-permute-done.second_ref
  44.8 11.5 %halo_both.1 = (bf16[1024,128]{1,0:T(8,128)(2,1)S(1)}, f32[1024,128]{1,0:T(8,128)S(1)}, f32[1024,128]{1,0:T(8,128)S(1)}, bf16[8,2,128,128]{3,2,1,0:T(8,128)(2,1)...) custom-call(s32[2]{0:T(128)S(1)} %pad_add_fusion.meta, f32[2]{0:T(128)S(1)} %copy-done.2, ...), custom_call_target="tpu_custom_call" | custom-call | flops 4026531840 | bytes 8388608 | tf_op jit(solution)/shard_map/halo_both/pallas_call | solution.py:366
  56.4 1.5 %collective-permute-start.2 = (bf16[8,2,128,128]{3,2,1,0:T(8,128)(2,1)S(1)}, bf16[8,2,128,128]{3,2,1,0:T(8,128)(2,1)}, u32[]{:S(2)}, u32[]{:S(2)}) collective-permute-start(bf16[8,2,128,128]{3,2,1,0:T(8,128)(2,1)S(1)} %get-tuple-element.29), channel_id=1, source_target_pairs={{8,16},{24,32},{40,48},{56,64},{72,80},{88,96},{104,112},{16,8},{3... | collective-permute-start | bytes 1572872 | tf_op jit(solution)/shard_map/ppermute | solution.py:453
  57.8 6.0 %collective-permute-start.3 = (bf16[8,2,128,128]{3,2,1,0:T(8,128)(2,1)S(1)}, bf16[8,2,128,128]{3,2,1,0:T(8,128)(2,1)}, u32[]{:S(2)}, u32[]{:S(2)}) collective-permute-start(bf16[8,2,128,128]{3,2,1,0:T(8,128)(2,1)S(1)} %get-tuple-element.30), channel_id=1, source_target_pairs={{0,8},{16,24},{32,40},{48,56},{64,72},{80,88},{96,104},{112,120},{... | collective-permute-start | bytes 1572872 | tf_op jit(solution)/shard_map/ppermute | solution.py:453
  63.9 6.1 %centre_backward.1 = (bf16[8,2,128,128]{3,2,1,0:T(8,128)(2,1)S(1)}, f32[8,2,128,128]{3,2,1,0:T(8,128)S(1)}, f32[2,128]{1,0:T(2,128)S(1)}) custom-call(s32[2]{0:T(128)S(1)} %pad_add_fusion.meta, f32[2]{0:T(128)S(1)} %copy-done.2, bf16[8,2,128,128]{3,2,1,0:T(8,128)(2,1)S(1)} %all_to_all.20.kv_ref, bf16[8,2,128,128]{3,2,1,0:T(8,128)(2,1)S(1)} %all-to-all-done.1.qd_ref, ...), custom_call_target="tpu_custom_call" | custom-call | flops 1000 | bytes 1000 | tf_op jit(solution)/shard_map/centre_backward/pallas_call | solution.py:392
  70.0 0.0 copy-start
  70.0 1.0 copy-done
  71.0 0.0 copy-start.1
  71.0 0.8 copy-done.1
  71.8 0.6 broadcast_in_dim.2
  72.4 15.8 %all-to-all-start.3 = ((f32[64,2,128]{2,1,0:T(2,128)}), f32[64,2,128]{2,1,0:T(2,128)S(1)}, u32[]{:S(2)}, u32[]{:S(2)}) async-start(f32[64,2,128]{2,1,0:T(2,128)} %broadcast_in_dim.2), calls=%async_computation.3 | async-start | bytes 131072 | tf_op jit(solution)/shard_map/all_to_all | solution.py:474
  88.2 0.0 collective-permute-done.2.first_ref
  88.2 0.0 collective-permute-done.3.second_ref
  88.3 2.8 %gather_grads.1 = bf16[8,4,128,128]{3,2,1,0:T(8,128)(2,1)} custom-call(bf16[8,2,128,128]{3,2,1,0:T(8,128)(2,1)} %copy-done.1, f32[8,2,128,128]{3,2,1,0:T(8,128)} %copy-done, bf16[8,2,128,128]{3,2,1,0:T(8,128)(2,1)} %collective-permute-done.2.first_ref, bf16[8,2,128,128]{3,2,1,0:T(8,128)(2,1)} %collective-permute-done.3.second_ref), custom_call_target="tpu_custom_call" | custom-call | tf_op jit(solution)/shard_map/gather_grads/pallas_call | solution.py:430
  91.1 8.1 %all-to-all-done.3 = f32[64,2,128]{2,1,0:T(2,128)S(1)} async-done(((f32[64,2,128]{2,1,0:T(2,128)}), f32[64,2,128]{2,1,0:T(2,128)S(1)}, u32[]{:S(2)}, u32[]{:S(2)}) %all-to-all-start.3) | async-done | bytes 65568 | tf_op jit(solution)/shard_map/all_to_all | solution.py:474
  99.2 8.7 %all-to-all-start.2 = ((bf16[8,4,128,128]{3,2,1,0:T(8,128)(2,1)}), bf16[8,4,128,128]{3,2,1,0:T(8,128)(2,1)S(1)}, u32[]{:S(2)}, u32[]{:S(2)}) async-start(bf16[8,4,128,128]{3,2,1,0:T(8,128)(2,1)} %gather_grads.1), calls=%async_computation.2 | async-start | bytes 2097152 | tf_op jit(solution)/shard_map/all_to_all | solution.py:448
  107.9 0.1 reduce_sum.9
  108.0 0.6 reshape_squeeze.3
  108.6 0.5 slice_bitcast_fusion
  109.1 13.9 %all-to-all-done.2.parts_ref = bf16[8,4,128,128]{3,2,1,0:T(8,128)(2,1)S(1)} async-done(((bf16[8,4,128,128]{3,2,1,0:T(8,128)(2,1)}), bf16[8,4,128,128]{3,2,1,0:T(8,128)(2,1)S(1)}, u32[]{:S(2)}, u32[]{:S(2)}) %all-to-all-start.2) | async-done | bytes 1048608 | tf_op jit(solution)/shard_map/all_to_all | solution.py:448
  123.0 0.0 copy-start.3
  123.0 1.0 copy-done.3
  124.0 2.5 %join_four.1 = (bf16[1,128,1024]{2,1,0:T(8,128)(2,1)}, bf16[1,128,1024]{2,1,0:T(8,128)(2,1)}, bf16[1,128,1024]{2,1,0:T(8,128)(2,1)}, bf16[1,128,1024]{2,1,0:T(8,128)(2,1)}) custom-call(bf16[8,4,128,128]{3,2,1,0:T(8,128)(2,1)} %copy-done.3), custom_call_target="tpu_custom_call" | custom-call | tf_op jit(solution)/shard_map/join_four/pallas_call | solution.py:444
  (1 shorter events, 0.0 us)
Async XLA Ops:
  0.6 31.2 %copy-start.4 = (f32[2,64]{1,0:T(2,128)S(1)}, f32[2,64]{1,0:T(2,128)}, u32[]{:S(2)}) copy-start(f32[2,64]{1,0:T(2,128)} %param.11) | copy-start | bytes 1540
  0.6 40.0 %copy-start.2 = (f32[2]{0:T(128)S(1)}, f32[2]{0:T(128)}, u32[]{:S(2)}) copy-start(f32[2]{0:T(128)} %slopes_ref.5) | copy-start | bytes 28
  22.2 22.6 %collective-permute-start.1 = (bf16[8,2,128,128]{3,2,1,0:T(8,128)(2,1)S(1)}, bf16[8,2,128,128]{3,2,1,0:T(8,128)(2,1)S(1)}, u32[]{:S(2)}, u32[]{:S(2)}) collective-permute-start(bf16[8,2,128,128]{3,2,1,0:T(8,128)(2,1)S(1)} %all_to_all.20.kv_ref), channel_id=1, source_target_pairs={{8,16},{24,32},{40,48},{56,64},{72,80},{88,96},{104,112},{16,8},{3... | collective-permute-start | bytes 1572872 | tf_op jit(solution)/shard_map/ppermute | solution.py:453
  22.9 21.9 %collective-permute-start = (bf16[8,2,128,128]{3,2,1,0:T(8,128)(2,1)S(1)}, bf16[8,2,128,128]{3,2,1,0:T(8,128)(2,1)S(1)}, u32[]{:S(2)}, u32[]{:S(2)}) collective-permute-start(bf16[8,2,128,128]{3,2,1,0:T(8,128)(2,1)S(1)} %all_to_all.20.kv_ref), channel_id=1, source_target_pairs={{0,8},{16,24},{32,40},{48,56},{64,72},{80,88},{96,104},{112,120},{... | collective-permute-start | bytes 1572872 | tf_op jit(solution)/shard_map/ppermute | solution.py:453
  26.7 13.9 %all-to-all-start.1 = ((bf16[8,2,128,128]{3,2,1,0:T(8,128)(2,1)}), bf16[8,2,128,128]{3,2,1,0:T(8,128)(2,1)S(1)}, u32[]{:S(2)}, u32[]{:S(2)}) async-start(bf16[8,2,128,128]{3,2,1,0:T(8,128)(2,1)} %split_pair.3), calls=%async_computation.1 | async-start | bytes 1048576 | tf_op jit(solution)/shard_map/all_to_all | solution.py:448
  56.4 31.9 %collective-permute-start.2 = (bf16[8,2,128,128]{3,2,1,0:T(8,128)(2,1)S(1)}, bf16[8,2,128,128]{3,2,1,0:T(8,128)(2,1)}, u32[]{:S(2)}, u32[]{:S(2)}) collective-permute-start(bf16[8,2,128,128]{3,2,1,0:T(8,128)(2,1)S(1)} %get-tuple-element.29), channel_id=1, source_target_pairs={{8,16},{24,32},{40,48},{56,64},{72,80},{88,96},{104,112},{16,8},{3... | collective-permute-start | bytes 1572872 | tf_op jit(solution)/shard_map/ppermute | solution.py:453
  57.8 30.4 %collective-permute-start.3 = (bf16[8,2,128,128]{3,2,1,0:T(8,128)(2,1)S(1)}, bf16[8,2,128,128]{3,2,1,0:T(8,128)(2,1)}, u32[]{:S(2)}, u32[]{:S(2)}) collective-permute-start(bf16[8,2,128,128]{3,2,1,0:T(8,128)(2,1)S(1)} %get-tuple-element.30), channel_id=1, source_target_pairs={{0,8},{16,24},{32,40},{48,56},{64,72},{80,88},{96,104},{112,120},{... | collective-permute-start | bytes 1572872 | tf_op jit(solution)/shard_map/ppermute | solution.py:453
  70.0 1.0 copy-start
  71.0 0.8 copy-start.1
  72.4 26.7 %all-to-all-start.3 = ((f32[64,2,128]{2,1,0:T(2,128)}), f32[64,2,128]{2,1,0:T(2,128)S(1)}, u32[]{:S(2)}, u32[]{:S(2)}) async-start(f32[64,2,128]{2,1,0:T(2,128)} %broadcast_in_dim.2), calls=%async_computation.3 | async-start | bytes 131072 | tf_op jit(solution)/shard_map/all_to_all | solution.py:474
  99.2 23.8 %all-to-all-start.2 = ((bf16[8,4,128,128]{3,2,1,0:T(8,128)(2,1)}), bf16[8,4,128,128]{3,2,1,0:T(8,128)(2,1)S(1)}, u32[]{:S(2)}, u32[]{:S(2)}) async-start(bf16[8,4,128,128]{3,2,1,0:T(8,128)(2,1)} %gather_grads.1), calls=%async_computation.2 | async-start | bytes 2097152 | tf_op jit(solution)/shard_map/all_to_all | solution.py:448
  123.0 1.0 copy-start.3

commit v4 on v3

--- a/solution.py
+++ b/solution.py
@@ -311,14 +311,17 @@
 
     c_first = {}
     chains = staggered([grade, scale, spread, finish])
-    sums_ref[0:1] = sum(c["bias"] for c in chains if c["head"] == 1)
+    bias_sum = sum(c["bias"] for c in chains if c["head"] == 1)
     row = iota((1, LANES), 1)
     totals = []
     for head in range(2):
         total = sum(c["slope"] for c in chains if c["head"] == head)
         total = jnp.sum(total + halo_slope_ref[pl.ds(head * 8, 1)], axis=1, keepdims=True)
         totals.append(-total / (slopes_ref[head] * LOG2E))
-    sums_ref[1:2] = jnp.where(row == 0, totals[0], jnp.where(row == 1, totals[1], 0.0))
+    slope_sum = jnp.where(row == 0, totals[0], jnp.where(row == 1, totals[1], 0.0))
+    sums = jnp.concatenate([bias_sum, slope_sum], axis=0)
+    for block in range(sums_ref.shape[0]):
+        sums_ref[block] = sums
     for peer in range(PEERS):
         cols = pl.ds(peer * CHUNK, CHUNK)
         dkv_ref[peer, 0] = dkt[:, cols].T
@@ -332,6 +335,10 @@
 
 def params():
     return pltpu.CompilerParams(vmem_limit_bytes=VMEM_LIMIT)
+
+
+def small():
+    return pltpu.CompilerParams(vmem_limit_bytes=12 * 1024 * 1024)
 
 
 def cost(keys, products):
@@ -393,7 +400,11 @@
         centre_backward,
         in_specs=[SMEM, SMEM] + [VMEM] * 8,
         out_specs=[VMEM] * 3,
-        out_shape=[shaped(PAIR, BF16), shaped(PAIR, F32), shaped((2, LANES), F32)],
+        out_shape=[
+            shaped(PAIR, BF16),
+            shaped(PAIR, F32),
+            shaped((lax.axis_size("blk"), 2, LANES), F32),
+        ],
         scratch_shapes=[
             pltpu.VMEM((2, BLOCK, LANES), BF16),
             pltpu.VMEM((2, BLOCK, LANES), BF16),
@@ -415,7 +426,7 @@
 
 
 def run_split(first, second):
-    return pl.pallas_call(split_pair, out_shape=shaped(PAIR, BF16), name="split_pair")(first, second)
+    return pl.pallas_call(split_pair, out_shape=shaped(PAIR, BF16), compiler_params=small(), name="split_pair")(first, second)
 
 
 def gather_grads(cq_ref, dkv_ref, first_ref, second_ref, out_ref):
@@ -428,7 +439,10 @@
 
 def run_gather(cq, dkv, from_first, from_second):
     return pl.pallas_call(
-        gather_grads, out_shape=shaped((PEERS, 4, CHUNK, LANES), BF16), name="gather_grads"
+        gather_grads,
+        out_shape=shaped((PEERS, 4, CHUNK, LANES), BF16),
+        compiler_params=small(),
+        name="gather_grads",
     )(cq, dkv, from_first, from_second)
 
 
@@ -441,11 +455,17 @@
 
 def run_join(parts):
     whole_rows = shaped((1, CHUNK, PEERS * LANES), BF16)
-    return pl.pallas_call(join_four, out_shape=[whole_rows] * 4, name="join_four")(parts)
+    return pl.pallas_call(join_four, out_shape=[whole_rows] * 4, compiler_params=small(), name="join_four")(parts)
 
 
 def across(pair):
     return lax.all_to_all(pair, "uly", split_axis=0, concat_axis=0, tiled=True)
+
+
+def over_recordings(partial):
+    around = [(i, i ^ 1) for i in range(4)], [(i, i ^ 2) for i in range(4)], [(i, i ^ 3) for i in range(4)]
+    one, two, three = (lax.ppermute(partial, "dp", route) for route in around)
+    return (partial + one) + (two + three)
 
 
 def swapped(block, lowest):
@@ -470,13 +490,11 @@
     cq, dkv, sums = run_centre_backward(
         meta, slopes, kv, qd, bias, powers, stats, context, dq, halo_slope
     )
-    group = lax.axis_size("dp") * lax.axis_size("blk")
-    spread = lax.all_to_all(
-        jnp.broadcast_to(sums[None], (group, 2, LANES)), ("dp", "blk"), 0, 0, tiled=True
-    )
+    spread = lax.all_to_all(sums, "blk", split_axis=0, concat_axis=0, tiled=True)
+    partial = jnp.sum(spread, axis=0)
     grads = run_gather(cq, dkv, from_first, from_second)
     context_out, query_out, key_out, value_out = run_join(across(grads))
-    total = jnp.sum(spread, axis=0)
+    total = over_recordings(partial)
     return (
         context_out,
         query_out,

time: 127 us -> 122 us (0.961)
  waiting for transfers between devices: 30.7 us -> 22.3 us
  starting transfers between devices: 39 us -> 45.1 us
  Pallas kernels: 31 us -> 26.5 us
  local copies, waits for them, and re-layouts: 4.65 us -> 6.91 us
    all_to_all x2, waiting for transfers between devices: 22.5 us -> 11.6 us  [across(): return lax.all_to_all(pair, 'uly', split_axis=0, concat_axis=0, tiled=True)]
    ppermute x0 -> x3, starting transfers between devices: none -> 9.29 us  [over_recordings(): one, two, three = (lax.ppermute(partial, 'dp', route) for route in around)]
    pallas_call x3, Pallas kernels: 6.33 us -> 2.23 us  [the longest x1 1.25 us: run_join(): pl.pallas_call(join_four, out_shape=[whole_rows] * 4, compiler_params=sma...]
    all_to_all x1, starting transfers between devices: 15.8 us -> 12.2 us  [local(): lax.all_to_all(sums, 'blk', split_axis=0, concat_axis=0, tiled=True)]
    unnamed x10 -> x16, local copies, waits for them, and re-layouts: 2.75 us -> 5.64 us
    pallas_call x1, Pallas kernels: 2.83 us -> 1.13 us  [run_gather(): pl.pallas_call(gather_grads, out_shape=shaped((PEERS, 4, CHUNK, LANES), B...]
    ppermute x0 -> x3, waiting for transfers between devices: none -> 1.69 us  [over_recordings(): one, two, three = (lax.ppermute(partial, 'dp', route) for route in around)]
  transfers between devices with their start and end apart: 7 -> 10, of which waited for: 3 -> 4; matrix products, arithmetic and copies ran while one was open for 2% -> 1% of each run, Pallas kernels for 12% -> 11%
where the time goes in v4:
time: 122 us; the launch traced here: 121 us
  starting transfers between devices  45.1 us (37%)
  Pallas kernels  26.5 us (22%)
  waiting for transfers between devices  22.3 us (18%)
  blocking collectives  18.6 us (15%)
  local copies, waits for them, and re-layouts  6.91 us (6%)
  between operations  1.45 us (1%)
    all_to_all x1, blocking collectives, across(): return lax.all_to_all(pair, 'uly', split_axis=0, concat_axis=0, tiled=True)  18.6 us
    all_to_all x2, starting transfers between devices, across(): return lax.all_to_all(pair, 'uly', split_axis=0, concat_axis=0, tiled=True)  13.3 us
    pallas_call x1, Pallas kernels, run_halo(): pl.pallas_call(halo_both, in_specs=[SMEM, SMEM] + [VMEM] * 5, out_specs=[...  12.4 us
    all_to_all x1, starting transfers between devices, local(): lax.all_to_all(sums, 'blk', split_axis=0, concat_axis=0, tiled=True)  12.2 us
    all_to_all x2, waiting for transfers between devices, across(): return lax.all_to_all(pair, 'uly', split_axis=0, concat_axis=0, tiled=True)  11.6 us
    ppermute x4, starting transfers between devices, swapped(): lax.ppermute(block, 'blk', pairs + [(high, low) for low, high in pairs])  10.3 us
    ppermute x3, starting transfers between devices, over_recordings(): one, two, three = (lax.ppermute(partial, 'dp', route) for route in around)  9.29 us
    all_to_all x1, waiting for transfers between devices, local(): lax.all_to_all(sums, 'blk', split_axis=0, concat_axis=0, tiled=True)  9.05 us
  transfers between devices with their start and end apart: 10, of which 4 were waited for; matrix products, arithmetic and copies ran while one was open for 1% of the time, Pallas kernels for 11%

profile of v4, /device:TPU:1, one launch (start us, length us, event | category | flops | bytes accessed | tf_op | source)
XLA Modules:
  0.0 121.0 jit_solution(7094758259405207703)
XLA Ops:
  0.6 0.0 copy-start.2
  0.6 0.9 copy-done.2
  1.6 0.0 copy-start.3
  1.6 0.9 copy-done.3
  2.5 0.0 copy-start.7
  2.5 0.0 copy-start.6
  2.5 0.1 split_pair.2
  2.6 18.6 %all_to_all.20.kv_ref = bf16[8,2,128,128]{3,2,1,0:T(8,128)(2,1)S(1)} all-to-all(bf16[8,2,128,128]{3,2,1,0:T(8,128)(2,1)S(1)} %split_pair.2), channel_id=1, replica_groups=mesh['dp'=4,'blk'=16,'uly'=8] {'uly'}, dimensions={0} | all-to-all | bytes 1048576 | tf_op jit(solution)/shard_map/all_to_all | solution.py:462
  21.3 0.7 collective-permute-start.1
  22.0 2.0 %collective-permute-start = (bf16[8,2,128,128]{3,2,1,0:T(8,128)(2,1)S(1)}, bf16[8,2,128,128]{3,2,1,0:T(8,128)(2,1)S(1)}, u32[]{:S(2)}, u32[]{:S(2)}) collective-permute-start(bf16[8,2,128,128]{3,2,1,0:T(8,128)(2,1)S(1)} %all_to_all.20.kv_ref), channel_id=1, source_target_pairs={{0,8},{16,24},{32,40},{48,56},{64,72},{80,88},{96,104},{112,120},{... | collective-permute-start | bytes 1572872 | tf_op jit(solution)/shard_map/ppermute | solution.py:473
  24.0 0.0 copy-start.4
  24.0 0.9 copy-done.4
  25.0 0.0 copy-start.5
  25.0 0.9 copy-done.5
  25.9 0.9 split_pair.3
  26.8 5.0 %all-to-all-start.1 = ((bf16[8,2,128,128]{3,2,1,0:T(8,128)(2,1)}), bf16[8,2,128,128]{3,2,1,0:T(8,128)(2,1)S(1)}, u32[]{:S(2)}, u32[]{:S(2)}) async-start(bf16[8,2,128,128]{3,2,1,0:T(8,128)(2,1)} %split_pair.3), calls=%async_computation.1 | async-start | bytes 1048576 | tf_op jit(solution)/shard_map/all_to_all | solution.py:462
  32.5 0.0 copy-done.7
  32.5 0.1 reshape.15.bias_ref
  32.5 0.1 pad_add_fusion.meta
  32.6 8.7 %all-to-all-done.1.qd_ref = bf16[8,2,128,128]{3,2,1,0:T(8,128)(2,1)S(1)} async-done(((bf16[8,2,128,128]{3,2,1,0:T(8,128)(2,1)}), bf16[8,2,128,128]{3,2,1,0:T(8,128)(2,1)S(1)}, u32[]{:S(2)}, u32[]{:S(2)}) %all-to-all-start.1) | async-done | bytes 524320 | tf_op jit(solution)/shard_map/all_to_all | solution.py:462
  41.3 0.0 copy-done.6
  41.3 4.1 %centre_forward.1 = (bf16[2,1024,1024]{2,1,0:T(8,128)(2,1)S(1)}, f32[2,1024,128]{2,1,0:T(8,128)S(1)}) custom-call(s32[2]{0:T(128)S(1)} %pad_add_fusion.meta, f32[2]{0:T(128)S(1)} %copy-done.6, bf16[8,2,128,128]{3,2,1,0:T(8,128)(2,1)S(1)} %all_to_all.20.kv_ref, bf16[8,2,128,128]{3,2,1,0:T(8,128)(2,1)S(1)} %all-to-all-done.1.qd_ref, f32[1,128]{1,0:T(1,128)S(1)} %reshape.15.bias_ref), custom_call_target="tpu_custom_call" | custom-call | flops 1000 | bytes 1000 | tf_op jit(solution)/shard_map/centre_forward/pallas_call | solution.py:356
  45.4 0.0 collective-permute-done.1.first_ref
  45.4 0.0 collective-permute-done.second_ref
  45.4 12.4 %halo_both.1 = (bf16[1024,128]{1,0:T(8,128)(2,1)S(1)}, f32[1024,128]{1,0:T(8,128)S(1)}, f32[1024,128]{1,0:T(8,128)S(1)}, bf16[8,2,128,128]{3,2,1,0:T(8,128)(2,1)...) custom-call(s32[2]{0:T(128)S(1)} %pad_add_fusion.meta, f32[2]{0:T(128)S(1)} %copy-done.6, ...), custom_call_target="tpu_custom_call" | custom-call | flops 4026531840 | bytes 8388608 | tf_op jit(solution)/shard_map/halo_both/pallas_call | solution.py:373
  57.8 0.7 collective-permute-start.2
  58.5 6.9 %collective-permute-start.3 = (bf16[8,2,128,128]{3,2,1,0:T(8,128)(2,1)}, bf16[8,2,128,128]{3,2,1,0:T(8,128)(2,1)S(1)}, u32[]{:S(2)}, u32[]{:S(2)}) collective-permute-start(bf16[8,2,128,128]{3,2,1,0:T(8,128)(2,1)} %get-tuple-element.30), channel_id=1, source_target_pairs={{0,8},{16,24},{32,40},{48,56},{64,72},{80,88},{96,104},{112,120},{... | collective-permute-start | bytes 1572872 | tf_op jit(solution)/shard_map/ppermute | solution.py:473
  65.4 6.7 %centre_backward.1 = (bf16[8,2,128,128]{3,2,1,0:T(8,128)(2,1)S(1)}, f32[8,2,128,128]{3,2,1,0:T(8,128)S(1)}, f32[16,2,128]{2,1,0:T(2,128)}) custom-call(s32[2]{0:T(128)S(1)} %pad_add_fusion.meta, f32[2]{0:T(128)S(1)} %copy-done.6, bf16[8,2,128,128]{3,2,1,0:T(8,128)(2,1)S(1)} %all_to_all.20.kv_ref, bf16[8,2,128,128]{3,2,1,0:T(8,128)(2,1)S(1)} %all-to-all-done.1.qd_ref, ...), custom_call_target="tpu_custom_call" | custom-call | flops 1000 | bytes 1000 | tf_op jit(solution)/shard_map/centre_backward/pallas_call | solution.py:399
  72.1 0.0 copy-start
  72.1 0.8 copy-done
  72.9 12.2 %all-to-all-start.3 = ((f32[16,2,128]{2,1,0:T(2,128)}), f32[16,2,128]{2,1,0:T(2,128)S(1)}, u32[]{:S(2)}, u32[]{:S(2)}) async-start(f32[16,2,128]{2,1,0:T(2,128)} %get-tuple-element.35), calls=%async_computation.3 | async-start | bytes 32768 | tf_op jit(solution)/shard_map/all_to_all | solution.py:493
  85.1 0.0 collective-permute-done.2.first_ref
  85.1 0.0 collective-permute-done.3.second_ref
  85.1 0.0 copy-start.1
  85.2 1.0 copy-done.1
  86.2 1.1 gather_grads.1
  87.3 9.1 %all-to-all-done.3 = f32[16,2,128]{2,1,0:T(2,128)S(1)} async-done(((f32[16,2,128]{2,1,0:T(2,128)}), f32[16,2,128]{2,1,0:T(2,128)S(1)}, u32[]{:S(2)}, u32[]{:S(2)}) %all-to-all-start.3) | async-done | bytes 16416 | tf_op jit(solution)/shard_map/all_to_all | solution.py:493
  96.4 8.3 %all-to-all-start.2 = ((bf16[8,4,128,128]{3,2,1,0:T(8,128)(2,1)}), bf16[8,4,128,128]{3,2,1,0:T(8,128)(2,1)S(1)}, u32[]{:S(2)}, u32[]{:S(2)}) async-start(bf16[8,4,128,128]{3,2,1,0:T(8,128)(2,1)} %gather_grads.1), calls=%async_computation.2 | async-start | bytes 2097152 | tf_op jit(solution)/shard_map/all_to_all | solution.py:462
  104.7 3.6 %collective-permute-start.6 = (f32[2,128]{1,0:T(2,128)S(1)}, f32[2,128]{1,0:T(2,128)S(1)}, u32[]{:S(2)}, u32[]{:S(2)}) collective-permute-start(f32[2,128]{1,0:T(2,128)S(1)} %reduce_sum.9), channel_id=1, source_target_pairs={{0,384},{128,256},{256,128},{384,0},{1,385},{129,257},{257,129},{3... | collective-permute-start | bytes 3080 | tf_op jit(solution)/shard_map/ppermute | solution.py:467
  108.3 2.8 %collective-permute-start.5 = (f32[2,128]{1,0:T(2,128)S(1)}, f32[2,128]{1,0:T(2,128)S(1)}, u32[]{:S(2)}, u32[]{:S(2)}) collective-permute-start(f32[2,128]{1,0:T(2,128)S(1)} %reduce_sum.9), channel_id=1, source_target_pairs={{0,256},{128,384},{256,0},{384,128},{1,257},{129,385},{257,1},{385... | collective-permute-start | bytes 3080 | tf_op jit(solution)/shard_map/ppermute | solution.py:467
  111.1 2.9 %collective-permute-start.4 = (f32[2,128]{1,0:T(2,128)S(1)}, f32[2,128]{1,0:T(2,128)S(1)}, u32[]{:S(2)}, u32[]{:S(2)}) collective-permute-start(f32[2,128]{1,0:T(2,128)S(1)} %reduce_sum.9), channel_id=1, source_target_pairs={{0,128},{128,0},{256,384},{384,256},{1,129},{129,1},{257,385},{385... | collective-permute-start | bytes 3080 | tf_op jit(solution)/shard_map/ppermute | solution.py:467
  114.0 0.0 collective-permute-done.6
  114.0 0.0 collective-permute-done.5
  114.0 1.7 %collective-permute-done.4 = f32[2,128]{1,0:T(2,128)S(1)} collective-permute-done((f32[2,128]{1,0:T(2,128)S(1)}, f32[2,128]{1,0:T(2,128)S(1)}, u32[]{:S(2)}, u32[]{:S(2)}) %collective-permute-start.4) | collective-permute-done | bytes 1056 | tf_op jit(solution)/shard_map/ppermute | solution.py:467
  115.8 0.6 reshape_squeeze.3
  116.4 0.5 slice_bitcast_fusion
  116.9 2.9 %all-to-all-done.2.parts_ref = bf16[8,4,128,128]{3,2,1,0:T(8,128)(2,1)S(1)} async-done(((bf16[8,4,128,128]{3,2,1,0:T(8,128)(2,1)}), bf16[8,4,128,128]{3,2,1,0:T(8,128)(2,1)S(1)}, u32[]{:S(2)}, u32[]{:S(2)}) %all-to-all-start.2) | async-done | bytes 1048608 | tf_op jit(solution)/shard_map/all_to_all | solution.py:462
  119.8 1.2 %join_four.1 = (bf16[1,128,1024]{2,1,0:T(8,128)(2,1)}, bf16[1,128,1024]{2,1,0:T(8,128)(2,1)}, bf16[1,128,1024]{2,1,0:T(8,128)(2,1)}, bf16[1,128,1024]{2,1,0:T(8,128)(2,1)}) custom-call(bf16[8,4,128,128]{3,2,1,0:T(8,128)(2,1)S(1)} %all-to-all-done.2.parts_ref), custom_call_target="tpu_custom_call" | custom-call | tf_op jit(solution)/shard_map/join_four/pallas_call | solution.py:458
  (3 shorter events, 0.1 us)
Async XLA Ops:
  0.6 1.0 copy-start.2
  1.6 0.9 copy-start.3
  2.5 29.9 %copy-start.7 = (f32[2,64]{1,0:T(2,128)S(1)}, f32[2,64]{1,0:T(2,128)}, u32[]{:S(2)}) copy-start(f32[2,64]{1,0:T(2,128)} %param.11) | copy-start | bytes 1540
  2.5 38.8 %copy-start.6 = (f32[2]{0:T(128)S(1)}, f32[2]{0:T(128)}, u32[]{:S(2)}) copy-start(f32[2]{0:T(128)} %slopes_ref.5) | copy-start | bytes 28
  21.3 24.1 %collective-permute-start.1 = (bf16[8,2,128,128]{3,2,1,0:T(8,128)(2,1)S(1)}, bf16[8,2,128,128]{3,2,1,0:T(8,128)(2,1)S(1)}, u32[]{:S(2)}, u32[]{:S(2)}) collective-permute-start(bf16[8,2,128,128]{3,2,1,0:T(8,128)(2,1)S(1)} %all_to_all.20.kv_ref), channel_id=1, source_target_pairs={{8,16},{24,32},{40,48},{56,64},{72,80},{88,96},{104,112},{16,8},{3... | collective-permute-start | bytes 1572872 | tf_op jit(solution)/shard_map/ppermute | solution.py:473
  22.0 23.5 %collective-permute-start = (bf16[8,2,128,128]{3,2,1,0:T(8,128)(2,1)S(1)}, bf16[8,2,128,128]{3,2,1,0:T(8,128)(2,1)S(1)}, u32[]{:S(2)}, u32[]{:S(2)}) collective-permute-start(bf16[8,2,128,128]{3,2,1,0:T(8,128)(2,1)S(1)} %all_to_all.20.kv_ref), channel_id=1, source_target_pairs={{0,8},{16,24},{32,40},{48,56},{64,72},{80,88},{96,104},{112,120},{... | collective-permute-start | bytes 1572872 | tf_op jit(solution)/shard_map/ppermute | solution.py:473
  24.0 1.0 copy-start.4
  25.0 0.9 copy-start.5
  26.8 14.5 %all-to-all-start.1 = ((bf16[8,2,128,128]{3,2,1,0:T(8,128)(2,1)}), bf16[8,2,128,128]{3,2,1,0:T(8,128)(2,1)S(1)}, u32[]{:S(2)}, u32[]{:S(2)}) async-start(bf16[8,2,128,128]{3,2,1,0:T(8,128)(2,1)} %split_pair.3), calls=%async_computation.1 | async-start | bytes 1048576 | tf_op jit(solution)/shard_map/all_to_all | solution.py:462
  57.8 27.3 %collective-permute-start.2 = (bf16[8,2,128,128]{3,2,1,0:T(8,128)(2,1)}, bf16[8,2,128,128]{3,2,1,0:T(8,128)(2,1)S(1)}, u32[]{:S(2)}, u32[]{:S(2)}) collective-permute-start(bf16[8,2,128,128]{3,2,1,0:T(8,128)(2,1)} %get-tuple-element.29), channel_id=1, source_target_pairs={{8,16},{24,32},{40,48},{56,64},{72,80},{88,96},{104,112},{16,8},{3... | collective-permute-start | bytes 1572872 | tf_op jit(solution)/shard_map/ppermute | solution.py:473
  58.5 26.6 %collective-permute-start.3 = (bf16[8,2,128,128]{3,2,1,0:T(8,128)(2,1)}, bf16[8,2,128,128]{3,2,1,0:T(8,128)(2,1)S(1)}, u32[]{:S(2)}, u32[]{:S(2)}) collective-permute-start(bf16[8,2,128,128]{3,2,1,0:T(8,128)(2,1)} %get-tuple-element.30), channel_id=1, source_target_pairs={{0,8},{16,24},{32,40},{48,56},{64,72},{80,88},{96,104},{112,120},{... | collective-permute-start | bytes 1572872 | tf_op jit(solution)/shard_map/ppermute | solution.py:473
  72.1 0.8 copy-start
  72.9 23.4 %all-to-all-start.3 = ((f32[16,2,128]{2,1,0:T(2,128)}), f32[16,2,128]{2,1,0:T(2,128)S(1)}, u32[]{:S(2)}, u32[]{:S(2)}) async-start(f32[16,2,128]{2,1,0:T(2,128)} %get-tuple-element.35), calls=%async_computation.3 | async-start | bytes 32768 | tf_op jit(solution)/shard_map/all_to_all | solution.py:493
  85.1 1.0 copy-start.1
  96.4 23.4 %all-to-all-start.2 = ((bf16[8,4,128,128]{3,2,1,0:T(8,128)(2,1)}), bf16[8,4,128,128]{3,2,1,0:T(8,128)(2,1)S(1)}, u32[]{:S(2)}, u32[]{:S(2)}) async-start(bf16[8,4,128,128]{3,2,1,0:T(8,128)(2,1)} %gather_grads.1), calls=%async_computation.2 | async-start | bytes 2097152 | tf_op jit(solution)/shard_map/all_to_all | solution.py:462
  104.7 9.3 %collective-permute-start.6 = (f32[2,128]{1,0:T(2,128)S(1)}, f32[2,128]{1,0:T(2,128)S(1)}, u32[]{:S(2)}, u32[]{:S(2)}) collective-permute-start(f32[2,128]{1,0:T(2,128)S(1)} %reduce_sum.9), channel_id=1, source_target_pairs={{0,384},{128,256},{256,128},{384,0},{1,385},{129,257},{257,129},{3... | collective-permute-start | bytes 3080 | tf_op jit(solution)/shard_map/ppermute | solution.py:467
  108.3 5.7 %collective-permute-start.5 = (f32[2,128]{1,0:T(2,128)S(1)}, f32[2,128]{1,0:T(2,128)S(1)}, u32[]{:S(2)}, u32[]{:S(2)}) collective-permute-start(f32[2,128]{1,0:T(2,128)S(1)} %reduce_sum.9), channel_id=1, source_target_pairs={{0,256},{128,384},{256,0},{384,128},{1,257},{129,385},{257,1},{385... | collective-permute-start | bytes 3080 | tf_op jit(solution)/shard_map/ppermute | solution.py:467
  111.1 4.6 %collective-permute-start.4 = (f32[2,128]{1,0:T(2,128)S(1)}, f32[2,128]{1,0:T(2,128)S(1)}, u32[]{:S(2)}, u32[]{:S(2)}) collective-permute-start(f32[2,128]{1,0:T(2,128)S(1)} %reduce_sum.9), channel_id=1, source_target_pairs={{0,128},{128,0},{256,384},{384,256},{1,129},{129,1},{257,385},{385... | collective-permute-start | bytes 3080 | tf_op jit(solution)/shard_map/ppermute | solution.py:467

commit v5 on v4

--- a/solution.py
+++ b/solution.py
@@ -426,7 +426,7 @@
 
 
 def run_split(first, second):
-    return pl.pallas_call(split_pair, out_shape=shaped(PAIR, BF16), compiler_params=small(), name="split_pair")(first, second)
+    return pl.pallas_call(split_pair, out_shape=shaped(PAIR, BF16), name="split_pair")(first, second)
 
 
 def gather_grads(cq_ref, dkv_ref, first_ref, second_ref, out_ref):

time: 122 us -> 122 us (level)
  local copies, waits for them, and re-layouts: 6.91 us -> 3.13 us
  Pallas kernels: 26.5 us -> 29.3 us
    unnamed x16 -> x8, local copies, waits for them, and re-layouts: 5.64 us -> 1.87 us
    pallas_call x2, Pallas kernels: 0.99 us -> 3.84 us  [run_split(): pl.pallas_call(split_pair, out_shape=shaped(PAIR, BF16), name='split_pair')]
where the time goes in v5:
time: 122 us; the launch traced here: 121 us
  starting transfers between devices  45.2 us (37%)
  Pallas kernels  29.3 us (24%)
  waiting for transfers between devices  22.3 us (18%)
  blocking collectives  19.6 us (16%)
  local copies, waits for them, and re-layouts  3.13 us (3%)
  between operations  1.45 us (1%)
    all_to_all x1, blocking collectives, across(): return lax.all_to_all(pair, 'uly', split_axis=0, concat_axis=0, tiled=True)  19.6 us
    all_to_all x2, starting transfers between devices, across(): return lax.all_to_all(pair, 'uly', split_axis=0, concat_axis=0, tiled=True)  13.6 us
    pallas_call x1, Pallas kernels, run_halo(): pl.pallas_call(halo_both, in_specs=[SMEM, SMEM] + [VMEM] * 5, out_specs=[...  12.5 us
    all_to_all x1, starting transfers between devices, local(): lax.all_to_all(sums, 'blk', split_axis=0, concat_axis=0, tiled=True)  12.2 us
    all_to_all x2, waiting for transfers between devices, across(): return lax.all_to_all(pair, 'uly', split_axis=0, concat_axis=0, tiled=True)  11.6 us
    ppermute x4, starting transfers between devices, swapped(): lax.ppermute(block, 'blk', pairs + [(high, low) for low, high in pairs])  10.1 us
    ppermute x3, starting transfers between devices, over_recordings(): one, two, three = (lax.ppermute(partial, 'dp', route) for route in around)  9.29 us
    all_to_all x1, waiting for transfers between devices, local(): lax.all_to_all(sums, 'blk', split_axis=0, concat_axis=0, tiled=True)  9 us
  transfers between devices with their start and end apart: 10, of which 4 were waited for; matrix products, arithmetic and copies ran while one was open for 1% of the time, Pallas kernels for 11%

profile of v5, /device:TPU:1, one launch (start us, length us, event | category | flops | bytes accessed | tf_op | source)
XLA Modules:
  0.0 121.0 jit_solution(16972812919787603532)
XLA Ops:
  0.6 0.0 copy-start.3
  0.6 0.0 copy-start.2
  0.7 1.9 %split_pair.2 = bf16[8,2,128,128]{3,2,1,0:T(8,128)(2,1)} custom-call(bf16[1,128,1024]{2,1,0:T(8,128)(2,1)} %first_ref.2, bf16[1,128,1024]{2,1,0:T(8,128)(2,1)} %second_ref.2), custom_call_target="tpu_custom_call" | custom-call | tf_op jit(solution)/shard_map/split_pair/pallas_call | solution.py:429
  2.6 19.6 %all_to_all.20.kv_ref = bf16[8,2,128,128]{3,2,1,0:T(8,128)(2,1)S(1)} all-to-all(bf16[8,2,128,128]{3,2,1,0:T(8,128)(2,1)} %split_pair.2), channel_id=1, replica_groups=mesh['dp'=4,'blk'=16,'uly'=8] {'uly'}, dimensions={0} | all-to-all | bytes 1048576 | tf_op jit(solution)/shard_map/all_to_all | solution.py:462
  22.2 0.7 collective-permute-start.1
  22.9 1.9 %collective-permute-start = (bf16[8,2,128,128]{3,2,1,0:T(8,128)(2,1)S(1)}, bf16[8,2,128,128]{3,2,1,0:T(8,128)(2,1)S(1)}, u32[]{:S(2)}, u32[]{:S(2)}) collective-permute-start(bf16[8,2,128,128]{3,2,1,0:T(8,128)(2,1)S(1)} %all_to_all.20.kv_ref), channel_id=1, source_target_pairs={{0,8},{16,24},{32,40},{48,56},{64,72},{80,88},{96,104},{112,120},{... | collective-permute-start | bytes 1572872 | tf_op jit(solution)/shard_map/ppermute | solution.py:473
  24.8 1.9 %split_pair.3 = bf16[8,2,128,128]{3,2,1,0:T(8,128)(2,1)} custom-call(bf16[1,128,1024]{2,1,0:T(8,128)(2,1)} %first_ref.3, bf16[1,128,1024]{2,1,0:T(8,128)(2,1)} %second_ref.3), custom_call_target="tpu_custom_call" | custom-call | tf_op jit(solution)/shard_map/split_pair/pallas_call | solution.py:429
  26.7 4.4 %all-to-all-start.1 = ((bf16[8,2,128,128]{3,2,1,0:T(8,128)(2,1)}), bf16[8,2,128,128]{3,2,1,0:T(8,128)(2,1)S(1)}, u32[]{:S(2)}, u32[]{:S(2)}) async-start(bf16[8,2,128,128]{3,2,1,0:T(8,128)(2,1)} %split_pair.3), calls=%async_computation.1 | async-start | bytes 1048576 | tf_op jit(solution)/shard_map/all_to_all | solution.py:462
  31.8 0.0 copy-done.3
  31.8 0.1 reshape.15.bias_ref
  31.9 0.1 pad_add_fusion.meta
  32.0 8.7 %all-to-all-done.1.qd_ref = bf16[8,2,128,128]{3,2,1,0:T(8,128)(2,1)S(1)} async-done(((bf16[8,2,128,128]{3,2,1,0:T(8,128)(2,1)}), bf16[8,2,128,128]{3,2,1,0:T(8,128)(2,1)S(1)}, u32[]{:S(2)}, u32[]{:S(2)}) %all-to-all-start.1) | async-done | bytes 524320 | tf_op jit(solution)/shard_map/all_to_all | solution.py:462
  40.7 0.0 copy-done.2
  40.7 4.1 %centre_forward.1 = (bf16[2,1024,1024]{2,1,0:T(8,128)(2,1)S(1)}, f32[2,1024,128]{2,1,0:T(8,128)S(1)}) custom-call(s32[2]{0:T(128)S(1)} %pad_add_fusion.meta, f32[2]{0:T(128)S(1)} %copy-done.2, bf16[8,2,128,128]{3,2,1,0:T(8,128)(2,1)S(1)} %all_to_all.20.kv_ref, bf16[8,2,128,128]{3,2,1,0:T(8,128)(2,1)S(1)} %all-to-all-done.1.qd_ref, f32[1,128]{1,0:T(1,128)S(1)} %reshape.15.bias_ref), custom_call_target="tpu_custom_call" | custom-call | flops 1000 | bytes 1000 | tf_op jit(solution)/shard_map/centre_forward/pallas_call | solution.py:356
  44.8 0.0 collective-permute-done.1.first_ref
  44.8 0.0 collective-permute-done.second_ref
  44.8 12.5 %halo_both.1 = (bf16[1024,128]{1,0:T(8,128)(2,1)S(1)}, f32[1024,128]{1,0:T(8,128)S(1)}, f32[1024,128]{1,0:T(8,128)S(1)}, bf16[8,2,128,128]{3,2,1,0:T(8,128)(2,1)...) custom-call(s32[2]{0:T(128)S(1)} %pad_add_fusion.meta, f32[2]{0:T(128)S(1)} %copy-done.2, ...), custom_call_target="tpu_custom_call" | custom-call | flops 4026531840 | bytes 8388608 | tf_op jit(solution)/shard_map/halo_both/pallas_call | solution.py:373
  57.3 0.7 collective-permute-start.2
  58.0 6.8 %collective-permute-start.3 = (bf16[8,2,128,128]{3,2,1,0:T(8,128)(2,1)}, bf16[8,2,128,128]{3,2,1,0:T(8,128)(2,1)S(1)}, u32[]{:S(2)}, u32[]{:S(2)}) collective-permute-start(bf16[8,2,128,128]{3,2,1,0:T(8,128)(2,1)} %get-tuple-element.30), channel_id=1, source_target_pairs={{0,8},{16,24},{32,40},{48,56},{64,72},{80,88},{96,104},{112,120},{... | collective-permute-start | bytes 1572872 | tf_op jit(solution)/shard_map/ppermute | solution.py:473
  64.8 6.4 %centre_backward.1 = (bf16[8,2,128,128]{3,2,1,0:T(8,128)(2,1)S(1)}, f32[8,2,128,128]{3,2,1,0:T(8,128)S(1)}, f32[16,2,128]{2,1,0:T(2,128)}) custom-call(s32[2]{0:T(128)S(1)} %pad_add_fusion.meta, f32[2]{0:T(128)S(1)} %copy-done.2, bf16[8,2,128,128]{3,2,1,0:T(8,128)(2,1)S(1)} %all_to_all.20.kv_ref, bf16[8,2,128,128]{3,2,1,0:T(8,128)(2,1)S(1)} %all-to-all-done.1.qd_ref, ...), custom_call_target="tpu_custom_call" | custom-call | flops 1000 | bytes 1000 | tf_op jit(solution)/shard_map/centre_backward/pallas_call | solution.py:399
  71.2 0.0 copy-start
  71.2 0.8 copy-done
  72.0 12.2 %all-to-all-start.3 = ((f32[16,2,128]{2,1,0:T(2,128)}), f32[16,2,128]{2,1,0:T(2,128)S(1)}, u32[]{:S(2)}, u32[]{:S(2)}) async-start(f32[16,2,128]{2,1,0:T(2,128)} %get-tuple-element.35), calls=%async_computation.3 | async-start | bytes 32768 | tf_op jit(solution)/shard_map/all_to_all | solution.py:493
  84.2 0.0 collective-permute-done.2.first_ref
  84.3 0.0 collective-permute-done.3.second_ref
  84.3 0.0 copy-start.1
  84.3 1.0 copy-done.1
  85.3 1.2 gather_grads.1
  86.5 9.0 %all-to-all-done.3 = f32[16,2,128]{2,1,0:T(2,128)S(1)} async-done(((f32[16,2,128]{2,1,0:T(2,128)}), f32[16,2,128]{2,1,0:T(2,128)S(1)}, u32[]{:S(2)}, u32[]{:S(2)}) %all-to-all-start.3) | async-done | bytes 16416 | tf_op jit(solution)/shard_map/all_to_all | solution.py:493
  95.5 9.2 %all-to-all-start.2 = ((bf16[8,4,128,128]{3,2,1,0:T(8,128)(2,1)}), bf16[8,4,128,128]{3,2,1,0:T(8,128)(2,1)S(1)}, u32[]{:S(2)}, u32[]{:S(2)}) async-start(bf16[8,4,128,128]{3,2,1,0:T(8,128)(2,1)} %gather_grads.1), calls=%async_computation.2 | async-start | bytes 2097152 | tf_op jit(solution)/shard_map/all_to_all | solution.py:462
  104.7 3.6 %collective-permute-start.6 = (f32[2,128]{1,0:T(2,128)S(1)}, f32[2,128]{1,0:T(2,128)S(1)}, u32[]{:S(2)}, u32[]{:S(2)}) collective-permute-start(f32[2,128]{1,0:T(2,128)S(1)} %reduce_sum.9), channel_id=1, source_target_pairs={{0,384},{128,256},{256,128},{384,0},{1,385},{129,257},{257,129},{3... | collective-permute-start | bytes 3080 | tf_op jit(solution)/shard_map/ppermute | solution.py:467
  108.3 2.8 %collective-permute-start.5 = (f32[2,128]{1,0:T(2,128)S(1)}, f32[2,128]{1,0:T(2,128)S(1)}, u32[]{:S(2)}, u32[]{:S(2)}) collective-permute-start(f32[2,128]{1,0:T(2,128)S(1)} %reduce_sum.9), channel_id=1, source_target_pairs={{0,256},{128,384},{256,0},{384,128},{1,257},{129,385},{257,1},{385... | collective-permute-start | bytes 3080 | tf_op jit(solution)/shard_map/ppermute | solution.py:467
  111.1 2.9 %collective-permute-start.4 = (f32[2,128]{1,0:T(2,128)S(1)}, f32[2,128]{1,0:T(2,128)S(1)}, u32[]{:S(2)}, u32[]{:S(2)}) collective-permute-start(f32[2,128]{1,0:T(2,128)S(1)} %reduce_sum.9), channel_id=1, source_target_pairs={{0,128},{128,0},{256,384},{384,256},{1,129},{129,1},{257,385},{385... | collective-permute-start | bytes 3080 | tf_op jit(solution)/shard_map/ppermute | solution.py:467
  114.0 0.0 collective-permute-done.6
  114.0 0.0 collective-permute-done.5
  114.0 1.7 %collective-permute-done.4 = f32[2,128]{1,0:T(2,128)S(1)} collective-permute-done((f32[2,128]{1,0:T(2,128)S(1)}, f32[2,128]{1,0:T(2,128)S(1)}, u32[]{:S(2)}, u32[]{:S(2)}) %collective-permute-start.4) | collective-permute-done | bytes 1056 | tf_op jit(solution)/shard_map/ppermute | solution.py:467
  115.7 0.6 reshape_squeeze.3
  116.4 0.5 slice_bitcast_fusion
  116.9 2.9 %all-to-all-done.2.parts_ref = bf16[8,4,128,128]{3,2,1,0:T(8,128)(2,1)S(1)} async-done(((bf16[8,4,128,128]{3,2,1,0:T(8,128)(2,1)}), bf16[8,4,128,128]{3,2,1,0:T(8,128)(2,1)S(1)}, u32[]{:S(2)}, u32[]{:S(2)}) %all-to-all-start.2) | async-done | bytes 1048608 | tf_op jit(solution)/shard_map/all_to_all | solution.py:462
  119.8 1.2 %join_four.1 = (bf16[1,128,1024]{2,1,0:T(8,128)(2,1)}, bf16[1,128,1024]{2,1,0:T(8,128)(2,1)}, bf16[1,128,1024]{2,1,0:T(8,128)(2,1)}, bf16[1,128,1024]{2,1,0:T(8,128)(2,1)}) custom-call(bf16[8,4,128,128]{3,2,1,0:T(8,128)(2,1)S(1)} %all-to-all-done.2.parts_ref), custom_call_target="tpu_custom_call" | custom-call | tf_op jit(solution)/shard_map/join_four/pallas_call | solution.py:458
  (3 shorter events, 0.1 us)
Async XLA Ops:
  0.6 31.2 %copy-start.3 = (f32[2,64]{1,0:T(2,128)S(1)}, f32[2,64]{1,0:T(2,128)}, u32[]{:S(2)}) copy-start(f32[2,64]{1,0:T(2,128)} %param.11) | copy-start | bytes 1540
  0.6 40.0 %copy-start.2 = (f32[2]{0:T(128)S(1)}, f32[2]{0:T(128)}, u32[]{:S(2)}) copy-start(f32[2]{0:T(128)} %slopes_ref.5) | copy-start | bytes 28
  22.2 22.6 %collective-permute-start.1 = (bf16[8,2,128,128]{3,2,1,0:T(8,128)(2,1)S(1)}, bf16[8,2,128,128]{3,2,1,0:T(8,128)(2,1)S(1)}, u32[]{:S(2)}, u32[]{:S(2)}) collective-permute-start(bf16[8,2,128,128]{3,2,1,0:T(8,128)(2,1)S(1)} %all_to_all.20.kv_ref), channel_id=1, source_target_pairs={{8,16},{24,32},{40,48},{56,64},{72,80},{88,96},{104,112},{16,8},{3... | collective-permute-start | bytes 1572872 | tf_op jit(solution)/shard_map/ppermute | solution.py:473
  22.9 21.9 %collective-permute-start = (bf16[8,2,128,128]{3,2,1,0:T(8,128)(2,1)S(1)}, bf16[8,2,128,128]{3,2,1,0:T(8,128)(2,1)S(1)}, u32[]{:S(2)}, u32[]{:S(2)}) collective-permute-start(bf16[8,2,128,128]{3,2,1,0:T(8,128)(2,1)S(1)} %all_to_all.20.kv_ref), channel_id=1, source_target_pairs={{0,8},{16,24},{32,40},{48,56},{64,72},{80,88},{96,104},{112,120},{... | collective-permute-start | bytes 1572872 | tf_op jit(solution)/shard_map/ppermute | solution.py:473
  26.7 13.9 %all-to-all-start.1 = ((bf16[8,2,128,128]{3,2,1,0:T(8,128)(2,1)}), bf16[8,2,128,128]{3,2,1,0:T(8,128)(2,1)S(1)}, u32[]{:S(2)}, u32[]{:S(2)}) async-start(bf16[8,2,128,128]{3,2,1,0:T(8,128)(2,1)} %split_pair.3), calls=%async_computation.1 | async-start | bytes 1048576 | tf_op jit(solution)/shard_map/all_to_all | solution.py:462
  57.3 26.9 %collective-permute-start.2 = (bf16[8,2,128,128]{3,2,1,0:T(8,128)(2,1)}, bf16[8,2,128,128]{3,2,1,0:T(8,128)(2,1)S(1)}, u32[]{:S(2)}, u32[]{:S(2)}) collective-permute-start(bf16[8,2,128,128]{3,2,1,0:T(8,128)(2,1)} %get-tuple-element.29), channel_id=1, source_target_pairs={{8,16},{24,32},{40,48},{56,64},{72,80},{88,96},{104,112},{16,8},{3... | collective-permute-start | bytes 1572872 | tf_op jit(solution)/shard_map/ppermute | solution.py:473
  58.0 26.2 %collective-permute-start.3 = (bf16[8,2,128,128]{3,2,1,0:T(8,128)(2,1)}, bf16[8,2,128,128]{3,2,1,0:T(8,128)(2,1)S(1)}, u32[]{:S(2)}, u32[]{:S(2)}) collective-permute-start(bf16[8,2,128,128]{3,2,1,0:T(8,128)(2,1)} %get-tuple-element.30), channel_id=1, source_target_pairs={{0,8},{16,24},{32,40},{48,56},{64,72},{80,88},{96,104},{112,120},{... | collective-permute-start | bytes 1572872 | tf_op jit(solution)/shard_map/ppermute | solution.py:473
  71.2 0.8 copy-start
  72.0 23.4 %all-to-all-start.3 = ((f32[16,2,128]{2,1,0:T(2,128)}), f32[16,2,128]{2,1,0:T(2,128)S(1)}, u32[]{:S(2)}, u32[]{:S(2)}) async-start(f32[16,2,128]{2,1,0:T(2,128)} %get-tuple-element.35), calls=%async_computation.3 | async-start | bytes 32768 | tf_op jit(solution)/shard_map/all_to_all | solution.py:493
  84.3 1.0 copy-start.1
  95.5 24.3 %all-to-all-start.2 = ((bf16[8,4,128,128]{3,2,1,0:T(8,128)(2,1)}), bf16[8,4,128,128]{3,2,1,0:T(8,128)(2,1)S(1)}, u32[]{:S(2)}, u32[]{:S(2)}) async-start(bf16[8,4,128,128]{3,2,1,0:T(8,128)(2,1)} %gather_grads.1), calls=%async_computation.2 | async-start | bytes 2097152 | tf_op jit(solution)/shard_map/all_to_all | solution.py:462
  104.7 9.3 %collective-permute-start.6 = (f32[2,128]{1,0:T(2,128)S(1)}, f32[2,128]{1,0:T(2,128)S(1)}, u32[]{:S(2)}, u32[]{:S(2)}) collective-permute-start(f32[2,128]{1,0:T(2,128)S(1)} %reduce_sum.9), channel_id=1, source_target_pairs={{0,384},{128,256},{256,128},{384,0},{1,385},{129,257},{257,129},{3... | collective-permute-start | bytes 3080 | tf_op jit(solution)/shard_map/ppermute | solution.py:467
  108.3 5.8 %collective-permute-start.5 = (f32[2,128]{1,0:T(2,128)S(1)}, f32[2,128]{1,0:T(2,128)S(1)}, u32[]{:S(2)}, u32[]{:S(2)}) collective-permute-start(f32[2,128]{1,0:T(2,128)S(1)} %reduce_sum.9), channel_id=1, source_target_pairs={{0,256},{128,384},{256,0},{384,128},{1,257},{129,385},{257,1},{385... | collective-permute-start | bytes 3080 | tf_op jit(solution)/shard_map/ppermute | solution.py:467
  111.1 4.6 %collective-permute-start.4 = (f32[2,128]{1,0:T(2,128)S(1)}, f32[2,128]{1,0:T(2,128)S(1)}, u32[]{:S(2)}, u32[]{:S(2)}) collective-permute-start(f32[2,128]{1,0:T(2,128)S(1)} %reduce_sum.9), channel_id=1, source_target_pairs={{0,128},{128,0},{256,384},{384,256},{1,129},{129,1},{257,385},{385... | collective-permute-start | bytes 3080 | tf_op jit(solution)/shard_map/ppermute | solution.py:467

commit v6 on v5

--- a/solution.py
+++ b/solution.py
@@ -324,8 +324,8 @@
         sums_ref[block] = sums
     for peer in range(PEERS):
         cols = pl.ds(peer * CHUNK, CHUNK)
-        dkv_ref[peer, 0] = dkt[:, cols].T
-        dkv_ref[peer, 1] = dvt[:, cols].T
+        dkv_ref[peer, 0] = dkt[:, cols].T.astype(BF16)
+        dkv_ref[peer, 1] = dvt[:, cols].T.astype(BF16)
 
 
 SMEM = pl.BlockSpec(memory_space=pltpu.SMEM)
@@ -402,7 +402,7 @@
         out_specs=[VMEM] * 3,
         out_shape=[
             shaped(PAIR, BF16),
-            shaped(PAIR, F32),
+            shaped(PAIR, BF16),
             shaped((lax.axis_size("blk"), 2, LANES), F32),
         ],
         scratch_shapes=[
@@ -434,7 +434,7 @@
         for part in range(2):
             out_ref[peer, part] = cq_ref[peer, part]
             passed = first_ref[peer, part].astype(F32) + second_ref[peer, part].astype(F32)
-            out_ref[peer, 2 + part] = (dkv_ref[peer, part] + passed).astype(BF16)
+            out_ref[peer, 2 + part] = (dkv_ref[peer, part].astype(F32) + passed).astype(BF16)
 
 
 def run_gather(cq, dkv, from_first, from_second):

time: 122 us -> 121 us (level)
  local copies, waits for them, and re-layouts: 3.13 us -> 1.27 us
    unnamed x8 -> x4, local copies, waits for them, and re-layouts: 1.87 us -> 0.01 us
where the time goes in v6:
time: 121 us; the launch traced here: 120 us
  starting transfers between devices  45.1 us (37%)
  Pallas kernels  29.4 us (24%)
  waiting for transfers between devices  23.3 us (19%)
  blocking collectives  19.6 us (16%)
  between operations  1.44 us (1%)
  local copies, waits for them, and re-layouts  1.27 us (1%)
    all_to_all x1, blocking collectives, across(): return lax.all_to_all(pair, 'uly', split_axis=0, concat_axis=0, tiled=True)  19.6 us
    all_to_all x2, starting transfers between devices, across(): return lax.all_to_all(pair, 'uly', split_axis=0, concat_axis=0, tiled=True)  13.5 us
    pallas_call x1, Pallas kernels, run_halo(): pl.pallas_call(halo_both, in_specs=[SMEM, SMEM] + [VMEM] * 5, out_specs=[...  12.5 us
    all_to_all x1, starting transfers between devices, local(): lax.all_to_all(sums, 'blk', split_axis=0, concat_axis=0, tiled=True)  12.2 us
    all_to_all x2, waiting for transfers between devices, across(): return lax.all_to_all(pair, 'uly', split_axis=0, concat_axis=0, tiled=True)  11.5 us
    ppermute x4, starting transfers between devices, swapped(): lax.ppermute(block, 'blk', pairs + [(high, low) for low, high in pairs])  10.1 us
    all_to_all x1, waiting for transfers between devices, local(): lax.all_to_all(sums, 'blk', split_axis=0, concat_axis=0, tiled=True)  10.1 us
    ppermute x3, starting transfers between devices, over_recordings(): one, two, three = (lax.ppermute(partial, 'dp', route) for route in around)  9.29 us
  transfers between devices with their start and end apart: 10, of which 4 were waited for; matrix products, arithmetic and copies ran while one was open for 1% of the time, Pallas kernels for 11%

profile of v6, /device:TPU:1, one launch (start us, length us, event | category | flops | bytes accessed | tf_op | source)
XLA Modules:
  0.0 120.3 jit_solution(6115528991283739524)
XLA Ops:
  0.6 0.0 copy-start.1
  0.6 0.0 copy-start
  0.7 1.9 %split_pair.2 = bf16[8,2,128,128]{3,2,1,0:T(8,128)(2,1)} custom-call(bf16[1,128,1024]{2,1,0:T(8,128)(2,1)} %first_ref.2, bf16[1,128,1024]{2,1,0:T(8,128)(2,1)} %second_ref.2), custom_call_target="tpu_custom_call" | custom-call | tf_op jit(solution)/shard_map/split_pair/pallas_call | solution.py:429
  2.6 19.6 %all_to_all.20.kv_ref = bf16[8,2,128,128]{3,2,1,0:T(8,128)(2,1)S(1)} all-to-all(bf16[8,2,128,128]{3,2,1,0:T(8,128)(2,1)} %split_pair.2), channel_id=1, replica_groups=mesh['dp'=4,'blk'=16,'uly'=8] {'uly'}, dimensions={0} | all-to-all | bytes 1048576 | tf_op jit(solution)/shard_map/all_to_all | solution.py:462
  22.2 0.7 collective-permute-start.1
  22.9 1.9 %collective-permute-start = (bf16[8,2,128,128]{3,2,1,0:T(8,128)(2,1)S(1)}, bf16[8,2,128,128]{3,2,1,0:T(8,128)(2,1)S(1)}, u32[]{:S(2)}, u32[]{:S(2)}) collective-permute-start(bf16[8,2,128,128]{3,2,1,0:T(8,128)(2,1)S(1)} %all_to_all.20.kv_ref), channel_id=1, source_target_pairs={{0,8},{16,24},{32,40},{48,56},{64,72},{80,88},{96,104},{112,120},{... | collective-permute-start | bytes 1572872 | tf_op jit(solution)/shard_map/ppermute | solution.py:473
  24.8 1.9 %split_pair.3 = bf16[8,2,128,128]{3,2,1,0:T(8,128)(2,1)} custom-call(bf16[1,128,1024]{2,1,0:T(8,128)(2,1)} %first_ref.3, bf16[1,128,1024]{2,1,0:T(8,128)(2,1)} %second_ref.3), custom_call_target="tpu_custom_call" | custom-call | tf_op jit(solution)/shard_map/split_pair/pallas_call | solution.py:429
  26.7 4.4 %all-to-all-start.1 = ((bf16[8,2,128,128]{3,2,1,0:T(8,128)(2,1)}), bf16[8,2,128,128]{3,2,1,0:T(8,128)(2,1)S(1)}, u32[]{:S(2)}, u32[]{:S(2)}) async-start(bf16[8,2,128,128]{3,2,1,0:T(8,128)(2,1)} %split_pair.3), calls=%async_computation.1 | async-start | bytes 1048576 | tf_op jit(solution)/shard_map/all_to_all | solution.py:462
  31.8 0.0 copy-done.1
  31.8 0.1 reshape.15.bias_ref
  31.9 0.1 pad_add_fusion.meta
  32.0 8.7 %all-to-all-done.1.qd_ref = bf16[8,2,128,128]{3,2,1,0:T(8,128)(2,1)S(1)} async-done(((bf16[8,2,128,128]{3,2,1,0:T(8,128)(2,1)}), bf16[8,2,128,128]{3,2,1,0:T(8,128)(2,1)S(1)}, u32[]{:S(2)}, u32[]{:S(2)}) %all-to-all-start.1) | async-done | bytes 524320 | tf_op jit(solution)/shard_map/all_to_all | solution.py:462
  40.7 0.0 copy-done
  40.7 4.1 %centre_forward.1 = (bf16[2,1024,1024]{2,1,0:T(8,128)(2,1)S(1)}, f32[2,1024,128]{2,1,0:T(8,128)S(1)}) custom-call(s32[2]{0:T(128)S(1)} %pad_add_fusion.meta, f32[2]{0:T(128)S(1)} %copy-done, bf16[8,2,128,128]{3,2,1,0:T(8,128)(2,1)S(1)} %all_to_all.20.kv_ref, bf16[8,2,128,128]{3,2,1,0:T(8,128)(2,1)S(1)} %all-to-all-done.1.qd_ref, f32[1,128]{1,0:T(1,128)S(1)} %reshape.15.bias_ref), custom_call_target="tpu_custom_call" | custom-call | flops 1000 | bytes 1000 | tf_op jit(solution)/shard_map/centre_forward/pallas_call | solution.py:356
  44.8 0.0 collective-permute-done.1.first_ref
  44.8 0.0 collective-permute-done.second_ref
  44.8 12.5 %halo_both.1 = (bf16[1024,128]{1,0:T(8,128)(2,1)S(1)}, f32[1024,128]{1,0:T(8,128)S(1)}, f32[1024,128]{1,0:T(8,128)S(1)}, bf16[8,2,128,128]{3,2,1,0:T(8,128)(2,1)...) custom-call(s32[2]{0:T(128)S(1)} %pad_add_fusion.meta, f32[2]{0:T(128)S(1)} %copy-done, ...), custom_call_target="tpu_custom_call" | custom-call | flops 4026531840 | bytes 8388608 | tf_op jit(solution)/shard_map/halo_both/pallas_call | solution.py:373
  57.3 0.7 collective-permute-start.2
  58.0 6.8 %collective-permute-start.3 = (bf16[8,2,128,128]{3,2,1,0:T(8,128)(2,1)}, bf16[8,2,128,128]{3,2,1,0:T(8,128)(2,1)S(1)}, u32[]{:S(2)}, u32[]{:S(2)}) collective-permute-start(bf16[8,2,128,128]{3,2,1,0:T(8,128)(2,1)} %get-tuple-element.30), channel_id=1, source_target_pairs={{0,8},{16,24},{32,40},{48,56},{64,72},{80,88},{96,104},{112,120},{... | collective-permute-start | bytes 1572872 | tf_op jit(solution)/shard_map/ppermute | solution.py:473
  64.8 6.5 %centre_backward.1 = (bf16[8,2,128,128]{3,2,1,0:T(8,128)(2,1)S(1)}, bf16[8,2,128,128]{3,2,1,0:T(8,128)(2,1)S(1)}, f32[16,2,128]{2,1,0:T(2,128)}) custom-call(s32[2]{0:T(128)S(1)} %pad_add_fusion.meta, f32[2]{0:T(128)S(1)} %copy-done, bf16[8,2,128,128]{3,2,1,0:T(8,128)(2,1)S(1)} %all_to_all.20.kv_ref, bf16[8,2,128,128]{3,2,1,0:T(8,128)(2,1)S(1)} %all-to-all-done.1.qd_ref, ...), custom_call_target="tpu_custom_call" | custom-call | flops 1000 | bytes 1000 | tf_op jit(solution)/shard_map/centre_backward/pallas_call | solution.py:399
  71.3 12.2 %all-to-all-start.3 = ((f32[16,2,128]{2,1,0:T(2,128)}), f32[16,2,128]{2,1,0:T(2,128)S(1)}, u32[]{:S(2)}, u32[]{:S(2)}) async-start(f32[16,2,128]{2,1,0:T(2,128)} %get-tuple-element.35), calls=%async_computation.3 | async-start | bytes 32768 | tf_op jit(solution)/shard_map/all_to_all | solution.py:493
  83.6 0.0 collective-permute-done.2.first_ref
  83.6 0.0 collective-permute-done.3.second_ref
  83.6 1.2 gather_grads.1
  84.8 10.1 %all-to-all-done.3 = f32[16,2,128]{2,1,0:T(2,128)S(1)} async-done(((f32[16,2,128]{2,1,0:T(2,128)}), f32[16,2,128]{2,1,0:T(2,128)S(1)}, u32[]{:S(2)}, u32[]{:S(2)}) %all-to-all-start.3) | async-done | bytes 16416 | tf_op jit(solution)/shard_map/all_to_all | solution.py:493
  94.8 9.1 %all-to-all-start.2 = ((bf16[8,4,128,128]{3,2,1,0:T(8,128)(2,1)}), bf16[8,4,128,128]{3,2,1,0:T(8,128)(2,1)S(1)}, u32[]{:S(2)}, u32[]{:S(2)}) async-start(bf16[8,4,128,128]{3,2,1,0:T(8,128)(2,1)} %gather_grads.1), calls=%async_computation.2 | async-start | bytes 2097152 | tf_op jit(solution)/shard_map/all_to_all | solution.py:462
  104.0 3.6 %collective-permute-start.6 = (f32[2,128]{1,0:T(2,128)S(1)}, f32[2,128]{1,0:T(2,128)S(1)}, u32[]{:S(2)}, u32[]{:S(2)}) collective-permute-start(f32[2,128]{1,0:T(2,128)S(1)} %reduce_sum.9), channel_id=1, source_target_pairs={{0,384},{128,256},{256,128},{384,0},{1,385},{129,257},{257,129},{3... | collective-permute-start | bytes 3080 | tf_op jit(solution)/shard_map/ppermute | solution.py:467
  107.6 2.8 %collective-permute-start.5 = (f32[2,128]{1,0:T(2,128)S(1)}, f32[2,128]{1,0:T(2,128)S(1)}, u32[]{:S(2)}, u32[]{:S(2)}) collective-permute-start(f32[2,128]{1,0:T(2,128)S(1)} %reduce_sum.9), channel_id=1, source_target_pairs={{0,256},{128,384},{256,0},{384,128},{1,257},{129,385},{257,1},{385... | collective-permute-start | bytes 3080 | tf_op jit(solution)/shard_map/ppermute | solution.py:467
  110.4 2.9 %collective-permute-start.4 = (f32[2,128]{1,0:T(2,128)S(1)}, f32[2,128]{1,0:T(2,128)S(1)}, u32[]{:S(2)}, u32[]{:S(2)}) collective-permute-start(f32[2,128]{1,0:T(2,128)S(1)} %reduce_sum.9), channel_id=1, source_target_pairs={{0,128},{128,0},{256,384},{384,256},{1,129},{129,1},{257,385},{385... | collective-permute-start | bytes 3080 | tf_op jit(solution)/shard_map/ppermute | solution.py:467
  113.3 0.0 collective-permute-done.6
  113.3 0.0 collective-permute-done.5
  113.3 1.7 %collective-permute-done.4 = f32[2,128]{1,0:T(2,128)S(1)} collective-permute-done((f32[2,128]{1,0:T(2,128)S(1)}, f32[2,128]{1,0:T(2,128)S(1)}, u32[]{:S(2)}, u32[]{:S(2)}) %collective-permute-start.4) | collective-permute-done | bytes 1056 | tf_op jit(solution)/shard_map/ppermute | solution.py:467
  115.0 0.6 reshape_squeeze.3
  115.7 0.5 slice_bitcast_fusion
  116.2 2.8 %all-to-all-done.2.parts_ref = bf16[8,4,128,128]{3,2,1,0:T(8,128)(2,1)S(1)} async-done(((bf16[8,4,128,128]{3,2,1,0:T(8,128)(2,1)}), bf16[8,4,128,128]{3,2,1,0:T(8,128)(2,1)S(1)}, u32[]{:S(2)}, u32[]{:S(2)}) %all-to-all-start.2) | async-done | bytes 1048608 | tf_op jit(solution)/shard_map/all_to_all | solution.py:462
  119.0 1.2 %join_four.1 = (bf16[1,128,1024]{2,1,0:T(8,128)(2,1)}, bf16[1,128,1024]{2,1,0:T(8,128)(2,1)}, bf16[1,128,1024]{2,1,0:T(8,128)(2,1)}, bf16[1,128,1024]{2,1,0:T(8,128)(2,1)}) custom-call(bf16[8,4,128,128]{3,2,1,0:T(8,128)(2,1)S(1)} %all-to-all-done.2.parts_ref), custom_call_target="tpu_custom_call" | custom-call | tf_op jit(solution)/shard_map/join_four/pallas_call | solution.py:458
  (3 shorter events, 0.1 us)
Async XLA Ops:
  0.6 31.2 %copy-start.1 = (f32[2,64]{1,0:T(2,128)S(1)}, f32[2,64]{1,0:T(2,128)}, u32[]{:S(2)}) copy-start(f32[2,64]{1,0:T(2,128)} %param.11) | copy-start | bytes 1540
  0.6 40.0 %copy-start = (f32[2]{0:T(128)S(1)}, f32[2]{0:T(128)}, u32[]{:S(2)}) copy-start(f32[2]{0:T(128)} %slopes_ref.5) | copy-start | bytes 28
  22.2 22.6 %collective-permute-start.1 = (bf16[8,2,128,128]{3,2,1,0:T(8,128)(2,1)S(1)}, bf16[8,2,128,128]{3,2,1,0:T(8,128)(2,1)S(1)}, u32[]{:S(2)}, u32[]{:S(2)}) collective-permute-start(bf16[8,2,128,128]{3,2,1,0:T(8,128)(2,1)S(1)} %all_to_all.20.kv_ref), channel_id=1, source_target_pairs={{8,16},{24,32},{40,48},{56,64},{72,80},{88,96},{104,112},{16,8},{3... | collective-permute-start | bytes 1572872 | tf_op jit(solution)/shard_map/ppermute | solution.py:473
  22.9 21.9 %collective-permute-start = (bf16[8,2,128,128]{3,2,1,0:T(8,128)(2,1)S(1)}, bf16[8,2,128,128]{3,2,1,0:T(8,128)(2,1)S(1)}, u32[]{:S(2)}, u32[]{:S(2)}) collective-permute-start(bf16[8,2,128,128]{3,2,1,0:T(8,128)(2,1)S(1)} %all_to_all.20.kv_ref), channel_id=1, source_target_pairs={{0,8},{16,24},{32,40},{48,56},{64,72},{80,88},{96,104},{112,120},{... | collective-permute-start | bytes 1572872 | tf_op jit(solution)/shard_map/ppermute | solution.py:473
  26.7 13.9 %all-to-all-start.1 = ((bf16[8,2,128,128]{3,2,1,0:T(8,128)(2,1)}), bf16[8,2,128,128]{3,2,1,0:T(8,128)(2,1)S(1)}, u32[]{:S(2)}, u32[]{:S(2)}) async-start(bf16[8,2,128,128]{3,2,1,0:T(8,128)(2,1)} %split_pair.3), calls=%async_computation.1 | async-start | bytes 1048576 | tf_op jit(solution)/shard_map/all_to_all | solution.py:462
  57.3 26.2 %collective-permute-start.2 = (bf16[8,2,128,128]{3,2,1,0:T(8,128)(2,1)}, bf16[8,2,128,128]{3,2,1,0:T(8,128)(2,1)S(1)}, u32[]{:S(2)}, u32[]{:S(2)}) collective-permute-start(bf16[8,2,128,128]{3,2,1,0:T(8,128)(2,1)} %get-tuple-element.29), channel_id=1, source_target_pairs={{8,16},{24,32},{40,48},{56,64},{72,80},{88,96},{104,112},{16,8},{3... | collective-permute-start | bytes 1572872 | tf_op jit(solution)/shard_map/ppermute | solution.py:473
  58.0 25.6 %collective-permute-start.3 = (bf16[8,2,128,128]{3,2,1,0:T(8,128)(2,1)}, bf16[8,2,128,128]{3,2,1,0:T(8,128)(2,1)S(1)}, u32[]{:S(2)}, u32[]{:S(2)}) collective-permute-start(bf16[8,2,128,128]{3,2,1,0:T(8,128)(2,1)} %get-tuple-element.30), channel_id=1, source_target_pairs={{0,8},{16,24},{32,40},{48,56},{64,72},{80,88},{96,104},{112,120},{... | collective-permute-start | bytes 1572872 | tf_op jit(solution)/shard_map/ppermute | solution.py:473
  71.3 23.5 %all-to-all-start.3 = ((f32[16,2,128]{2,1,0:T(2,128)}), f32[16,2,128]{2,1,0:T(2,128)S(1)}, u32[]{:S(2)}, u32[]{:S(2)}) async-start(f32[16,2,128]{2,1,0:T(2,128)} %get-tuple-element.35), calls=%async_computation.3 | async-start | bytes 32768 | tf_op jit(solution)/shard_map/all_to_all | solution.py:493
  94.8 24.2 %all-to-all-start.2 = ((bf16[8,4,128,128]{3,2,1,0:T(8,128)(2,1)}), bf16[8,4,128,128]{3,2,1,0:T(8,128)(2,1)S(1)}, u32[]{:S(2)}, u32[]{:S(2)}) async-start(bf16[8,4,128,128]{3,2,1,0:T(8,128)(2,1)} %gather_grads.1), calls=%async_computation.2 | async-start | bytes 2097152 | tf_op jit(solution)/shard_map/all_to_all | solution.py:462
  104.0 9.3 %collective-permute-start.6 = (f32[2,128]{1,0:T(2,128)S(1)}, f32[2,128]{1,0:T(2,128)S(1)}, u32[]{:S(2)}, u32[]{:S(2)}) collective-permute-start(f32[2,128]{1,0:T(2,128)S(1)} %reduce_sum.9), channel_id=1, source_target_pairs={{0,384},{128,256},{256,128},{384,0},{1,385},{129,257},{257,129},{3... | collective-permute-start | bytes 3080 | tf_op jit(solution)/shard_map/ppermute | solution.py:467
  107.6 5.7 %collective-permute-start.5 = (f32[2,128]{1,0:T(2,128)S(1)}, f32[2,128]{1,0:T(2,128)S(1)}, u32[]{:S(2)}, u32[]{:S(2)}) collective-permute-start(f32[2,128]{1,0:T(2,128)S(1)} %reduce_sum.9), channel_id=1, source_target_pairs={{0,256},{128,384},{256,0},{384,128},{1,257},{129,385},{257,1},{385... | collective-permute-start | bytes 3080 | tf_op jit(solution)/shard_map/ppermute | solution.py:467
  110.4 4.6 %collective-permute-start.4 = (f32[2,128]{1,0:T(2,128)S(1)}, f32[2,128]{1,0:T(2,128)S(1)}, u32[]{:S(2)}, u32[]{:S(2)}) collective-permute-start(f32[2,128]{1,0:T(2,128)S(1)} %reduce_sum.9), channel_id=1, source_target_pairs={{0,128},{128,0},{256,384},{384,256},{1,129},{129,1},{257,385},{385... | collective-permute-start | bytes 3080 | tf_op jit(solution)/shard_map/ppermute | solution.py:467
